TPU v7x, 512 devices: a whole 4x4x16 slice. The times are simulated.
512 devices in a mesh: ctx: 16 (over y, x), head: 32 (over z, core).
Axes of the slice: x: 4, y: 4, z: 16, core: 2. Of those that a mesh axis runs over, the one named last changes fastest.
Arguments:
- queries: bfloat16 [32, 96, 65536], P(None, None, ('ctx', 'head')), may hold values from -9 to 9
- keys: bfloat16 [32, 96, 65536], P(None, None, ('ctx', 'head')), may hold values from -9 to 9
- values: bfloat16 [32, 96, 65536], P(None, None, ('ctx', 'head')), may hold values from -6 to 6
- doc_start: int32 [65536], P(('ctx', 'head')), may hold values from 0 to 65535, as said below
Outputs:
- grad_queries: bfloat16 [32, 96, 65536], P(None, None, ('ctx', 'head'))
- grad_keys: bfloat16 [32, 96, 65536], P(None, None, ('ctx', 'head'))
- grad_values: bfloat16 [32, 96, 65536], P(None, None, ('ctx', 'head'))
Inputs may be any that keep to these rules, and one draw needn't show every extreme that they name: doc_start never falls; doc_start[t] is t or doc_start[t-1], t - doc_start[t] < 512, the first document has exactly 512 positions, and at every multiple k of 4096 after 0 a document starts at k - 256 and runs through k + 512 // 2 - 1.
All inputs are finite; a program needn't handle non-finite values.
Results may differ from a plain program's by a relative error of at most 0.02.
Values may be sent and summed in bfloat16 or wider, within the bound.
No kernel may reach another device: no remote copies, remote signals or barrier semaphores. Data moves between devices by JAX's collectives and lax.ppermute only.
A program may use at most 128 MiB of HBM per device.

v0:
```python
import math

import jax
import jax.numpy as jnp
from jax import lax
from jax.sharding import PartitionSpec as P

DOC_MAX = 512


def from_behind(value, axis, steps):
    count = lax.axis_size(axis)
    first, last = (max(0, -steps), min(count, count - steps))
    return lax.ppermute(value, axis, [(source, source + steps) for source in range(first, last)])


def block_grads(query_blk, key_win, value_win, first_pos, query_pos, key_pos, score_scale):
    visible = (key_pos[None, :] >= first_pos[:, None]) & (key_pos[None, :] <= query_pos[:, None])
    scores = (
        jnp.einsum("hdq,hdk->hqk", query_blk, key_win, preferred_element_type=jnp.float32)
        * score_scale
    )
    scores = jnp.where(visible[None], scores, -jnp.inf)
    row_peak = jnp.max(scores, axis=2, keepdims=True)
    weights = jnp.exp(scores - row_peak)
    soft_probs = weights / jnp.sum(weights, axis=2, keepdims=True)
    probs_low = soft_probs.astype(jnp.bfloat16)
    attended = jnp.einsum(
        "hqk,hdk->hdq", probs_low, value_win, preferred_element_type=jnp.float32
    ).astype(jnp.bfloat16)
    grad_value = jnp.einsum("hqk,hdq->hdk", probs_low, attended, preferred_element_type=jnp.float32)
    grad_probs = jnp.einsum("hdq,hdk->hqk", attended, value_win, preferred_element_type=jnp.float32)
    wide_att = attended.astype(jnp.float32)
    row_dot = jnp.sum(wide_att * wide_att, axis=1)
    grad_scores = (soft_probs * (grad_probs - row_dot[:, :, None])).astype(jnp.bfloat16)
    grad_query = (
        jnp.einsum("hqk,hdk->hdq", grad_scores, key_win, preferred_element_type=jnp.float32)
        * score_scale
    ).astype(jnp.bfloat16)
    grad_key = jnp.einsum(
        "hqk,hdq->hdk", grad_scores, query_blk, preferred_element_type=jnp.float32
    )
    return (grad_query, grad_key, grad_value)


def shards(queries, keys, values, doc_start):
    score_scale = 1.0 / math.sqrt(queries.shape[1])
    head_q, head_k, head_v = (
        lax.all_to_all(queries, "head", split_axis=0, concat_axis=2, tiled=True),
        lax.all_to_all(keys, "head", split_axis=0, concat_axis=2, tiled=True),
        lax.all_to_all(values, "head", split_axis=0, concat_axis=2, tiled=True),
    )
    starts = lax.all_gather(doc_start, "head", axis=0, tiled=True)
    local_heads = head_q.shape[0]
    head_depth = head_q.shape[1]
    group_span = head_q.shape[2]
    window = DOC_MAX
    blocks = group_span // window
    prior_k, prior_v = from_behind(
        (head_k[:, :, group_span - window :], head_v[:, :, group_span - window :]), "ctx", 1
    )
    anchor = lax.axis_index("ctx") * group_span
    key_ext = jnp.concatenate([prior_k, head_k], axis=2).reshape(
        local_heads, head_depth, blocks + 1, window
    )
    value_ext = jnp.concatenate([prior_v, head_v], axis=2).reshape(
        local_heads, head_depth, blocks + 1, window
    )
    key_wins = jnp.moveaxis(jnp.concatenate([key_ext[:, :, :-1], key_ext[:, :, 1:]], axis=3), 2, 0)
    value_wins = jnp.moveaxis(
        jnp.concatenate([value_ext[:, :, :-1], value_ext[:, :, 1:]], axis=3), 2, 0
    )
    query_blocks = jnp.moveaxis(head_q.reshape(local_heads, head_depth, blocks, window), 2, 0)
    start_blocks = starts.reshape(blocks, window)
    offsets = jnp.arange(window, dtype=jnp.int32)
    spread = jnp.arange(2 * window, dtype=jnp.int32)

    def one_block(unused_carry, block_item):
        query_blk, key_win, value_win, first_pos, number = block_item
        block_base = anchor + number * window
        query_pos = block_base + offsets
        key_pos = block_base - window + spread
        return (
            unused_carry,
            block_grads(query_blk, key_win, value_win, first_pos, query_pos, key_pos, score_scale),
        )

    _, (query_stack, key_stack, value_stack) = lax.scan(
        one_block,
        jnp.int32(0),
        (query_blocks, key_wins, value_wins, start_blocks, jnp.arange(blocks, dtype=jnp.int32)),
    )
    far_k = key_stack[..., :window]
    far_v = value_stack[..., :window]
    own_k = key_stack[..., window:] + jnp.concatenate(
        [far_k[1:], jnp.zeros_like(far_k[:1])], axis=0
    )
    own_v = value_stack[..., window:] + jnp.concatenate(
        [far_v[1:], jnp.zeros_like(far_v[:1])], axis=0
    )
    back_k, back_v = from_behind((far_k[0], far_v[0]), "ctx", -1)
    own_k = own_k.at[blocks - 1].add(back_k)
    own_v = own_v.at[blocks - 1].add(back_v)

    def to_span(stacked):
        return jnp.moveaxis(stacked, 0, 2).reshape(local_heads, head_depth, group_span)

    grad_q = to_span(query_stack)
    grad_k = (to_span(own_k) * score_scale).astype(jnp.bfloat16)
    grad_v = to_span(own_v).astype(jnp.bfloat16)
    return (
        lax.all_to_all(grad_q, "head", split_axis=2, concat_axis=0, tiled=True),
        lax.all_to_all(grad_k, "head", split_axis=2, concat_axis=0, tiled=True),
        lax.all_to_all(grad_v, "head", split_axis=2, concat_axis=0, tiled=True),
    )


def solution(mesh):
    return jax.shard_map(
        shards,
        mesh=mesh,
        in_specs=(
            P(None, None, ("ctx", "head")),
            P(None, None, ("ctx", "head")),
            P(None, None, ("ctx", "head")),
            P(("ctx", "head")),
        ),
        out_specs=(
            P(None, None, ("ctx", "head")),
            P(None, None, ("ctx", "head")),
            P(None, None, ("ctx", "head")),
        ),
        check_vma=False,
    )
```

profile of v0, /device:TPU:25, one launch (start us, length us, event | category | flops | bytes accessed | tf_op | source)
XLA Modules:
  0.0 475.6 jit_solution(5532687387087716205)
XLA Ops:
  0.7 60.7 %all_to_all.105 = bf16[32,96,128]{2,1,0:T(8,128)(2,1)S(1)} all-to-all(bf16[32,96,128]{2,1,0:T(8,128)(2,1)} %param.11), channel_id=1, replica_groups=mesh['ctx'=16,'head'=32] {'head'}, dimensions={0} | all-to-all | bytes 1572864 | tf_op jit(solution)/shard_map/all_to_all | solution.py:50
  61.4 47.8 %all_to_all.106 = bf16[32,96,128]{2,1,0:T(8,128)(2,1)S(1)} all-to-all(bf16[32,96,128]{2,1,0:T(8,128)(2,1)S(1)} %copy-done.5), channel_id=1, replica_groups=mesh['ctx'=16,'head'=32] {'head'}, dimensions={0} | all-to-all | bytes 1572864 | tf_op jit(solution)/shard_map/all_to_all | solution.py:51
  109.2 4.5 all-to-all-start.1
  113.7 60.5 %all-gather = s32[32,1,128]{2,1,0:T(1,128)S(1)} all-gather(s32[1,1,128]{2,1,0:T(1,128)S(1)} %bitcast.177), channel_id=1, replica_groups=mesh['ctx'=16,'head'=32] {'head'}, dimensions={0}, use_global_device_ids=true | all-gather | bytes 16896 | tf_op jit(solution)/shard_map/all_gather | solution.py:53
  175.5 3.1 collective-permute-start
  178.7 3.1 collective-permute-start.1
  185.8 2.5 copy.26
  189.9 2.5 copy.28
  192.5 91.4 %while.19 = (s32[]{:T(128)}, bf16[8,1,96,512]{3,2,1,0:T(8,128)(2,1)S(1)}, f32[8,1,96,1024]{3,2,1,0:T(8,128)}, f32[8,1,96,1024]{3,2,1,0:T(8,128)}, bf16[8,1,96,10...) while((s32[]{:T(128)}, ...), condition=%wide.region_4.5_spmd.clone, body=%wide.region_0.4_spmd.clone.sunk | while | flops 614236160 | bytes 15839929 | solution.py:88
  257.6 2.0 fusion.68
  280.5 2.0 fusion.68
  287.4 22.6 %reduce.23 = bf16[4096,96]{1,0:T(8,128)(2,1)S(1)} reduce(bf16[4096,1,96]{2,1,0:T(2,128)(2,1)S(1)} %bitcast.161, bf16[]{:T(256)} %broadcast.107), dimensions={1}, to_apply=%bitcast.106.reduce_sub_computation | reduce | bytes 1572866
  310.0 2.5 reshape.244
  312.5 11.4 %all-to-all-start.3 = ((bf16[32,2,6144]{2,1,0:T(2,128)(2,1)}), bf16[32,2,6144]{2,1,0:T(2,128)(2,1)}, u32[]{:S(2)}, u32[]{:S(2)}) async-start(bf16[32,2,6144]{2,1,0:T(2,128)(2,1)} %reshape.244), calls=%async_computation.3 | async-start | bytes 1572864 | tf_op jit(solution)/shard_map/all_to_all | solution.py:112
  325.6 4.2 collective-permute-start.3
  331.7 2.2 collective-permute-done.3
  335.2 22.4 %reduce.25 = bf16[4096,96]{1,0:T(8,128)(2,1)S(1)} reduce(bf16[4096,1,96]{2,1,0:T(2,128)(2,1)S(1)} %bitcast.163, bf16[]{:T(256)} %broadcast.107), dimensions={1}, to_apply=%bitcast.110.reduce_sub_computation | reduce | bytes 1572866
  357.7 2.5 reshape.248
  360.1 8.5 %all-to-all-done.3 = bf16[32,2,6144]{2,1,0:T(2,128)(2,1)} async-done(((bf16[32,2,6144]{2,1,0:T(2,128)(2,1)}), bf16[32,2,6144]{2,1,0:T(2,128)(2,1)}, u32[]{:S(2)}, u32[]{:S(2)}) %all-to-all-start.3) | async-done | bytes 786464 | tf_op jit(solution)/shard_map/all_to_all | solution.py:112
  368.6 4.7 all-to-all-start.5
  374.3 5.9 %collective-permute-start.2 = (f32[1,96,512]{2,1,0:T(8,128)S(1)}, f32[1,96,512]{2,1,0:T(8,128)S(1)}, u32[]{:S(2)}, u32[]{:S(2)}) collective-permute-start(f32[1,96,512]{2,1,0:T(8,128)S(1)} %slice_bitcast_fusion.1), channel_id=1, source_target_pairs={{32,0},{64,32},{96,64},{128,96},{160,128},{192,160},{224,192},{256... | collective-permute-start | bytes 589832 | tf_op jit(solution)/shard_map/ppermute | solution.py:14
  380.2 4.0 collective-permute-done.2
  387.6 22.4 %reduce.24 = bf16[4096,96]{1,0:T(8,128)(2,1)S(1)} reduce(bf16[4096,1,96]{2,1,0:T(2,128)(2,1)S(1)} %bitcast.162, bf16[]{:T(256)} %broadcast.107), dimensions={1}, to_apply=%bitcast.108.reduce_sub_computation | reduce | bytes 1572866
  410.0 2.5 reshape.246
  412.5 5.6 %all-to-all-done.5 = bf16[32,2,6144]{2,1,0:T(2,128)(2,1)} async-done(((bf16[32,2,6144]{2,1,0:T(2,128)(2,1)}), bf16[32,2,6144]{2,1,0:T(2,128)(2,1)}, u32[]{:S(2)}, u32[]{:S(2)}) %all-to-all-start.5) | async-done | bytes 786464 | tf_op jit(solution)/shard_map/all_to_all | solution.py:114
  418.0 7.4 %all-to-all-start.4 = ((bf16[32,2,6144]{2,1,0:T(2,128)(2,1)}), bf16[32,2,6144]{2,1,0:T(2,128)(2,1)S(1)}, u32[]{:S(2)}, u32[]{:S(2)}) async-start(bf16[32,2,6144]{2,1,0:T(2,128)(2,1)} %reshape.246), calls=%async_computation.4 | async-start | bytes 1572864 | tf_op jit(solution)/shard_map/all_to_all | solution.py:113
  425.4 4.5 reshape.245
  430.0 3.7 copy.31
  436.2 4.5 reshape.249
  440.7 3.7 copy.37
  447.0 23.1 %all-to-all-done.4 = bf16[32,2,6144]{2,1,0:T(2,128)(2,1)S(1)} async-done(((bf16[32,2,6144]{2,1,0:T(2,128)(2,1)}), bf16[32,2,6144]{2,1,0:T(2,128)(2,1)S(1)}, u32[]{:S(2)}, u32[]{:S(2)}) %all-to-all-start.4) | async-done | bytes 786464 | tf_op jit(solution)/shard_map/all_to_all | solution.py:113
  471.6 2.4 copy.34
  (151 shorter events, 109.2 us)
Async XLA Ops:
  0.6 60.7 %copy-start.5 = (bf16[32,96,128]{2,1,0:T(8,128)(2,1)S(1)}, bf16[32,96,128]{2,1,0:T(8,128)(2,1)}, u32[]{:S(2)}) copy-start(bf16[32,96,128]{2,1,0:T(8,128)(2,1)} %param.12) | copy-start | bytes 2359300
  0.6 113.1 %copy-start.6 = (s32[128]{0:T(128)S(1)}, s32[128]{0:T(128)}, u32[]{:S(2)}) copy-start(s32[128]{0:T(128)} %param.13) | copy-start | bytes 1540
  109.2 72.7 %all-to-all-start.1 = ((bf16[32,96,128]{2,1,0:T(8,128)(2,1)}), bf16[32,96,128]{2,1,0:T(8,128)(2,1)S(1)}, u32[]{:S(2)}, u32[]{:S(2)}) async-start(bf16[32,96,128]{2,1,0:T(8,128)(2,1)} %param.10), calls=%async_computation.1 | async-start | bytes 1572864 | tf_op jit(solution)/shard_map/all_to_all | solution.py:49
  175.5 8.3 %collective-permute-start = (bf16[1,96,512]{2,1,0:T(8,128)(2,1)S(1)}, bf16[1,96,512]{2,1,0:T(8,128)(2,1)S(1)}, u32[]{:S(2)}, u32[]{:S(2)}) collective-permute-start(bf16[1,96,512]{2,1,0:T(8,128)(2,1)S(1)} %slice.110), channel_id=1, source_target_pairs={{0,32},{32,64},{64,96},{96,128},{128,160},{160,192},{192,224},{224... | collective-permute-start | bytes 294920 | tf_op jit(solution)/shard_map/ppermute | solution.py:14
  178.7 9.6 %collective-permute-start.1 = (bf16[1,96,512]{2,1,0:T(8,128)(2,1)S(1)}, bf16[1,96,512]{2,1,0:T(8,128)(2,1)S(1)}, u32[]{:S(2)}, u32[]{:S(2)}) collective-permute-start(bf16[1,96,512]{2,1,0:T(8,128)(2,1)S(1)} %slice.113), channel_id=1, source_target_pairs={{0,32},{32,64},{64,96},{96,128},{128,160},{160,192},{192,224},{224... | collective-permute-start | bytes 294920 | tf_op jit(solution)/shard_map/ppermute | solution.py:14
  189.9 2.6 copy-start.3
  283.9 0.9 copy-start.4
  312.5 12.9 %copy-start.2 = (f32[8,1,96,1024]{3,2,1,0:T(8,128)S(1)}, f32[8,1,96,1024]{3,2,1,0:T(8,128)}, u32[]{:S(2)}) copy-start(f32[8,1,96,1024]{3,2,1,0:T(8,128)} %get-tuple-element.180) | copy-start | bytes 9437188
  312.5 56.1 %all-to-all-start.3 = ((bf16[32,2,6144]{2,1,0:T(2,128)(2,1)}), bf16[32,2,6144]{2,1,0:T(2,128)(2,1)}, u32[]{:S(2)}, u32[]{:S(2)}) async-start(bf16[32,2,6144]{2,1,0:T(2,128)(2,1)} %reshape.244), calls=%async_computation.3 | async-start | bytes 1572864 | tf_op jit(solution)/shard_map/all_to_all | solution.py:112
  325.4 4.4 copy-start.1
  325.6 8.3 %collective-permute-start.3 = (f32[1,96,512]{2,1,0:T(8,128)S(1)}, f32[1,96,512]{2,1,0:T(8,128)S(1)}, u32[]{:S(2)}, u32[]{:S(2)}) collective-permute-start(f32[1,96,512]{2,1,0:T(8,128)S(1)} %slice_bitcast_fusion), channel_id=1, source_target_pairs={{32,0},{64,32},{96,64},{128,96},{160,128},{192,160},{224,192},{256... | collective-permute-start | bytes 589832 | tf_op jit(solution)/shard_map/ppermute | solution.py:14
  357.6 26.5 %copy-start = (f32[8,1,96,512]{3,2,1,0:T(8,128)S(1)}, f32[8,1,96,512]{3,2,1,0:T(8,128)}, u32[]{:S(2)}) copy-start(f32[8,1,96,512]{3,2,1,0:T(8,128)} %get-tuple-element.259) | copy-start | bytes 4718596
  368.6 49.4 %all-to-all-start.5 = ((bf16[32,2,6144]{2,1,0:T(2,128)(2,1)}), bf16[32,2,6144]{2,1,0:T(2,128)(2,1)}, u32[]{:S(2)}, u32[]{:S(2)}) async-start(bf16[32,2,6144]{2,1,0:T(2,128)(2,1)} %reshape.248), calls=%async_computation.5 | async-start | bytes 1572864 | tf_op jit(solution)/shard_map/all_to_all | solution.py:114
  374.3 9.9 %collective-permute-start.2 = (f32[1,96,512]{2,1,0:T(8,128)S(1)}, f32[1,96,512]{2,1,0:T(8,128)S(1)}, u32[]{:S(2)}, u32[]{:S(2)}) collective-permute-start(f32[1,96,512]{2,1,0:T(8,128)S(1)} %slice_bitcast_fusion.1), channel_id=1, source_target_pairs={{32,0},{64,32},{96,64},{128,96},{160,128},{192,160},{224,192},{256... | collective-permute-start | bytes 589832 | tf_op jit(solution)/shard_map/ppermute | solution.py:14
  418.0 52.1 %all-to-all-start.4 = ((bf16[32,2,6144]{2,1,0:T(2,128)(2,1)}), bf16[32,2,6144]{2,1,0:T(2,128)(2,1)S(1)}, u32[]{:S(2)}, u32[]{:S(2)}) async-start(bf16[32,2,6144]{2,1,0:T(2,128)(2,1)} %reshape.246), calls=%async_computation.4 | async-start | bytes 1572864 | tf_op jit(solution)/shard_map/all_to_all | solution.py:113
where the time goes:
time: 483 us; the launch traced here: 476 us
  blocking collectives  169 us (35%)
  matrix products  76.8 us (16%)
  other arithmetic  76.4 us (16%)
  local copies, waits for them, and re-layouts  58.7 us (12%)
  starting transfers between devices  44.4 us (9%)
  waiting for transfers between devices  43.3 us (9%)
  loops' own time  5.7 us (1%)
    unnamed x3, other arithmetic  67.4 us
    all_to_all x1, blocking collectives, shards(): lax.all_to_all(keys, 'head', split_axis=0, concat_axis=2, tiled=True)  60.7 us
    all_gather x1, blocking collectives, shards(): starts = lax.all_gather(doc_start, 'head', axis=0, tiled=True)  60.5 us
    all_to_all x1, blocking collectives, shards(): lax.all_to_all(values, 'head', split_axis=0, concat_axis=2, tiled=True)  47.8 us
    unnamed x30, local copies, waits for them, and re-layouts  31.9 us
    all_to_all x1, waiting for transfers between devices, shards(): lax.all_to_all(grad_k, 'head', split_axis=2, concat_axis=0, tiled=True)  23.1 us
    ppermute x4, starting transfers between devices, from_behind(): lax.ppermute(value, axis, [(source, source + steps) for source in range(f...  16.4 us
    dot_general x8, matrix products, block_grads(): jnp.einsum('hqk,hdq->hdk', grad_scores, query_blk, preferred_element_type...  15.9 us
  transfers between devices with their start and end apart: 8, of which 5 were waited for; matrix products, arithmetic and copies ran while one was open for 19% of the time, Pallas kernels for 0%

commit v1 on v0

v1 whole, which is shorter than its diff:
```python
import functools
import math

import jax
import jax.numpy as jnp
from jax import lax
from jax.experimental import pallas as pl
from jax.experimental.pallas import tpu as pltpu
from jax.sharding import PartitionSpec as P

CHUNKS = (4, 4, 4, 4)
LOG2E = 1.4426950408889634
HIDDEN = -1e30


def dot_tn(a, b):
    return lax.dot_general(a, b, (((0,), (0,)), ((), ())), preferred_element_type=jnp.float32)


def dot_nt(a, b):
    return lax.dot_general(a, b, (((1,), (1,)), ((), ())), preferred_element_type=jnp.float32)


def dot_nn(a, b):
    return lax.dot_general(a, b, (((1,), (0,)), ((), ())), preferred_element_type=jnp.float32)


def attention_kernel(
    first_ref, lo_ref, q_ref, kv0_ref, kv1_ref, kv2_ref, dq_ref, d0_ref, d1_ref, d2_ref, *, score_scale
):
    heads = q_ref.shape[1]
    half = q_ref.shape[3]
    span = 2 * half
    lo = lo_ref[...]
    refs = (kv2_ref, kv1_ref, kv0_ref)
    outs = (d2_ref, d1_ref, d0_ref)

    def wide(ref, *index):
        return jnp.concatenate([ref[(0, *index)], ref[(1, *index)]], axis=1)

    def put(ref, index, value):
        ref[(0, *index)] = value[:, :half].astype(ref.dtype)
        ref[(1, *index)] = value[:, half:].astype(ref.dtype)

    def run(first_block):
        number = range(first_block, 3)
        for h in range(heads):
            q = wide(q_ref, h)
            scores = {}
            for b in number:
                raw = dot_tn(wide(refs[b], h, 0), q) * (score_scale * LOG2E)
                key_pos = lax.broadcasted_iota(jnp.int32, (span, span), 0) + b * span
                visible = key_pos >= lo
                if b == 2:
                    row = lax.broadcasted_iota(jnp.int32, (span, span), 1) + b * span
                    visible = visible & (key_pos <= row)
                scores[b] = jnp.where(visible, raw, HIDDEN)
            peak = functools.reduce(
                jnp.maximum, [jnp.max(scores[b], axis=0, keepdims=True) for b in number]
            )
            weights = {b: jnp.exp2(scores[b] - peak) for b in number}
            total = sum(jnp.sum(weights[b], axis=0, keepdims=True) for b in number)
            inverse = 1.0 / total
            probs = {b: weights[b] * inverse for b in number}
            low = {b: probs[b].astype(jnp.bfloat16) for b in number}
            attended = sum(dot_nn(wide(refs[b], h, 1), low[b]) for b in number).astype(jnp.bfloat16)
            wide_att = attended.astype(jnp.float32)
            row_dot = jnp.sum(wide_att * wide_att, axis=0, keepdims=True)
            dq = jnp.zeros((q.shape[0], span), jnp.float32)
            for b in number:
                put(outs[b], (h, 1), dot_nt(attended, low[b]))
                grad_probs = dot_tn(wide(refs[b], h, 1), attended)
                grad_scores = (probs[b] * (grad_probs - row_dot)).astype(jnp.bfloat16)
                dq = dq + dot_nn(wide(refs[b], h, 0), grad_scores)
                put(outs[b], (h, 0), dot_nt(q, grad_scores) * score_scale)
            put(dq_ref, (h,), dq * score_scale)
        for b in range(first_block):
            outs[b][...] = jnp.zeros_like(outs[b])

    far = first_ref[0] < span

    @pl.when(far)
    def _():
        run(0)

    @pl.when(jnp.logical_not(far))
    def _():
        run(1)


def attention(first, lo, q, kv0, kv1, kv2, chunk_start, score_scale, per_step):
    _, chunk, _, depth, half = kv0.shape
    q_spec = pl.BlockSpec((2, per_step, depth, half), lambda g, s: (0, g + chunk_start // per_step, 0, 0))
    dq_spec = pl.BlockSpec((2, per_step, depth, half), lambda g, s: (0, g, 0, 0))
    kv_spec = pl.BlockSpec((2, per_step, 2, depth, half), lambda g, s: (0, g, 0, 0, 0))
    lo_spec = pl.BlockSpec((1, 2 * half), lambda g, s: (0, 0))
    kv_shape = (2, chunk, 2, depth, half)
    pairs = chunk * (2 * half) * (6 * half)
    return pl.pallas_call(
        functools.partial(attention_kernel, score_scale=score_scale),
        grid_spec=pltpu.PrefetchScalarGridSpec(
            num_scalar_prefetch=1,
            grid=(chunk // per_step,),
            in_specs=[lo_spec, q_spec, kv_spec, kv_spec, kv_spec],
            out_specs=[dq_spec, kv_spec, kv_spec, kv_spec],
        ),
        out_shape=[
            jax.ShapeDtypeStruct((2, chunk, depth, half), jnp.bfloat16),
            jax.ShapeDtypeStruct(kv_shape, jnp.float32),
            jax.ShapeDtypeStruct(kv_shape, jnp.bfloat16),
            jax.ShapeDtypeStruct(kv_shape, jnp.bfloat16),
        ],
        compiler_params=pltpu.CompilerParams(vmem_limit_bytes=32 * 1024 * 1024),
        cost_estimate=pl.CostEstimate(
            flops=pairs * depth * 12, bytes_accessed=chunk * depth * half * 40, transcendentals=pairs
        ),
        name="attention",
    )(first, lo, q, kv0, kv1, kv2)


def shards(queries, keys, values, doc_start):
    heads, depth, half = queries.shape
    score_scale = 1.0 / math.sqrt(depth)
    ctx_count = lax.axis_size("ctx")
    head_count = lax.axis_size("head")
    chips = head_count // 2
    mine = heads // 2
    span = 2 * half
    pairs = [[2 * z, 2 * z + 1] for z in range(chips)]

    def cores(value):
        return lax.all_to_all(
            value, "head", split_axis=0, concat_axis=0, tiled=True, axis_index_groups=pairs
        )

    count = ctx_count * head_count
    near_up = [(s, s + 2) for s in range(count - 2)]
    near_down = [(s + 2, s) for s in range(count - 2)]
    far_up = [(s, s + 2) for s in range(2, head_count - 2)]
    far_down = [(s + 2, s) for s in range(2, head_count - 2)]
    flat = ("ctx", "head")

    other = lax.ppermute(doc_start, "head", [(s, s ^ 1) for s in range(head_count)])
    place = lax.axis_index("head")
    odd = place % 2
    starts = jnp.where(
        odd == 0, jnp.concatenate([doc_start, other]), jnp.concatenate([other, doc_start])
    )
    base = (lax.axis_index("ctx") * chips + place // 2) * span
    lo = (starts - (base - 2 * span)).reshape(1, span)
    first = lo[0, :1]

    packed = jnp.stack(
        [keys.reshape(2, mine, depth, half), values.reshape(2, mine, depth, half)], axis=2
    )
    packed = cores(packed)
    q_all = cores(queries.reshape(2, mine, depth, half))

    dq_parts, dkv_parts = [], []
    begin = 0
    for chunk in CHUNKS:
        kv0 = packed[:, begin : begin + chunk]
        kv1 = lax.ppermute(kv0, flat, near_up)
        kv2 = lax.ppermute(kv1, "head", far_up)
        dq, d0, d1, d2 = attention(first, lo, q_all, kv0, kv1, kv2, begin, score_scale, 2)
        back2 = lax.ppermute(d2, "head", far_down)
        d1 = (d1.astype(jnp.float32) + back2.astype(jnp.float32)).astype(jnp.bfloat16)
        back1 = lax.ppermute(d1, flat, near_down)
        dq_parts.append(dq)
        dkv_parts.append((d0 + back1.astype(jnp.float32)).astype(jnp.bfloat16))
        begin += chunk

    def home(value):
        return cores(value).reshape(heads, depth, half)

    dkv = jnp.concatenate(dkv_parts, axis=1)
    return (
        home(jnp.concatenate(dq_parts, axis=1)),
        home(dkv[:, :, 0]),
        home(dkv[:, :, 1]),
    )


def solution(mesh):
    return jax.shard_map(
        shards,
        mesh=mesh,
        in_specs=(
            P(None, None, ("ctx", "head")),
            P(None, None, ("ctx", "head")),
            P(None, None, ("ctx", "head")),
            P(("ctx", "head")),
        ),
        out_specs=(
            P(None, None, ("ctx", "head")),
            P(None, None, ("ctx", "head")),
            P(None, None, ("ctx", "head")),
        ),
        check_vma=False,
    )
```

time: 483 us -> 162 us (0.34); the launches traced: 476 us -> 160 us
  blocking collectives: 169 us -> 19.2 us
  matrix products: 76.8 us -> 0 us
  other arithmetic: 76.4 us -> 2.57 us
  local copies, waits for them, and re-layouts: 58.7 us -> 3.39 us
  Pallas kernels: 0 us -> 24.4 us
  waiting for transfers between devices: 43.3 us -> 55.1 us
  starting transfers between devices: 44.4 us -> 54.3 us
  loops' own time: 5.7 us -> 0 us
    all_to_all x2 -> x4, blocking collectives: 108 us -> 19.2 us  [cores(): lax.all_to_all(value, 'head', split_axis=0, concat_axis=0, tiled=True, ax...]
    dot_general x48 -> x0, matrix products: 76.8 us -> none  [the longest x8 15.9 us: block_grads(): jnp.einsum('hqk,hdq->hdk', grad_scores, query_blk, preferred_element_type...]
    unnamed x3 -> x0, other arithmetic: 67.4 us -> none
    all_gather x1 -> x0, blocking collectives: 60.5 us -> none  [shards(): starts = lax.all_gather(doc_start, 'head', axis=0, tiled=True)]
    ppermute x4 -> x17, waiting for transfers between devices: 6.2 us -> 54.1 us  [the longest x4 28.3 us: shards(): kv1 = lax.ppermute(kv0, flat, near_up)]
    all_to_all x4 -> x1, waiting for transfers between devices: 37.1 us -> 1 us  [cores(): lax.all_to_all(value, 'head', split_axis=0, concat_axis=0, tiled=True, ax...]
    ppermute x4 -> x17, starting transfers between devices: 16.4 us -> 50.7 us  [the longest x4 24 us: shards(): back1 = lax.ppermute(d1, flat, near_down)]
    unnamed x30 -> x5, local copies, waits for them, and re-layouts: 31.9 us -> 2.64 us
  transfers between devices with their start and end apart: 8 -> 18, of which waited for: 5 -> 9; matrix products, arithmetic and copies ran while one was open for 19% -> 1% of each run, Pallas kernels for 0% -> 15%
where the time goes in v1:
time: 162 us; the launch traced here: 160 us
  waiting for transfers between devices  55.1 us (34%)
  starting transfers between devices  54.3 us (34%)
  Pallas kernels  24.4 us (15%)
  blocking collectives  19.2 us (12%)
  local copies, waits for them, and re-layouts  3.39 us (2%)
  other arithmetic  2.57 us (2%)
    ppermute x4, waiting for transfers between devices, shards(): kv1 = lax.ppermute(kv0, flat, near_up)  28.3 us
    ppermute x4, waiting for transfers between devices, shards(): back1 = lax.ppermute(d1, flat, near_down)  25.8 us
    pallas_call x4, Pallas kernels, attention(): pl.pallas_call(functools.partial(attention_kernel, score_scale=score_scal...  24.4 us
    ppermute x4, starting transfers between devices, shards(): back1 = lax.ppermute(d1, flat, near_down)  24 us
    all_to_all x4, blocking collectives, cores(): lax.all_to_all(value, 'head', split_axis=0, concat_axis=0, tiled=True, ax...  19.2 us
    ppermute x4, starting transfers between devices, shards(): kv1 = lax.ppermute(kv0, flat, near_up)  15.4 us
    ppermute x4, starting transfers between devices, shards(): kv2 = lax.ppermute(kv1, 'head', far_up)  5.65 us
    all_to_all x1, starting transfers between devices, cores(): lax.all_to_all(value, 'head', split_axis=0, concat_axis=0, tiled=True, ax...  3.55 us
  transfers between devices with their start and end apart: 18, of which 9 were waited for; matrix products, arithmetic and copies ran while one was open for 1% of the time, Pallas kernels for 15%

profile of v1, /device:TPU:25, one launch (start us, length us, event | category | flops | bytes accessed | tf_op | source)
XLA Modules:
  0.0 159.9 jit_solution(2950065404997300357)
XLA Ops:
  0.6 1.5 pad_maximum_fusion
  2.1 5.3 %all_to_all.25 = bf16[2,16,2,96,128]{4,3,2,1,0:T(8,128)(2,1)S(1)} all-to-all(bf16[2,16,2,96,128]{4,3,2,1,0:T(8,128)(2,1)S(1)} %pad_maximum_fusion), channel_id=1, replica_groups={{0,1},{2,3},{4,5},{6,7},{8,9},{10,11},{12,13},{14,15},{16,17},{18,19},{..., dimensions={0} | all-to-all | bytes 3145728 | tf_op jit(solution)/shard_map/all_to_all | solution.py:132
  7.6 3.5 %collective-permute-start.1 = (bf16[2,4,2,96,128]{4,3,2,1,0:T(8,128)(2,1)S(1)}, bf16[2,4,2,96,128]{4,3,2,1,0:T(8,128)(2,1)}, u32[]{:S(2)}, u32[]{:S(2)}) collective-permute-start(bf16[2,4,2,96,128]{4,3,2,1,0:T(8,128)(2,1)S(1)} %get-tuple-element.37.kv0_ref), channel_id=1, source_target_pairs={{0,2},{1,3},{2,4},{3,5},{4,6},{5,7},{6,8},{7,9},{8,10},{9,11},{10,... | collective-permute-start | bytes 1179656 | tf_op jit(solution)/shard_map/ppermute | solution.py:163
  11.1 3.5 %collective-permute-start.3 = (bf16[2,4,2,96,128]{4,3,2,1,0:T(8,128)(2,1)S(1)}, bf16[2,4,2,96,128]{4,3,2,1,0:T(8,128)(2,1)S(1)}, u32[]{:S(2)}, u32[]{:S(2)}) collective-permute-start(bf16[2,4,2,96,128]{4,3,2,1,0:T(8,128)(2,1)S(1)} %get-tuple-element.40.kv0_ref), channel_id=1, source_target_pairs={{0,2},{1,3},{2,4},{3,5},{4,6},{5,7},{6,8},{7,9},{8,10},{9,11},{10,... | collective-permute-start | bytes 1179656 | tf_op jit(solution)/shard_map/ppermute | solution.py:163
  14.7 3.5 %collective-permute-start.5 = (bf16[2,4,2,96,128]{4,3,2,1,0:T(8,128)(2,1)S(1)}, bf16[2,4,2,96,128]{4,3,2,1,0:T(8,128)(2,1)S(1)}, u32[]{:S(2)}, u32[]{:S(2)}) collective-permute-start(bf16[2,4,2,96,128]{4,3,2,1,0:T(8,128)(2,1)S(1)} %get-tuple-element.39.kv0_ref), channel_id=1, source_target_pairs={{0,2},{1,3},{2,4},{3,5},{4,6},{5,7},{6,8},{7,9},{8,10},{9,11},{10,... | collective-permute-start | bytes 1179656 | tf_op jit(solution)/shard_map/ppermute | solution.py:163
  18.2 4.8 %collective-permute-start.7 = (bf16[2,4,2,96,128]{4,3,2,1,0:T(8,128)(2,1)S(1)}, bf16[2,4,2,96,128]{4,3,2,1,0:T(8,128)(2,1)S(1)}, u32[]{:S(2)}, u32[]{:S(2)}) collective-permute-start(bf16[2,4,2,96,128]{4,3,2,1,0:T(8,128)(2,1)S(1)} %get-tuple-element.38.kv0_ref), channel_id=1, source_target_pairs={{0,2},{1,3},{2,4},{3,5},{4,6},{5,7},{6,8},{7,9},{8,10},{9,11},{10,... | collective-permute-start | bytes 1179656 | tf_op jit(solution)/shard_map/ppermute | solution.py:163
  23.0 7.4 %collective-permute-done.1.kv1_ref = bf16[2,4,2,96,128]{4,3,2,1,0:T(8,128)(2,1)} collective-permute-done((bf16[2,4,2,96,128]{4,3,2,1,0:T(8,128)(2,1)S(1)}, bf16[2,4,2,96,128]{4,3,2,1,0:T(8,128)(2,1)}, u32[]{:S(2)}, u32[]{:S(2)}) %collective-permute-start.1) | collective-permute-done | bytes 393248 | tf_op jit(solution)/shard_map/ppermute | solution.py:163
  30.3 1.4 collective-permute-start.2
  31.8 6.9 %collective-permute-done.3.kv1_ref = bf16[2,4,2,96,128]{4,3,2,1,0:T(8,128)(2,1)S(1)} collective-permute-done((bf16[2,4,2,96,128]{4,3,2,1,0:T(8,128)(2,1)S(1)}, bf16[2,4,2,96,128]{4,3,2,1,0:T(8,128)(2,1)S(1)}, u32[]{:S(2)}, u32[]{:S(2)}) %collective-permute-start.3) | collective-permute-done | bytes 393248 | tf_op jit(solution)/shard_map/ppermute | solution.py:163
  38.7 1.4 collective-permute-start.4
  40.1 7.0 %collective-permute-done.5.kv1_ref = bf16[2,4,2,96,128]{4,3,2,1,0:T(8,128)(2,1)S(1)} collective-permute-done((bf16[2,4,2,96,128]{4,3,2,1,0:T(8,128)(2,1)S(1)}, bf16[2,4,2,96,128]{4,3,2,1,0:T(8,128)(2,1)S(1)}, u32[]{:S(2)}, u32[]{:S(2)}) %collective-permute-start.5) | collective-permute-done | bytes 393248 | tf_op jit(solution)/shard_map/ppermute | solution.py:163
  47.1 1.4 collective-permute-start.6
  48.5 7.0 %collective-permute-done.7.kv1_ref = bf16[2,4,2,96,128]{4,3,2,1,0:T(8,128)(2,1)S(1)} collective-permute-done((bf16[2,4,2,96,128]{4,3,2,1,0:T(8,128)(2,1)S(1)}, bf16[2,4,2,96,128]{4,3,2,1,0:T(8,128)(2,1)S(1)}, u32[]{:S(2)}, u32[]{:S(2)}) %collective-permute-start.7) | collective-permute-done | bytes 393248 | tf_op jit(solution)/shard_map/ppermute | solution.py:163
  55.5 1.4 collective-permute-start.8
  56.9 2.8 %collective-permute-start = (s32[128]{0:T(128)S(1)}, s32[128]{0:T(128)S(1)}, u32[]{:S(2)}, u32[]{:S(2)}) collective-permute-start(s32[128]{0:T(128)S(1)} %copy-done), channel_id=1, source_target_pairs={{0,1},{1,0},{2,3},{3,2},{4,5},{5,4},{6,7},{7,6},{8,9},{9,8},{10,11... | collective-permute-start | bytes 1544 | tf_op jit(solution)/shard_map/ppermute | solution.py:143
  59.7 3.5 %all-to-all-start = ((bf16[2,16,96,128]{3,2,1,0:T(8,128)(2,1)}), bf16[2,16,96,128]{3,2,1,0:T(8,128)(2,1)S(1)}, u32[]{:S(2)}, u32[]{:S(2)}) async-start(bf16[2,16,96,128]{3,2,1,0:T(8,128)(2,1)} %bitcast.16), calls=%async_computation | async-start | bytes 1572864 | tf_op jit(solution)/shard_map/all_to_all | solution.py:132
  63.8 1.0 all-to-all-done.q_ref
  64.8 6.2 %attention.4 = (bf16[2,4,96,128]{3,2,1,0:T(8,128)(2,1)S(1)}, f32[2,4,2,96,128]{4,3,2,1,0:T(8,128)S(1)}, bf16[2,4,2,96,128]{4,3,2,1,0:T(8,128)(2,1)S(1)}, bf16[2,4,2,96,128]{4,3,2,1,0:T(8,128)(2,1)S(1)}) custom-call(s32[1]{0:T(128)} %bitcast.2.first_ref, s32[1,256]{1,0:T(1,128)S(1)} %fusion.lo_ref, bf16[2,16,96,128]{3,2,1,0:T(8,128)(2,1)S(1)} %all-to-all-done.q_ref, ...), custom_call_target="tpu_custom_call" | custom-call | flops 905969664 | bytes 1966080 | tf_op jit(solution)/shard_map/attention/pallas_call | solution.py:99
  71.7 6.1 %attention.5 = (bf16[2,4,96,128]{3,2,1,0:T(8,128)(2,1)S(1)}, f32[2,4,2,96,128]{4,3,2,1,0:T(8,128)S(1)}, bf16[2,4,2,96,128]{4,3,2,1,0:T(8,128)(2,1)S(1)}, bf16[2,4,2,96,128]{4,3,2,1,0:T(8,128)(2,1)S(1)}) custom-call(s32[1]{0:T(128)} %bitcast.2.first_ref, s32[1,256]{1,0:T(1,128)S(1)} %fusion.lo_ref, bf16[2,16,96,128]{3,2,1,0:T(8,128)(2,1)S(1)} %all-to-all-done.q_ref, ...), custom_call_target="tpu_custom_call" | custom-call | flops 905969664 | bytes 1966080 | tf_op jit(solution)/shard_map/attention/pallas_call | solution.py:99
  78.7 6.1 %attention.6 = (bf16[2,4,96,128]{3,2,1,0:T(8,128)(2,1)S(1)}, f32[2,4,2,96,128]{4,3,2,1,0:T(8,128)S(1)}, bf16[2,4,2,96,128]{4,3,2,1,0:T(8,128)(2,1)S(1)}, bf16[2,4,2,96,128]{4,3,2,1,0:T(8,128)(2,1)S(1)}) custom-call(s32[1]{0:T(128)} %bitcast.2.first_ref, s32[1,256]{1,0:T(1,128)S(1)} %fusion.lo_ref, bf16[2,16,96,128]{3,2,1,0:T(8,128)(2,1)S(1)} %all-to-all-done.q_ref, ...), custom_call_target="tpu_custom_call" | custom-call | flops 905969664 | bytes 1966080 | tf_op jit(solution)/shard_map/attention/pallas_call | solution.py:99
  85.4 6.1 %attention.7 = (bf16[2,4,96,128]{3,2,1,0:T(8,128)(2,1)S(1)}, f32[2,4,2,96,128]{4,3,2,1,0:T(8,128)S(1)}, bf16[2,4,2,96,128]{4,3,2,1,0:T(8,128)(2,1)S(1)}, bf16[2,4,2,96,128]{4,3,2,1,0:T(8,128)(2,1)S(1)}) custom-call(s32[1]{0:T(128)} %bitcast.2.first_ref, s32[1,256]{1,0:T(1,128)S(1)} %fusion.lo_ref, bf16[2,16,96,128]{3,2,1,0:T(8,128)(2,1)S(1)} %all-to-all-done.q_ref, ...), custom_call_target="tpu_custom_call" | custom-call | flops 905969664 | bytes 1966080 | tf_op jit(solution)/shard_map/attention/pallas_call | solution.py:99
  92.3 4.4 %all_to_all.26 = bf16[2,16,96,128]{3,2,1,0:T(8,128)(2,1)S(1)} all-to-all(bf16[2,16,96,128]{3,2,1,0:T(8,128)(2,1)S(1)} %pad_maximum_fusion.2), channel_id=1, replica_groups={{0,1},{2,3},{4,5},{6,7},{8,9},{10,11},{12,13},{14,15},{16,17},{18,19},{..., dimensions={0} | all-to-all | bytes 1572864 | tf_op jit(solution)/shard_map/all_to_all | solution.py:132
  96.8 17.1 %collective-permute-start.10 = (bf16[2,4,2,96,128]{4,3,2,1,0:T(8,128)(2,1)S(1)}, bf16[2,4,2,96,128]{4,3,2,1,0:T(8,128)(2,1)S(1)}, u32[]{:S(2)}, u32[]{:S(2)}) collective-permute-start(bf16[2,4,2,96,128]{4,3,2,1,0:T(8,128)(2,1)S(1)} %add_convert_fusion.7), channel_id=1, source_target_pairs={{2,0},{3,1},{4,2},{5,3},{6,4},{7,5},{8,6},{9,7},{10,8},{11,9},{12,... | collective-permute-start | bytes 1179656 | tf_op jit(solution)/shard_map/ppermute | solution.py:168
  114.0 1.9 %collective-permute-start.12 = (bf16[2,4,2,96,128]{4,3,2,1,0:T(8,128)(2,1)S(1)}, bf16[2,4,2,96,128]{4,3,2,1,0:T(8,128)(2,1)S(1)}, u32[]{:S(2)}, u32[]{:S(2)}) collective-permute-start(bf16[2,4,2,96,128]{4,3,2,1,0:T(8,128)(2,1)S(1)} %add_convert_fusion.5), channel_id=1, source_target_pairs={{2,0},{3,1},{4,2},{5,3},{6,4},{7,5},{8,6},{9,7},{10,8},{11,9},{12,... | collective-permute-start | bytes 1179656 | tf_op jit(solution)/shard_map/ppermute | solution.py:168
  116.1 2.1 %collective-permute-start.14 = (bf16[2,4,2,96,128]{4,3,2,1,0:T(8,128)(2,1)S(1)}, bf16[2,4,2,96,128]{4,3,2,1,0:T(8,128)(2,1)S(1)}, u32[]{:S(2)}, u32[]{:S(2)}) collective-permute-start(bf16[2,4,2,96,128]{4,3,2,1,0:T(8,128)(2,1)S(1)} %add_convert_fusion.3), channel_id=1, source_target_pairs={{2,0},{3,1},{4,2},{5,3},{6,4},{7,5},{8,6},{9,7},{10,8},{11,9},{12,... | collective-permute-start | bytes 1179656 | tf_op jit(solution)/shard_map/ppermute | solution.py:168
  118.3 2.8 %collective-permute-start.16 = (bf16[2,4,2,96,128]{4,3,2,1,0:T(8,128)(2,1)S(1)}, bf16[2,4,2,96,128]{4,3,2,1,0:T(8,128)(2,1)S(1)}, u32[]{:S(2)}, u32[]{:S(2)}) collective-permute-start(bf16[2,4,2,96,128]{4,3,2,1,0:T(8,128)(2,1)S(1)} %add_convert_fusion.1), channel_id=1, source_target_pairs={{2,0},{3,1},{4,2},{5,3},{6,4},{7,5},{8,6},{9,7},{10,8},{11,9},{12,... | collective-permute-start | bytes 1179656 | tf_op jit(solution)/shard_map/ppermute | solution.py:168
  122.1 8.3 %collective-permute-done.12 = bf16[2,4,2,96,128]{4,3,2,1,0:T(8,128)(2,1)S(1)} collective-permute-done((bf16[2,4,2,96,128]{4,3,2,1,0:T(8,128)(2,1)S(1)}, bf16[2,4,2,96,128]{4,3,2,1,0:T(8,128)(2,1)S(1)}, u32[]{:S(2)}, u32[]{:S(2)}) %collective-permute-start.12) | collective-permute-done | bytes 393248 | tf_op jit(solution)/shard_map/ppermute | solution.py:168
  130.5 8.3 %collective-permute-done.14 = bf16[2,4,2,96,128]{4,3,2,1,0:T(8,128)(2,1)S(1)} collective-permute-done((bf16[2,4,2,96,128]{4,3,2,1,0:T(8,128)(2,1)S(1)}, bf16[2,4,2,96,128]{4,3,2,1,0:T(8,128)(2,1)S(1)}, u32[]{:S(2)}, u32[]{:S(2)}) %collective-permute-start.14) | collective-permute-done | bytes 393248 | tf_op jit(solution)/shard_map/ppermute | solution.py:168
  138.9 8.3 %collective-permute-done.16 = bf16[2,4,2,96,128]{4,3,2,1,0:T(8,128)(2,1)S(1)} collective-permute-done((bf16[2,4,2,96,128]{4,3,2,1,0:T(8,128)(2,1)S(1)}, bf16[2,4,2,96,128]{4,3,2,1,0:T(8,128)(2,1)S(1)}, u32[]{:S(2)}, u32[]{:S(2)}) %collective-permute-start.16) | collective-permute-done | bytes 393248 | tf_op jit(solution)/shard_map/ppermute | solution.py:168
  147.7 5.2 %all_to_all.27 = bf16[2,16,96,128]{3,2,1,0:T(8,128)(2,1)S(1)} all-to-all(bf16[2,16,96,128]{3,2,1,0:T(8,128)(2,1)S(1)} %get-tuple-element.36), channel_id=1, replica_groups={{0,1},{2,3},{4,5},{6,7},{8,9},{10,11},{12,13},{14,15},{16,17},{18,19},{..., dimensions={0} | all-to-all | bytes 1572864 | tf_op jit(solution)/shard_map/all_to_all | solution.py:132
  152.9 4.4 %all_to_all.28 = bf16[2,16,96,128]{3,2,1,0:T(8,128)(2,1)S(1)} all-to-all(bf16[2,16,96,128]{3,2,1,0:T(8,128)(2,1)S(1)} %get-tuple-element.35), channel_id=1, replica_groups={{0,1},{2,3},{4,5},{6,7},{8,9},{10,11},{12,13},{14,15},{16,17},{18,19},{..., dimensions={0} | all-to-all | bytes 1572864 | tf_op jit(solution)/shard_map/all_to_all | solution.py:132
  159.0 0.9 copy.12
  (32 shorter events, 7.3 us)
Async XLA Ops:
  7.4 49.5 %copy-start = (s32[128]{0:T(128)S(1)}, s32[128]{0:T(128)}, u32[]{:S(2)}) copy-start(s32[128]{0:T(128)} %param.7) | copy-start | bytes 1540
  7.6 22.8 %collective-permute-start.1 = (bf16[2,4,2,96,128]{4,3,2,1,0:T(8,128)(2,1)S(1)}, bf16[2,4,2,96,128]{4,3,2,1,0:T(8,128)(2,1)}, u32[]{:S(2)}, u32[]{:S(2)}) collective-permute-start(bf16[2,4,2,96,128]{4,3,2,1,0:T(8,128)(2,1)S(1)} %get-tuple-element.37.kv0_ref), channel_id=1, source_target_pairs={{0,2},{1,3},{2,4},{3,5},{4,6},{5,7},{6,8},{7,9},{8,10},{9,11},{10,... | collective-permute-start | bytes 1179656 | tf_op jit(solution)/shard_map/ppermute | solution.py:163
  11.1 27.5 %collective-permute-start.3 = (bf16[2,4,2,96,128]{4,3,2,1,0:T(8,128)(2,1)S(1)}, bf16[2,4,2,96,128]{4,3,2,1,0:T(8,128)(2,1)S(1)}, u32[]{:S(2)}, u32[]{:S(2)}) collective-permute-start(bf16[2,4,2,96,128]{4,3,2,1,0:T(8,128)(2,1)S(1)} %get-tuple-element.40.kv0_ref), channel_id=1, source_target_pairs={{0,2},{1,3},{2,4},{3,5},{4,6},{5,7},{6,8},{7,9},{8,10},{9,11},{10,... | collective-permute-start | bytes 1179656 | tf_op jit(solution)/shard_map/ppermute | solution.py:163
  14.7 32.4 %collective-permute-start.5 = (bf16[2,4,2,96,128]{4,3,2,1,0:T(8,128)(2,1)S(1)}, bf16[2,4,2,96,128]{4,3,2,1,0:T(8,128)(2,1)S(1)}, u32[]{:S(2)}, u32[]{:S(2)}) collective-permute-start(bf16[2,4,2,96,128]{4,3,2,1,0:T(8,128)(2,1)S(1)} %get-tuple-element.39.kv0_ref), channel_id=1, source_target_pairs={{0,2},{1,3},{2,4},{3,5},{4,6},{5,7},{6,8},{7,9},{8,10},{9,11},{10,... | collective-permute-start | bytes 1179656 | tf_op jit(solution)/shard_map/ppermute | solution.py:163
  18.2 37.3 %collective-permute-start.7 = (bf16[2,4,2,96,128]{4,3,2,1,0:T(8,128)(2,1)S(1)}, bf16[2,4,2,96,128]{4,3,2,1,0:T(8,128)(2,1)S(1)}, u32[]{:S(2)}, u32[]{:S(2)}) collective-permute-start(bf16[2,4,2,96,128]{4,3,2,1,0:T(8,128)(2,1)S(1)} %get-tuple-element.38.kv0_ref), channel_id=1, source_target_pairs={{0,2},{1,3},{2,4},{3,5},{4,6},{5,7},{6,8},{7,9},{8,10},{9,11},{10,... | collective-permute-start | bytes 1179656 | tf_op jit(solution)/shard_map/ppermute | solution.py:163
  30.3 34.5 %collective-permute-start.2 = (bf16[2,4,2,96,128]{4,3,2,1,0:T(8,128)(2,1)}, bf16[2,4,2,96,128]{4,3,2,1,0:T(8,128)(2,1)}, u32[]{:S(2)}, u32[]{:S(2)}) collective-permute-start(bf16[2,4,2,96,128]{4,3,2,1,0:T(8,128)(2,1)} %collective-permute-done.1.kv1_ref), channel_id=1, source_target_pairs={{2,4},{3,5},{4,6},{5,7},{6,8},{7,9},{8,10},{9,11},{10,12},{11,13},... | collective-permute-start | bytes 1179656 | tf_op jit(solution)/shard_map/ppermute | solution.py:164
  38.7 33.0 %collective-permute-start.4 = (bf16[2,4,2,96,128]{4,3,2,1,0:T(8,128)(2,1)S(1)}, bf16[2,4,2,96,128]{4,3,2,1,0:T(8,128)(2,1)}, u32[]{:S(2)}, u32[]{:S(2)}) collective-permute-start(bf16[2,4,2,96,128]{4,3,2,1,0:T(8,128)(2,1)S(1)} %collective-permute-done.3.kv1_ref), channel_id=1, source_target_pairs={{2,4},{3,5},{4,6},{5,7},{6,8},{7,9},{8,10},{9,11},{10,12},{11,13},... | collective-permute-start | bytes 1179656 | tf_op jit(solution)/shard_map/ppermute | solution.py:164
  47.1 31.6 %collective-permute-start.6 = (bf16[2,4,2,96,128]{4,3,2,1,0:T(8,128)(2,1)S(1)}, bf16[2,4,2,96,128]{4,3,2,1,0:T(8,128)(2,1)}, u32[]{:S(2)}, u32[]{:S(2)}) collective-permute-start(bf16[2,4,2,96,128]{4,3,2,1,0:T(8,128)(2,1)S(1)} %collective-permute-done.5.kv1_ref), channel_id=1, source_target_pairs={{2,4},{3,5},{4,6},{5,7},{6,8},{7,9},{8,10},{9,11},{10,12},{11,13},... | collective-permute-start | bytes 1179656 | tf_op jit(solution)/shard_map/ppermute | solution.py:164
  55.5 29.9 %collective-permute-start.8 = (bf16[2,4,2,96,128]{4,3,2,1,0:T(8,128)(2,1)S(1)}, bf16[2,4,2,96,128]{4,3,2,1,0:T(8,128)(2,1)}, u32[]{:S(2)}, u32[]{:S(2)}) collective-permute-start(bf16[2,4,2,96,128]{4,3,2,1,0:T(8,128)(2,1)S(1)} %collective-permute-done.7.kv1_ref), channel_id=1, source_target_pairs={{2,4},{3,5},{4,6},{5,7},{6,8},{7,9},{8,10},{9,11},{10,12},{11,13},... | collective-permute-start | bytes 1179656 | tf_op jit(solution)/shard_map/ppermute | solution.py:164
  56.9 6.4 %collective-permute-start = (s32[128]{0:T(128)S(1)}, s32[128]{0:T(128)S(1)}, u32[]{:S(2)}, u32[]{:S(2)}) collective-permute-start(s32[128]{0:T(128)S(1)} %copy-done), channel_id=1, source_target_pairs={{0,1},{1,0},{2,3},{3,2},{4,5},{5,4},{6,7},{7,6},{8,9},{9,8},{10,11... | collective-permute-start | bytes 1544 | tf_op jit(solution)/shard_map/ppermute | solution.py:143
  59.7 5.1 %all-to-all-start = ((bf16[2,16,96,128]{3,2,1,0:T(8,128)(2,1)}), bf16[2,16,96,128]{3,2,1,0:T(8,128)(2,1)S(1)}, u32[]{:S(2)}, u32[]{:S(2)}) async-start(bf16[2,16,96,128]{3,2,1,0:T(8,128)(2,1)} %bitcast.16), calls=%async_computation | async-start | bytes 1572864 | tf_op jit(solution)/shard_map/all_to_all | solution.py:132
  71.0 25.7 %collective-permute-start.9 = (bf16[2,4,2,96,128]{4,3,2,1,0:T(8,128)(2,1)S(1)}, bf16[2,4,2,96,128]{4,3,2,1,0:T(8,128)(2,1)S(1)}, u32[]{:S(2)}, u32[]{:S(2)}) collective-permute-start(bf16[2,4,2,96,128]{4,3,2,1,0:T(8,128)(2,1)S(1)} %get-tuple-element.25), channel_id=1, source_target_pairs={{4,2},{5,3},{6,4},{7,5},{8,6},{9,7},{10,8},{11,9},{12,10},{13,11},... | collective-permute-start | bytes 1179656 | tf_op jit(solution)/shard_map/ppermute | solution.py:166
  77.8 36.1 %collective-permute-start.11 = (bf16[2,4,2,96,128]{4,3,2,1,0:T(8,128)(2,1)S(1)}, bf16[2,4,2,96,128]{4,3,2,1,0:T(8,128)(2,1)S(1)}, u32[]{:S(2)}, u32[]{:S(2)}) collective-permute-start(bf16[2,4,2,96,128]{4,3,2,1,0:T(8,128)(2,1)S(1)} %get-tuple-element.28), channel_id=1, source_target_pairs={{4,2},{5,3},{6,4},{7,5},{8,6},{9,7},{10,8},{11,9},{12,10},{13,11},... | collective-permute-start | bytes 1179656 | tf_op jit(solution)/shard_map/ppermute | solution.py:166
  84.7 31.2 %collective-permute-start.13 = (bf16[2,4,2,96,128]{4,3,2,1,0:T(8,128)(2,1)S(1)}, bf16[2,4,2,96,128]{4,3,2,1,0:T(8,128)(2,1)S(1)}, u32[]{:S(2)}, u32[]{:S(2)}) collective-permute-start(bf16[2,4,2,96,128]{4,3,2,1,0:T(8,128)(2,1)S(1)} %get-tuple-element.31), channel_id=1, source_target_pairs={{4,2},{5,3},{6,4},{7,5},{8,6},{9,7},{10,8},{11,9},{12,10},{13,11},... | collective-permute-start | bytes 1179656 | tf_op jit(solution)/shard_map/ppermute | solution.py:166
  91.5 26.7 %collective-permute-start.15 = (bf16[2,4,2,96,128]{4,3,2,1,0:T(8,128)(2,1)S(1)}, bf16[2,4,2,96,128]{4,3,2,1,0:T(8,128)(2,1)S(1)}, u32[]{:S(2)}, u32[]{:S(2)}) collective-permute-start(bf16[2,4,2,96,128]{4,3,2,1,0:T(8,128)(2,1)S(1)} %get-tuple-element.34), channel_id=1, source_target_pairs={{4,2},{5,3},{6,4},{7,5},{8,6},{9,7},{10,8},{11,9},{12,10},{13,11},... | collective-permute-start | bytes 1179656 | tf_op jit(solution)/shard_map/ppermute | solution.py:166
  96.8 25.2 %collective-permute-start.10 = (bf16[2,4,2,96,128]{4,3,2,1,0:T(8,128)(2,1)S(1)}, bf16[2,4,2,96,128]{4,3,2,1,0:T(8,128)(2,1)S(1)}, u32[]{:S(2)}, u32[]{:S(2)}) collective-permute-start(bf16[2,4,2,96,128]{4,3,2,1,0:T(8,128)(2,1)S(1)} %add_convert_fusion.7), channel_id=1, source_target_pairs={{2,0},{3,1},{4,2},{5,3},{6,4},{7,5},{8,6},{9,7},{10,8},{11,9},{12,... | collective-permute-start | bytes 1179656 | tf_op jit(solution)/shard_map/ppermute | solution.py:168
  114.0 16.4 %collective-permute-start.12 = (bf16[2,4,2,96,128]{4,3,2,1,0:T(8,128)(2,1)S(1)}, bf16[2,4,2,96,128]{4,3,2,1,0:T(8,128)(2,1)S(1)}, u32[]{:S(2)}, u32[]{:S(2)}) collective-permute-start(bf16[2,4,2,96,128]{4,3,2,1,0:T(8,128)(2,1)S(1)} %add_convert_fusion.5), channel_id=1, source_target_pairs={{2,0},{3,1},{4,2},{5,3},{6,4},{7,5},{8,6},{9,7},{10,8},{11,9},{12,... | collective-permute-start | bytes 1179656 | tf_op jit(solution)/shard_map/ppermute | solution.py:168
  116.1 22.8 %collective-permute-start.14 = (bf16[2,4,2,96,128]{4,3,2,1,0:T(8,128)(2,1)S(1)}, bf16[2,4,2,96,128]{4,3,2,1,0:T(8,128)(2,1)S(1)}, u32[]{:S(2)}, u32[]{:S(2)}) collective-permute-start(bf16[2,4,2,96,128]{4,3,2,1,0:T(8,128)(2,1)S(1)} %add_convert_fusion.3), channel_id=1, source_target_pairs={{2,0},{3,1},{4,2},{5,3},{6,4},{7,5},{8,6},{9,7},{10,8},{11,9},{12,... | collective-permute-start | bytes 1179656 | tf_op jit(solution)/shard_map/ppermute | solution.py:168
  118.3 29.0 %collective-permute-start.16 = (bf16[2,4,2,96,128]{4,3,2,1,0:T(8,128)(2,1)S(1)}, bf16[2,4,2,96,128]{4,3,2,1,0:T(8,128)(2,1)S(1)}, u32[]{:S(2)}, u32[]{:S(2)}) collective-permute-start(bf16[2,4,2,96,128]{4,3,2,1,0:T(8,128)(2,1)S(1)} %add_convert_fusion.1), channel_id=1, source_target_pairs={{2,0},{3,1},{4,2},{5,3},{6,4},{7,5},{8,6},{9,7},{10,8},{11,9},{12,... | collective-permute-start | bytes 1179656 | tf_op jit(solution)/shard_map/ppermute | solution.py:168

commit v2 on v1

v2 whole, which is shorter than its diff:
```python
import functools
import math

import jax
import jax.numpy as jnp
from jax import lax
from jax.experimental import pallas as pl
from jax.experimental.pallas import tpu as pltpu
from jax.sharding import PartitionSpec as P

CHUNKS = (8, 8)
PER_STEP = 4
GROUP = 4
MARK_ROWS = 16
VMEM = 32 * 1024 * 1024
LOG2E = 1.4426950408889634
HIDDEN = -1e30


def dot_tn(a, b):
    return lax.dot_general(a, b, (((0,), (0,)), ((), ())), preferred_element_type=jnp.float32)


def dot_nt(a, b):
    return lax.dot_general(a, b, (((1,), (1,)), ((), ())), preferred_element_type=jnp.float32)


def dot_nn(a, b):
    return lax.dot_general(a, b, (((1,), (0,)), ((), ())), preferred_element_type=jnp.float32)


def pack_kernel(first_ref, start_ref, k_ref, v_ref, q_ref, out_ref):
    _, chunk, depth, half = k_ref.shape
    into = first_ref[0] + lax.broadcasted_iota(jnp.int32, (1, half), 1) - start_ref[...]
    row = lax.broadcasted_iota(jnp.int32, (MARK_ROWS, half), 0)
    coarse, fine = into // 2, into % 2
    marks = jnp.where(row == 0, coarse, jnp.where(row == 1, fine, 0))
    marks = marks.astype(jnp.float32).astype(jnp.bfloat16)
    for core in range(2):
        for h in range(chunk):
            for n, ref in enumerate((k_ref, v_ref, q_ref)):
                out_ref[core, pl.ds((3 * h + n) * depth, depth), :] = ref[core, h]
        out_ref[core, pl.ds(3 * chunk * depth, MARK_ROWS), :] = marks


def pack(first, starts, keys, values, queries, begin, chunk):
    _, _, depth, half = keys.shape
    block = pl.BlockSpec((2, chunk, depth, half), lambda g, s: (0, begin // chunk, 0, 0))
    shape = (2, 3 * chunk * depth + MARK_ROWS, half)
    return pl.pallas_call(
        pack_kernel,
        grid_spec=pltpu.PrefetchScalarGridSpec(
            num_scalar_prefetch=1,
            grid=(1,),
            in_specs=[pl.BlockSpec((1, half), lambda g, s: (0, 0)), block, block, block],
            out_specs=pl.BlockSpec(shape, lambda g, s: (0, 0, 0)),
        ),
        out_shape=jax.ShapeDtypeStruct(shape, jnp.bfloat16),
        compiler_params=pltpu.CompilerParams(vmem_limit_bytes=VMEM),
        name="pack",
    )(first, starts, keys, values, queries)


def attention_kernel(
    edge_ref,
    marks_next_ref,
    marks_own_ref,
    next0_ref,
    next1_ref,
    own0_ref,
    own1_ref,
    prior_ref,
    to_next_ref,
    kept_ref,
    to_prior_ref,
    *,
    score_scale,
):
    _, heads, _, depth, half = to_prior_ref.shape
    span = 2 * half
    place = lax.broadcasted_iota(jnp.int32, (1, span), 1)
    prior, own, following = range(3)
    outs = (to_prior_ref, kept_ref, to_next_ref)

    def first_visible(marks_ref, before):
        marks = jnp.concatenate([marks_ref[0], marks_ref[1]], axis=1).astype(jnp.float32)
        into = (marks[0:1] * 2 + marks[1:2]).astype(jnp.int32)
        return before * span + place - into

    def load(b, h, n):
        if b == prior:
            return jnp.concatenate([prior_ref[0, h, n], prior_ref[1, h, n]], axis=1)
        first, second = ((own0_ref, own1_ref), (next0_ref, next1_ref))[b - 1]
        rows = pl.ds((3 * h + n) * depth, depth)
        return jnp.concatenate([first[0, rows, :], second[0, rows, :]], axis=1)

    def put(ref, index, value, add):
        for core in range(2):
            part = value[:, core * half : (core + 1) * half]
            if add:
                part = part + ref[(core, *index)].astype(jnp.float32)
            ref[(core, *index)] = part.astype(ref.dtype)

    def run(blocks, lo, rows_ref, add=None):
        diagonal = len(blocks) - 1
        hidden = []
        for at in range(len(blocks)):
            key_pos = lax.broadcasted_iota(jnp.int32, (span, span), 0) + at * span
            visible = key_pos >= lo
            if at == diagonal:
                row = lax.broadcasted_iota(jnp.int32, (span, span), 1) + at * span
                visible = visible & (key_pos <= row)
            hidden.append(jnp.where(visible, 0.0, HIDDEN))
        ones = jnp.ones((MARK_ROWS, span), jnp.bfloat16)
        for begin in range(0, heads, GROUP):
            group = range(begin, begin + GROUP)
            keys = {h: [load(b, h, 0) for b in blocks] for h in group}
            values = {h: [load(b, h, 1) for b in blocks] for h in group}
            q = {h: load(blocks[-1], h, 2) for h in group}
            scores = {
                h: [
                    dot_tn(key, q[h]) * (score_scale * LOG2E) + mask
                    for key, mask in zip(keys[h], hidden)
                ]
                for h in group
            }
            peak = {
                h: functools.reduce(
                    jnp.maximum, [jnp.max(score, axis=0, keepdims=True) for score in scores[h]]
                )
                for h in group
            }
            wide = {h: [jnp.exp2(score - peak[h]) for score in scores[h]] for h in group}
            low = {h: [weight.astype(jnp.bfloat16) for weight in wide[h]] for h in group}
            raw = {
                h: sum(
                    dot_nn(jnp.concatenate([value, ones], axis=0), weight)
                    for value, weight in zip(values[h], low[h])
                )
                for h in group
            }
            shared, row_dot = {}, {}
            for h in group:
                inverse = 1.0 / raw[h][depth : depth + 1]
                attended = (raw[h][:depth] * inverse).astype(jnp.bfloat16).astype(jnp.float32)
                row_dot[h] = jnp.sum(attended * attended, axis=0, keepdims=True) * inverse
                shared[h] = (attended * inverse).astype(jnp.bfloat16)
            grad_values = {h: [dot_nt(shared[h], weight) for weight in low[h]] for h in group}
            grad_scores = {
                h: [
                    (weight * (dot_tn(value, shared[h]) - row_dot[h])).astype(jnp.bfloat16)
                    for value, weight in zip(values[h], wide[h])
                ]
                for h in group
            }
            dq = {
                h: sum(dot_nn(key, grad) for key, grad in zip(keys[h], grad_scores[h]))
                for h in group
            }
            grad_keys = {h: [dot_nt(q[h], grad) for grad in grad_scores[h]] for h in group}
            for h in group:
                for at, b in enumerate(blocks):
                    put(outs[b], (h, 1), grad_values[h][at], b == add)
                    put(outs[b], (h, 0), grad_keys[h][at] * score_scale, b == add)
                put(rows_ref, (h, 2), dq[h] * score_scale, False)

    def clear(ref, kinds):
        for n in kinds:
            ref[:, :, n] = jnp.zeros_like(ref[:, :, n])

    edge = edge_ref[0] == 1

    @pl.when(jnp.logical_not(edge))
    def _():
        lo = first_visible(marks_next_ref, 2)
        far = jnp.min(lo) < span
        clear(kept_ref, (2,))

        @pl.when(far)
        def _():
            run((prior, own, following), lo, to_next_ref)

        @pl.when(jnp.logical_not(far))
        def _():
            run((own, following), lo - span, to_next_ref)
            clear(to_prior_ref, (0, 1))

    @pl.when(edge)
    def _():
        lo_own = first_visible(marks_own_ref, 1)
        lo_next = first_visible(marks_next_ref, 1)
        across_own = jnp.min(lo_own) < span
        across_next = jnp.min(lo_next) < span

        @pl.when(across_own)
        def _():
            run((prior, own), lo_own, kept_ref)

        @pl.when(jnp.logical_not(across_own))
        def _():
            run((own,), lo_own - span, kept_ref)
            clear(to_prior_ref, (0, 1))

        @pl.when(across_next)
        def _():
            run((own, following), lo_next, to_next_ref, add=own)

        @pl.when(jnp.logical_not(across_next))
        def _():
            run((following,), lo_next - span, to_next_ref)


def attention(edge, following, own, prior, score_scale):
    _, chunk, _, depth, half = prior.shape
    rows = 3 * PER_STEP * depth

    def spec(kinds):
        return pl.BlockSpec((2, PER_STEP, kinds, depth, half), lambda g, s: (0, g, 0, 0, 0))

    def out(kinds):
        return jax.ShapeDtypeStruct((2, chunk, kinds, depth, half), jnp.bfloat16)

    def side(core):
        return pl.BlockSpec((1, rows, half), lambda g, s: (core, g, 0))

    marks = pl.BlockSpec((2, MARK_ROWS, half), lambda g, s: (0, 3 * chunk * depth // MARK_ROWS, 0))
    pairs = chunk * (2 * half) * (6 * half)
    return pl.pallas_call(
        functools.partial(attention_kernel, score_scale=score_scale),
        grid_spec=pltpu.PrefetchScalarGridSpec(
            num_scalar_prefetch=1,
            grid=(chunk // PER_STEP,),
            in_specs=[marks, marks, side(0), side(1), side(0), side(1), spec(2)],
            out_specs=[spec(3), spec(3), spec(2)],
        ),
        out_shape=[out(3), out(3), out(2)],
        compiler_params=pltpu.CompilerParams(vmem_limit_bytes=VMEM),
        cost_estimate=pl.CostEstimate(
            flops=pairs * depth * 12, bytes_accessed=chunk * depth * half * 40, transcendentals=pairs
        ),
        name="attention",
    )(edge, following, own, following, following, own, own, prior)


def merge_kernel(kept_ref, from_prior_ref, from_next_ref, out_ref):
    for n in range(3):
        total = kept_ref[:, :, n].astype(jnp.float32) + from_prior_ref[:, :, n].astype(jnp.float32)
        if n < 2:
            total = total + from_next_ref[:, :, n].astype(jnp.float32)
        out_ref[:, :, n] = total.astype(jnp.bfloat16)


def merge(kept, from_prior, from_next):
    _, chunk, _, depth, half = kept.shape

    def spec(kinds):
        return pl.BlockSpec((2, PER_STEP, kinds, depth, half), lambda g: (0, g, 0, 0, 0))

    return pl.pallas_call(
        merge_kernel,
        grid=(chunk // PER_STEP,),
        in_specs=[spec(3), spec(3), spec(2)],
        out_specs=spec(3),
        out_shape=jax.ShapeDtypeStruct(kept.shape, jnp.bfloat16),
        compiler_params=pltpu.CompilerParams(vmem_limit_bytes=VMEM),
        name="merge",
    )(kept, from_prior, from_next)


def finish_kernel(early_ref, late_ref, out_q, out_k, out_v, sems):
    begin, mine = early_ref.shape[1], early_ref.shape[1] + late_ref.shape[1]
    pieces = []
    for half in range(2):
        for n, out in enumerate((out_k, out_v, out_q)):
            pieces.append((early_ref.at[half, :, n], out.at[pl.ds(half * mine, begin)]))
            pieces.append((late_ref.at[half, :, n], out.at[pl.ds(half * mine + begin, mine - begin)]))
    copies = [
        pltpu.make_async_copy(source, target, sems.at[i])
        for i, (source, target) in enumerate(pieces)
    ]
    for copy in copies:
        copy.start()
    for copy in copies:
        copy.wait()


def finish(early, late):
    _, begin, _, depth, half = early.shape
    heads = 2 * (begin + late.shape[1])
    out = jax.ShapeDtypeStruct((heads, depth, half), jnp.bfloat16)
    return pl.pallas_call(
        finish_kernel,
        in_specs=[pl.BlockSpec(memory_space=pltpu.VMEM)] * 2,
        out_specs=[pl.BlockSpec(memory_space=pl.ANY)] * 3,
        out_shape=[out] * 3,
        scratch_shapes=[pltpu.SemaphoreType.DMA((12,))],
        compiler_params=pltpu.CompilerParams(vmem_limit_bytes=VMEM),
        name="finish",
    )(early, late)


def after(value, *earlier):
    return lax.optimization_barrier((value, *earlier))[0]


def shards(queries, keys, values, doc_start):
    heads, depth, half = queries.shape
    score_scale = 1.0 / math.sqrt(depth)
    ctx_count = lax.axis_size("ctx")
    head_count = lax.axis_size("head")
    mine = heads // 2
    pairs = [[2 * z, 2 * z + 1] for z in range(head_count // 2)]

    def cores(value):
        return lax.all_to_all(
            value, "head", split_axis=0, concat_axis=0, tiled=True, axis_index_groups=pairs
        )

    column_up = [
        (c * head_count + s, c * head_count + s + 2)
        for c in range(ctx_count)
        for s in range(head_count - 2)
    ]
    across = [
        (c * head_count - 2 + core, c * head_count + core)
        for c in range(1, ctx_count)
        for core in range(2)
    ]
    inner_up = [
        (c * head_count + s, c * head_count + s + 2)
        for c in range(ctx_count)
        for s in range(2, head_count - 4)
    ] + across
    column_down = [(t, s) for s, t in column_up]
    inner_down = [(t, s) for s, t in inner_up]
    flat = ("ctx", "head")
    begins = [sum(CHUNKS[:c]) for c in range(len(CHUNKS) + 1)]
    last = len(CHUNKS) - 1
    by_core = (2, mine, depth, half)
    keys, values, queries = (x.reshape(by_core) for x in (keys, values, queries))
    position = (lax.axis_index("ctx") * head_count + lax.axis_index("head")) * half
    first = position.astype(jnp.int32).reshape(1)
    starts = doc_start.reshape(1, half)

    own, following, prior, to_next, kept, to_prior, back_next, back_prior, done = (
        [None] * len(CHUNKS) for _ in range(9)
    )

    def pair(c):
        body = own[c][:, : 3 * CHUNKS[c] * depth].reshape(2, CHUNKS[c], 3, depth, half)
        return body[:, :, :2]

    for c in range(last + 1):
        packed = pack(first, starts, keys, values, queries, begins[c], CHUNKS[c])
        if c:
            packed = after(packed, own[c - 1])
        own[c] = cores(packed)
        down, up = own[c], pair(c)
        if c:
            down = after(down, following[c - 1])
        following[c] = lax.ppermute(down, flat, column_down)
        prior[c] = lax.ppermute(up, flat, inner_up)

    edge = (lax.axis_index("head") < 2).astype(jnp.int32).reshape(1)
    for c in range(last + 1):
        to_next[c], kept[c], to_prior[c] = attention(
            edge, following[c], own[c], prior[c], score_scale
        )
        back_next[c] = lax.ppermute(
            after(to_next[c], back_next[c - 1] if c else prior[last]), flat, column_up
        )
        back_prior[c] = lax.ppermute(
            after(to_prior[c], back_prior[c - 1] if c else following[last]), flat, inner_down
        )
        done[c] = merge(kept[c], back_next[c], back_prior[c])
    early = cores(done[0] if last == 1 else jnp.concatenate(done[:last], axis=1))
    late = cores(after(done[last], early))
    grad_q, grad_k, grad_v = finish(early, late)
    return grad_q, grad_k, grad_v


def solution(mesh):
    return jax.shard_map(
        shards,
        mesh=mesh,
        in_specs=(
            P(None, None, ("ctx", "head")),
            P(None, None, ("ctx", "head")),
            P(None, None, ("ctx", "head")),
            P(("ctx", "head")),
        ),
        out_specs=(
            P(None, None, ("ctx", "head")),
            P(None, None, ("ctx", "head")),
            P(None, None, ("ctx", "head")),
        ),
        check_vma=False,
    )
```

time: 162 us -> 131 us (0.81)
  starting transfers between devices: 54.3 us -> 35.1 us
  waiting for transfers between devices: 55.1 us -> 41.4 us
  local copies, waits for them, and re-layouts: 3.39 us -> 12.7 us
  other arithmetic: 2.57 us -> 0 us
  Pallas kernels: 24.4 us -> 22.3 us
    ppermute x17 -> x8, starting transfers between devices: 50.7 us -> 28.2 us  [the longest x2 20.4 us: shards(): lax.ppermute(after(to_prior[c], back_prior[c - 1] if c else following[las...]
    ppermute x17 -> x8, waiting for transfers between devices: 54.1 us -> 41.4 us  [the longest x2 25.4 us: shards(): following[c] = lax.ppermute(down, flat, column_down)]
    unnamed x5 -> x20, local copies, waits for them, and re-layouts: 2.64 us -> 10.6 us
    pallas_call x4 -> x2, Pallas kernels: 24.4 us -> 17.5 us  [attention(): pl.pallas_call(functools.partial(attention_kernel, score_scale=score_scal...]
    pallas_call x0 -> x5, Pallas kernels: none -> 4.82 us  [the longest x2 3.02 us: merge(): pl.pallas_call(merge_kernel, grid=(chunk // PER_STEP,), in_specs=[spec(3)...]
    all_to_all x1, starting transfers between devices: 3.55 us -> 6.92 us  [cores(): lax.all_to_all(value, 'head', split_axis=0, concat_axis=0, tiled=True, ax...]
    all_to_all x4 -> x3, blocking collectives: 19.2 us -> 17.9 us  [cores(): lax.all_to_all(value, 'head', split_axis=0, concat_axis=0, tiled=True, ax...]
  transfers between devices with their start and end apart: 18 -> 9, of which waited for: 9 -> 7; matrix products, arithmetic and copies ran while one was open for 1% -> 2% of each run, Pallas kernels for 15% -> 16%
where the time goes in v2:
time: 131 us; the launch traced here: 130 us
  waiting for transfers between devices  41.4 us (32%)
  starting transfers between devices  35.1 us (27%)
  Pallas kernels  22.3 us (17%)
  blocking collectives  17.9 us (14%)
  local copies, waits for them, and re-layouts  12.7 us (10%)
    ppermute x2, waiting for transfers between devices, shards(): following[c] = lax.ppermute(down, flat, column_down)  25.4 us
    ppermute x2, starting transfers between devices, shards(): lax.ppermute(after(to_prior[c], back_prior[c - 1] if c else following[las...  20.4 us
    all_to_all x3, blocking collectives, cores(): lax.all_to_all(value, 'head', split_axis=0, concat_axis=0, tiled=True, ax...  17.9 us
    pallas_call x2, Pallas kernels, attention(): pl.pallas_call(functools.partial(attention_kernel, score_scale=score_scal...  17.5 us
    unnamed x20, local copies, waits for them, and re-layouts  10.6 us
    ppermute x2, waiting for transfers between devices, shards(): prior[c] = lax.ppermute(up, flat, inner_up)  9.28 us
    all_to_all x1, starting transfers between devices, cores(): lax.all_to_all(value, 'head', split_axis=0, concat_axis=0, tiled=True, ax...  6.92 us
    ppermute x2, waiting for transfers between devices, shards(): lax.ppermute(after(to_prior[c], back_prior[c - 1] if c else following[las...  3.74 us
  transfers between devices with their start and end apart: 9, of which 7 were waited for; matrix products, arithmetic and copies ran while one was open for 2% of the time, Pallas kernels for 16%

profile of v2, /device:TPU:25, one launch (start us, length us, event | category | flops | bytes accessed | tf_op | source)
XLA Modules:
  0.0 130.3 jit_solution(14688120844097875988)
XLA Ops:
  0.6 1.1 copy-done.2
  1.8 1.1 copy-done.3
  2.9 1.1 copy-done.4
  4.9 5.0 %all_to_all.20.marks_own_ref.own0_ref.own1_ref = bf16[2,2320,128]{2,1,0:T(8,128)(2,1)S(1)} all-to-all(bf16[2,2320,128]{2,1,0:T(8,128)(2,1)S(1)} %pack.2), channel_id=1, replica_groups={{0,1},{2,3},{4,5},{6,7},{8,9},{10,11},{12,13},{14,15},{16,17},{18,19},{..., dimensions={0} | all-to-all | bytes 2375680 | tf_op jit(solution)/shard_map/all_to_all | solution.py:315
  9.8 1.3 collective-permute-start
  11.2 1.0 slice.17
  12.2 1.3 collective-permute-start.1
  13.6 4.7 %all_to_all.21.marks_own_ref.own0_ref.own1_ref = bf16[2,2320,128]{2,1,0:T(8,128)(2,1)S(1)} all-to-all(bf16[2,2320,128]{2,1,0:T(8,128)(2,1)S(1)} %pack.3), channel_id=1, replica_groups={{0,1},{2,3},{4,5},{6,7},{8,9},{10,11},{12,13},{14,15},{16,17},{18,19},{..., dimensions={0} | all-to-all | bytes 2375680 | tf_op jit(solution)/shard_map/all_to_all | solution.py:315
  19.3 1.3 collective-permute-start.2
  20.6 19.0 %collective-permute-done.marks_next_ref.next0_ref.next1_ref = bf16[2,2320,128]{2,1,0:T(8,128)(2,1)S(1)} collective-permute-done((bf16[2,2320,128]{2,1,0:T(8,128)(2,1)S(1)}, bf16[2,2320,128]{2,1,0:T(8,128)(2,1)S(1)}, u32[]{:S(2)}, u32[]{:S(2)}) %collective-permute-start) | collective-permute-done | bytes 1187872 | tf_op jit(solution)/shard_map/ppermute | solution.py:361
  39.5 1.0 copy-done
  40.6 1.3 collective-permute-start.4
  41.9 2.2 %collective-permute-done.1.prior_ref = bf16[2,8,2,96,128]{4,3,2,1,0:T(8,128)(2,1)} collective-permute-done((bf16[2,8,2,96,128]{4,3,2,1,0:T(8,128)(2,1)}, bf16[2,8,2,96,128]{4,3,2,1,0:T(8,128)(2,1)}, u32[]{:S(2)}, u32[]{:S(2)}) %collective-permute-start.1) | collective-permute-done | bytes 786464 | tf_op jit(solution)/shard_map/ppermute | solution.py:362
  44.0 1.3 copy-done.1
  45.3 8.4 %attention.2 = (bf16[2,8,3,96,128]{4,3,2,1,0:T(8,128)(2,1)S(1)}, bf16[2,8,3,96,128]{4,3,2,1,0:T(8,128)(2,1)S(1)}, bf16[2,8,2,96,128]{4,3,2,1,0:T(8,128)(2,1)S(1)}) custom-call(s32[1]{0:T(128)} %bitcast.edge_ref, bf16[2,2320,128]{2,1,0:T(8,128)(2,1)S(1)} %copy-done.1, bf16[2,2320,128]{2,1,0:T(8,128)(2,1)S(1)} %all_to_all.20.marks_own_ref.own0_ref.own1_ref, ...), custom_call_target="tpu_custom_call" | custom-call | flops 1811939328 | bytes 3932160 | tf_op jit(solution)/shard_map/attention/pallas_call | solution.py:228
  53.7 7.1 %collective-permute-done.2.prior_ref = bf16[2,8,2,96,128]{4,3,2,1,0:T(8,128)(2,1)S(1)} collective-permute-done((bf16[2,8,2,96,128]{4,3,2,1,0:T(8,128)(2,1)}, bf16[2,8,2,96,128]{4,3,2,1,0:T(8,128)(2,1)S(1)}, u32[]{:S(2)}, u32[]{:S(2)}) %collective-permute-start.2) | collective-permute-done | bytes 786464 | tf_op jit(solution)/shard_map/ppermute | solution.py:362
  61.7 1.4 %collective-permute-start.3 = (bf16[2,8,3,96,128]{4,3,2,1,0:T(8,128)(2,1)S(1)}, bf16[2,8,3,96,128]{4,3,2,1,0:T(8,128)(2,1)S(1)}, u32[]{:S(2)}, u32[]{:S(2)}) collective-permute-start(bf16[2,8,3,96,128]{4,3,2,1,0:T(8,128)(2,1)S(1)} %get-tuple-element.19), channel_id=1, source_target_pairs={{0,2},{1,3},{2,4},{3,5},{4,6},{5,7},{6,8},{7,9},{8,10},{9,11},{10,... | collective-permute-start | bytes 3538952 | tf_op jit(solution)/shard_map/ppermute | solution.py:369
  63.0 6.5 %collective-permute-done.4.marks_next_ref.next0_ref.next1_ref = bf16[2,2320,128]{2,1,0:T(8,128)(2,1)} collective-permute-done((bf16[2,2320,128]{2,1,0:T(8,128)(2,1)S(1)}, bf16[2,2320,128]{2,1,0:T(8,128)(2,1)}, u32[]{:S(2)}, u32[]{:S(2)}) %collective-permute-start.4) | collective-permute-done | bytes 1187872 | tf_op jit(solution)/shard_map/ppermute | solution.py:361
  69.5 11.2 %collective-permute-start.5 = (bf16[2,8,2,96,128]{4,3,2,1,0:T(8,128)(2,1)S(1)}, bf16[2,8,2,96,128]{4,3,2,1,0:T(8,128)(2,1)S(1)}, u32[]{:S(2)}, u32[]{:S(2)}) collective-permute-start(bf16[2,8,2,96,128]{4,3,2,1,0:T(8,128)(2,1)S(1)} %get-tuple-element.22), channel_id=1, source_target_pairs={{4,2},{5,3},{6,4},{7,5},{8,6},{9,7},{10,8},{11,9},{12,10},{13,11},... | collective-permute-start | bytes 2359304 | tf_op jit(solution)/shard_map/ppermute | solution.py:372
  80.7 1.1 copy-done.8
  81.8 9.1 %attention.3 = (bf16[2,8,3,96,128]{4,3,2,1,0:T(8,128)(2,1)}, bf16[2,8,3,96,128]{4,3,2,1,0:T(8,128)(2,1)S(1)}, bf16[2,8,2,96,128]{4,3,2,1,0:T(8,128)(2,1)}) custom-call(s32[1]{0:T(128)} %bitcast.edge_ref, bf16[2,2320,128]{2,1,0:T(8,128)(2,1)} %collective-permute-done.4.marks_next_ref.next0_ref.next1_ref, ...), custom_call_target="tpu_custom_call" | custom-call | flops 1811939328 | bytes 3932160 | tf_op jit(solution)/shard_map/attention/pallas_call | solution.py:228
  90.9 1.4 %collective-permute-start.6 = (bf16[2,8,3,96,128]{4,3,2,1,0:T(8,128)(2,1)}, bf16[2,8,3,96,128]{4,3,2,1,0:T(8,128)(2,1)S(1)}, u32[]{:S(2)}, u32[]{:S(2)}) collective-permute-start(bf16[2,8,3,96,128]{4,3,2,1,0:T(8,128)(2,1)} %get-tuple-element.25), channel_id=1, source_target_pairs={{0,2},{1,3},{2,4},{3,5},{4,6},{5,7},{6,8},{7,9},{8,10},{9,11},{10,... | collective-permute-start | bytes 3538952 | tf_op jit(solution)/shard_map/ppermute | solution.py:369
  92.2 2.9 %collective-permute-done.5.from_next_ref = bf16[2,8,2,96,128]{4,3,2,1,0:T(8,128)(2,1)S(1)} collective-permute-done((bf16[2,8,2,96,128]{4,3,2,1,0:T(8,128)(2,1)S(1)}, bf16[2,8,2,96,128]{4,3,2,1,0:T(8,128)(2,1)S(1)}, u32[]{:S(2)}, u32[]{:S(2)}) %collective-permute-start.5) | collective-permute-done | bytes 786464 | tf_op jit(solution)/shard_map/ppermute | solution.py:372
  95.1 9.2 %collective-permute-start.7 = (bf16[2,8,2,96,128]{4,3,2,1,0:T(8,128)(2,1)}, bf16[2,8,2,96,128]{4,3,2,1,0:T(8,128)(2,1)}, u32[]{:S(2)}, u32[]{:S(2)}) collective-permute-start(bf16[2,8,2,96,128]{4,3,2,1,0:T(8,128)(2,1)} %get-tuple-element.27), channel_id=1, source_target_pairs={{4,2},{5,3},{6,4},{7,5},{8,6},{9,7},{10,8},{11,9},{12,10},{13,11},... | collective-permute-start | bytes 2359304 | tf_op jit(solution)/shard_map/ppermute | solution.py:372
  104.3 1.5 %merge.2 = bf16[2,8,3,96,128]{4,3,2,1,0:T(8,128)(2,1)} custom-call(bf16[2,8,3,96,128]{4,3,2,1,0:T(8,128)(2,1)S(1)} %get-tuple-element.16.kept_ref, bf16[2,8,3,96,128]{4,3,2,1,0:T(8,128)(2,1)S(1)} %collective-permute-done.3.from_prior_ref, bf16[2,8,2,96,128]{4,3,2,1,0:T(8,128)(2,1)S(1)} %collective-permute-done.5.from_next_ref), custom_call_target="tpu_custom_call" | custom-call | tf_op jit(solution)/shard_map/merge/pallas_call | solution.py:259
  105.8 6.9 %all-to-all-start.2 = ((bf16[2,8,3,96,128]{4,3,2,1,0:T(8,128)(2,1)}), bf16[2,8,3,96,128]{4,3,2,1,0:T(8,128)(2,1)S(1)}, u32[]{:S(2)}, u32[]{:S(2)}) async-start(bf16[2,8,3,96,128]{4,3,2,1,0:T(8,128)(2,1)} %merge.2), calls=%async_computation.2 | async-start | bytes 2359296 | tf_op jit(solution)/shard_map/all_to_all | solution.py:315
  112.7 2.9 %collective-permute-done.6.from_prior_ref = bf16[2,8,3,96,128]{4,3,2,1,0:T(8,128)(2,1)S(1)} collective-permute-done((bf16[2,8,3,96,128]{4,3,2,1,0:T(8,128)(2,1)}, bf16[2,8,3,96,128]{4,3,2,1,0:T(8,128)(2,1)S(1)}, u32[]{:S(2)}, u32[]{:S(2)}) %collective-permute-start.6) | collective-permute-done | bytes 1179680 | tf_op jit(solution)/shard_map/ppermute | solution.py:369
  115.6 1.0 copy-done.5
  117.5 1.3 copy-done.6
  118.8 1.6 %merge.3 = bf16[2,8,3,96,128]{4,3,2,1,0:T(8,128)(2,1)S(1)} custom-call(bf16[2,8,3,96,128]{4,3,2,1,0:T(8,128)(2,1)S(1)} %get-tuple-element.23.kept_ref, bf16[2,8,3,96,128]{4,3,2,1,0:T(8,128)(2,1)S(1)} %copy-done.6, bf16[2,8,2,96,128]{4,3,2,1,0:T(8,128)(2,1)} %collective-permute-done.7.from_next_ref), custom_call_target="tpu_custom_call" | custom-call | tf_op jit(solution)/shard_map/merge/pallas_call | solution.py:259
  120.4 8.3 %all_to_all.22.late_ref = bf16[2,8,3,96,128]{4,3,2,1,0:T(8,128)(2,1)S(1)} all-to-all(bf16[2,8,3,96,128]{4,3,2,1,0:T(8,128)(2,1)S(1)} %merge.3), channel_id=1, replica_groups={{0,1},{2,3},{4,5},{6,7},{8,9},{10,11},{12,13},{14,15},{16,17},{18,19},{..., dimensions={0} | all-to-all | bytes 2359296 | tf_op jit(solution)/shard_map/all_to_all | solution.py:315
  128.6 1.5 %finish.1 = (bf16[32,96,128]{2,1,0:T(8,128)(2,1)}, bf16[32,96,128]{2,1,0:T(8,128)(2,1)}, bf16[32,96,128]{2,1,0:T(8,128)(2,1)}) custom-call(bf16[2,8,3,96,128]{4,3,2,1,0:T(8,128)(2,1)S(1)} %all-to-all-done.2.early_ref, bf16[2,8,3,96,128]{4,3,2,1,0:T(8,128)(2,1)S(1)} %all_to_all.22.late_ref), custom_call_target="tpu_custom_call" | custom-call | tf_op jit(solution)/shard_map/finish/pallas_call | solution.py:291
  (20 shorter events, 3.9 us)
Async XLA Ops:
  0.6 1.1 copy-start.2
  1.8 1.1 copy-start.3
  2.9 1.1 copy-start.4
  4.0 0.7 copy-start.9
  9.8 29.7 %collective-permute-start = (bf16[2,2320,128]{2,1,0:T(8,128)(2,1)S(1)}, bf16[2,2320,128]{2,1,0:T(8,128)(2,1)S(1)}, u32[]{:S(2)}, u32[]{:S(2)}) collective-permute-start(bf16[2,2320,128]{2,1,0:T(8,128)(2,1)S(1)} %all_to_all.20.marks_own_ref.own0_ref.own1_ref), channel_id=1, source_target_pairs={{2,0},{3,1},{4,2},{5,3},{6,4},{7,5},{8,6},{9,7},{10,8},{11,9},{12,... | collective-permute-start | bytes 3563528 | tf_op jit(solution)/shard_map/ppermute | solution.py:361
  12.2 31.9 %collective-permute-start.1 = (bf16[2,8,2,96,128]{4,3,2,1,0:T(8,128)(2,1)}, bf16[2,8,2,96,128]{4,3,2,1,0:T(8,128)(2,1)}, u32[]{:S(2)}, u32[]{:S(2)}) collective-permute-start(bf16[2,8,2,96,128]{4,3,2,1,0:T(8,128)(2,1)} %slice.17), channel_id=1, source_target_pairs={{2,4},{3,5},{4,6},{5,7},{6,8},{7,9},{8,10},{9,11},{10,12},{11,13},... | collective-permute-start | bytes 2359304 | tf_op jit(solution)/shard_map/ppermute | solution.py:362
  19.3 41.5 %collective-permute-start.2 = (bf16[2,8,2,96,128]{4,3,2,1,0:T(8,128)(2,1)}, bf16[2,8,2,96,128]{4,3,2,1,0:T(8,128)(2,1)S(1)}, u32[]{:S(2)}, u32[]{:S(2)}) collective-permute-start(bf16[2,8,2,96,128]{4,3,2,1,0:T(8,128)(2,1)} %slice.19), channel_id=1, source_target_pairs={{2,4},{3,5},{4,6},{5,7},{6,8},{7,9},{8,10},{9,11},{10,12},{11,13},... | collective-permute-start | bytes 2359304 | tf_op jit(solution)/shard_map/ppermute | solution.py:362
  39.5 1.0 copy-start
  40.6 28.9 %collective-permute-start.4 = (bf16[2,2320,128]{2,1,0:T(8,128)(2,1)S(1)}, bf16[2,2320,128]{2,1,0:T(8,128)(2,1)}, u32[]{:S(2)}, u32[]{:S(2)}) collective-permute-start(bf16[2,2320,128]{2,1,0:T(8,128)(2,1)S(1)} %all_to_all.21.marks_own_ref.own0_ref.own1_ref), channel_id=1, source_target_pairs={{2,0},{3,1},{4,2},{5,3},{6,4},{7,5},{8,6},{9,7},{10,8},{11,9},{12,... | collective-permute-start | bytes 3563528 | tf_op jit(solution)/shard_map/ppermute | solution.py:361
  44.0 1.3 copy-start.1
  60.8 0.9 copy-start.7
  61.7 29.2 %collective-permute-start.3 = (bf16[2,8,3,96,128]{4,3,2,1,0:T(8,128)(2,1)S(1)}, bf16[2,8,3,96,128]{4,3,2,1,0:T(8,128)(2,1)S(1)}, u32[]{:S(2)}, u32[]{:S(2)}) collective-permute-start(bf16[2,8,3,96,128]{4,3,2,1,0:T(8,128)(2,1)S(1)} %get-tuple-element.19), channel_id=1, source_target_pairs={{0,2},{1,3},{2,4},{3,5},{4,6},{5,7},{6,8},{7,9},{8,10},{9,11},{10,... | collective-permute-start | bytes 3538952 | tf_op jit(solution)/shard_map/ppermute | solution.py:369
  69.5 25.6 %collective-permute-start.5 = (bf16[2,8,2,96,128]{4,3,2,1,0:T(8,128)(2,1)S(1)}, bf16[2,8,2,96,128]{4,3,2,1,0:T(8,128)(2,1)S(1)}, u32[]{:S(2)}, u32[]{:S(2)}) collective-permute-start(bf16[2,8,2,96,128]{4,3,2,1,0:T(8,128)(2,1)S(1)} %get-tuple-element.22), channel_id=1, source_target_pairs={{4,2},{5,3},{6,4},{7,5},{8,6},{9,7},{10,8},{11,9},{12,10},{13,11},... | collective-permute-start | bytes 2359304 | tf_op jit(solution)/shard_map/ppermute | solution.py:372
  80.6 1.1 copy-start.8
  90.9 24.7 %collective-permute-start.6 = (bf16[2,8,3,96,128]{4,3,2,1,0:T(8,128)(2,1)}, bf16[2,8,3,96,128]{4,3,2,1,0:T(8,128)(2,1)S(1)}, u32[]{:S(2)}, u32[]{:S(2)}) collective-permute-start(bf16[2,8,3,96,128]{4,3,2,1,0:T(8,128)(2,1)} %get-tuple-element.25), channel_id=1, source_target_pairs={{0,2},{1,3},{2,4},{3,5},{4,6},{5,7},{6,8},{7,9},{8,10},{9,11},{10,... | collective-permute-start | bytes 3538952 | tf_op jit(solution)/shard_map/ppermute | solution.py:369
  95.1 22.4 %collective-permute-start.7 = (bf16[2,8,2,96,128]{4,3,2,1,0:T(8,128)(2,1)}, bf16[2,8,2,96,128]{4,3,2,1,0:T(8,128)(2,1)}, u32[]{:S(2)}, u32[]{:S(2)}) collective-permute-start(bf16[2,8,2,96,128]{4,3,2,1,0:T(8,128)(2,1)} %get-tuple-element.27), channel_id=1, source_target_pairs={{4,2},{5,3},{6,4},{7,5},{8,6},{9,7},{10,8},{11,9},{12,10},{13,11},... | collective-permute-start | bytes 2359304 | tf_op jit(solution)/shard_map/ppermute | solution.py:372
  105.8 14.6 %all-to-all-start.2 = ((bf16[2,8,3,96,128]{4,3,2,1,0:T(8,128)(2,1)}), bf16[2,8,3,96,128]{4,3,2,1,0:T(8,128)(2,1)S(1)}, u32[]{:S(2)}, u32[]{:S(2)}) async-start(bf16[2,8,3,96,128]{4,3,2,1,0:T(8,128)(2,1)} %merge.2), calls=%async_computation.2 | async-start | bytes 2359296 | tf_op jit(solution)/shard_map/all_to_all | solution.py:315
  115.6 1.0 copy-start.5
  117.5 1.3 copy-start.6

commit v3 on v2

v3 whole, which is shorter than its diff:
```python
import functools
import math

import jax
import jax.numpy as jnp
from jax import lax
from jax.experimental import pallas as pl
from jax.experimental.pallas import tpu as pltpu
from jax.sharding import PartitionSpec as P

CHUNKS = (8, 8)
PER_STEP = 4
GROUP = 4
MARK_ROWS = 16
VMEM = 32 * 1024 * 1024
PACK_VMEM = 56 * 1024 * 1024
LOG2E = 1.4426950408889634
HIDDEN = -1e30


def dot_tn(a, b):
    return lax.dot_general(a, b, (((0,), (0,)), ((), ())), preferred_element_type=jnp.float32)


def dot_nt(a, b):
    return lax.dot_general(a, b, (((1,), (1,)), ((), ())), preferred_element_type=jnp.float32)


def dot_nn(a, b):
    return lax.dot_general(a, b, (((1,), (0,)), ((), ())), preferred_element_type=jnp.float32)


def pack_kernel(first_ref, parity_ref, start_ref, k_ref, v_ref, q_ref, *rest, begin, rows):
    outs, sems = rest[:-1], rest[-1]
    half = start_ref.shape[1]
    parity = parity_ref[0]
    pieces = []
    for n, ref in enumerate((k_ref, v_ref, q_ref)):
        into = pl.ds(n * rows, rows)
        for core in range(2):
            source = ref.at[core, pl.ds(begin, rows)]
            pieces.append((source, outs[0].at[core, into]))
        for turn, out in enumerate(outs[1:]):
            if n < 2 or turn < 2:
                source = ref.at[lax.rem(parity + turn, 2), pl.ds(begin, rows)]
                pieces.append((source, out.at[0, into]))
    copies = [
        pltpu.make_async_copy(source, target, sems.at[i])
        for i, (source, target) in enumerate(pieces)
    ]
    for copy in copies:
        copy.start()
    into = first_ref[0] + lax.broadcasted_iota(jnp.int32, (1, half), 1) - start_ref[...]
    row = lax.broadcasted_iota(jnp.int32, (MARK_ROWS, half), 0)
    marks = jnp.where(row == 0, into // 2, jnp.where(row == 1, into % 2, 0))
    marks = marks.astype(jnp.float32).astype(jnp.bfloat16)
    for out in outs[:3]:
        for lead in range(out.shape[0]):
            out[lead, pl.ds(3 * rows, MARK_ROWS), :] = marks
    for copy in copies:
        copy.wait()


def pack(first, parity, starts, keys, values, queries, begin, chunk, direct):
    _, _, depth, half = keys.shape
    rows = chunk * depth
    flat = [x.reshape(2, -1, half) for x in (keys, values, queries)]
    whole, pair = 3 * rows + MARK_ROWS, 2 * rows
    out = [(2, whole, half), (1, whole, half), (1, whole, half), (1, pair, half), (1, pair, half)]
    out = [jax.ShapeDtypeStruct(shape, jnp.bfloat16) for shape in (out if direct else out[:1])]
    smem = pl.BlockSpec(memory_space=pltpu.SMEM)
    vmem = pl.BlockSpec(memory_space=pltpu.VMEM)
    return pl.pallas_call(
        functools.partial(pack_kernel, begin=begin * depth, rows=rows),
        in_specs=[smem, smem, vmem] + [pl.BlockSpec(memory_space=pltpu.HBM)] * 3,
        out_specs=[vmem] * len(out),
        out_shape=out,
        scratch_shapes=[pltpu.SemaphoreType.DMA((16,))],
        compiler_params=pltpu.CompilerParams(vmem_limit_bytes=PACK_VMEM),
        name="pack",
    )(first, parity, starts, *flat)


def attention_kernel(
    edge_ref, turned_ref, out_turn_ref, *refs, score_scale, parted
):
    next_marks, own_marks = refs[:2], refs[2]
    next_refs = (refs[3:6], refs[6:9])
    own_refs, prior_refs = refs[9:12], (refs[12:14], refs[14:16])
    results = refs[16:]
    if parted:
        to_next, kept, to_prior = results[:2], results[2:4], results[4:]
    else:
        to_next, kept, to_prior = ((ref.at[0], ref.at[1]) for ref in results)
    heads, _, depth, half = to_prior[0].shape
    span = 2 * half
    prior, own, following = range(3)
    outs = (to_prior, kept, to_next)
    turned = turned_ref[0]
    turns = (turned, 0, turned)
    out_turn = out_turn_ref[0]

    def positions(b, axis):
        shape = (1, span) if axis == 1 else (span, span)
        return lax.broadcasted_iota(jnp.int32, shape, axis) ^ (turns[b] * half)

    def first_visible(b, before):
        first, second = next_marks if b == following else (own_marks.at[0], own_marks.at[1])
        first, second = (first[0], second[0]) if b == following else (first[...], second[...])
        marks = jnp.concatenate([first, second], axis=1).astype(jnp.float32)
        into = (marks[0:1] * 2 + marks[1:2]).astype(jnp.int32)
        return before * span + positions(b, 1) - into

    def load(b, h, n):
        rows = pl.ds(h * depth, depth)
        if b == own:
            first, second = own_refs[n][0, rows, :], own_refs[n][1, rows, :]
        else:
            first, second = (prior_refs, None, next_refs)[b]
            first, second = first[n][0, rows, :], second[n][0, rows, :]
        return jnp.concatenate([first, second], axis=1)

    def put(b, pair, index, value, add):
        straight = (turns[b] ^ out_turn) == 0
        first, second = value[:, :half], value[:, half:]
        parts = (jnp.where(straight, first, second), jnp.where(straight, second, first))
        for ref, part in zip(pair, parts):
            if add:
                part = part + ref[index].astype(jnp.float32)
            ref[index] = part.astype(ref.dtype)

    def run(blocks, lo, rows_out, add=None):
        diagonal = len(blocks) - 1
        hidden = []
        for at in range(len(blocks)):
            key_pos = positions(blocks[at], 0) + at * span
            visible = key_pos >= lo
            if at == diagonal:
                visible = visible & (key_pos <= positions(blocks[at], 1) + at * span)
            hidden.append(jnp.where(visible, 0.0, HIDDEN))
        ones = jnp.ones((MARK_ROWS, span), jnp.bfloat16)
        for begin in range(0, heads, GROUP):
            group = range(begin, begin + GROUP)
            keys = {h: [load(b, h, 0) for b in blocks] for h in group}
            values = {h: [load(b, h, 1) for b in blocks] for h in group}
            q = {h: load(blocks[-1], h, 2) for h in group}
            scores = {
                h: [
                    dot_tn(key, q[h]) * (score_scale * LOG2E) + mask
                    for key, mask in zip(keys[h], hidden)
                ]
                for h in group
            }
            peak = {
                h: functools.reduce(
                    jnp.maximum, [jnp.max(score, axis=0, keepdims=True) for score in scores[h]]
                )
                for h in group
            }
            wide = {h: [jnp.exp2(score - peak[h]) for score in scores[h]] for h in group}
            low = {h: [weight.astype(jnp.bfloat16) for weight in wide[h]] for h in group}
            raw = {
                h: sum(
                    dot_nn(jnp.concatenate([value, ones], axis=0), weight)
                    for value, weight in zip(values[h], low[h])
                )
                for h in group
            }
            shared, row_dot = {}, {}
            for h in group:
                inverse = 1.0 / raw[h][depth : depth + 1]
                attended = (raw[h][:depth] * inverse).astype(jnp.bfloat16).astype(jnp.float32)
                row_dot[h] = jnp.sum(attended * attended, axis=0, keepdims=True) * inverse
                shared[h] = (attended * inverse).astype(jnp.bfloat16)
            grad_values = {h: [dot_nt(shared[h], weight) for weight in low[h]] for h in group}
            grad_scores = {
                h: [
                    (weight * (dot_tn(value, shared[h]) - row_dot[h])).astype(jnp.bfloat16)
                    for value, weight in zip(values[h], wide[h])
                ]
                for h in group
            }
            dq = {
                h: sum(dot_nn(key, grad) for key, grad in zip(keys[h], grad_scores[h]))
                for h in group
            }
            grad_keys = {h: [dot_nt(q[h], grad) for grad in grad_scores[h]] for h in group}
            for h in group:
                for at, b in enumerate(blocks):
                    put(b, outs[b], (h, 1), grad_values[h][at], b == add)
                    put(b, outs[b], (h, 0), grad_keys[h][at] * score_scale, b == add)
                put(blocks[-1], rows_out, (h, 2), dq[h] * score_scale, False)

    def clear(pair, kinds):
        for ref in pair:
            for n in kinds:
                ref[:, n] = jnp.zeros_like(ref[:, n])

    edge = edge_ref[0] == 1

    @pl.when(jnp.logical_not(edge))
    def _():
        lo = first_visible(following, 2)
        far = jnp.min(lo) < span
        clear(kept, (2,))

        @pl.when(far)
        def _():
            run((prior, own, following), lo, to_next)

        @pl.when(jnp.logical_not(far))
        def _():
            run((own, following), lo - span, to_next)
            clear(to_prior, (0, 1))

    @pl.when(edge)
    def _():
        lo_own = first_visible(own, 1)
        lo_next = first_visible(following, 1)
        across_own = jnp.min(lo_own) < span
        across_next = jnp.min(lo_next) < span

        @pl.when(across_own)
        def _():
            run((prior, own), lo_own, kept)

        @pl.when(jnp.logical_not(across_own))
        def _():
            run((own,), lo_own - span, kept)
            clear(to_prior, (0, 1))

        @pl.when(across_next)
        def _():
            run((own, following), lo_next, to_next, add=own)

        @pl.when(jnp.logical_not(across_next))
        def _():
            run((following,), lo_next - span, to_next)


def attention(edge, turned, out_turn, following, own, prior, score_scale, depth, parted):
    _, rows, half = own.shape
    chunk = rows // 3 // depth
    steps = chunk // PER_STEP
    block = PER_STEP * depth

    def spec(kinds):
        if parted:
            return [pl.BlockSpec((PER_STEP, kinds, depth, half), lambda g, e, t, o: (g, 0, 0, 0))] * 2
        return [pl.BlockSpec((2, PER_STEP, kinds, depth, half), lambda g, e, t, o: (0, g, 0, 0, 0))]

    def out(kinds):
        if parted:
            return [jax.ShapeDtypeStruct((chunk, kinds, depth, half), jnp.bfloat16)] * 2
        return [jax.ShapeDtypeStruct((2, chunk, kinds, depth, half), jnp.bfloat16)]

    def side(lead, n, cores=1):
        return pl.BlockSpec((cores, block, half), lambda g, e, t, o: (lead, n * steps + g, 0))

    def marks(lead, cores=1):
        return pl.BlockSpec(
            (cores, MARK_ROWS, half), lambda g, e, t, o: (lead, 3 * chunk * depth // MARK_ROWS, 0)
        )

    (first, first_row), (second, second_row) = following
    (prior0, prior0_row), (prior1, prior1_row) = prior
    specs = [marks(first_row), marks(second_row), marks(0, 2)]
    specs += [side(first_row, n) for n in range(3)] + [side(second_row, n) for n in range(3)]
    specs += [side(0, n, 2) for n in range(3)]
    for row in (prior0_row, prior1_row):
        specs += [side(row, n) for n in range(2)]
    pairs = chunk * (2 * half) * (6 * half)
    return pl.pallas_call(
        functools.partial(attention_kernel, score_scale=score_scale, parted=parted),
        grid_spec=pltpu.PrefetchScalarGridSpec(
            num_scalar_prefetch=3,
            grid=(steps,),
            in_specs=specs,
            out_specs=spec(3) + spec(3) + spec(2),
        ),
        out_shape=out(3) + out(3) + out(2),
        compiler_params=pltpu.CompilerParams(vmem_limit_bytes=PACK_VMEM),
        cost_estimate=pl.CostEstimate(
            flops=pairs * depth * 12, bytes_accessed=chunk * depth * half * 40, transcendentals=pairs
        ),
        name="attention",
    )(
        edge, turned, out_turn, first, second, own, *[first] * 3, *[second] * 3, *[own] * 3,
        *[prior0] * 2, *[prior1] * 2,
    )


def merge_kernel(kept_ref, from_prior_ref, *rest):
    *from_next_refs, out_ref = rest
    for n in range(3):
        total = kept_ref[:, :, n].astype(jnp.float32) + from_prior_ref[:, :, n].astype(jnp.float32)
        if n < 2:
            for ref in from_next_refs:
                total = total + ref[:, :, n].astype(jnp.float32)
        out_ref[:, :, n] = total.astype(jnp.bfloat16)


def merge(kept, from_prior, *from_next):
    _, chunk, _, depth, half = kept.shape

    def spec(kinds):
        return pl.BlockSpec((2, PER_STEP, kinds, depth, half), lambda g: (0, g, 0, 0, 0))

    return pl.pallas_call(
        merge_kernel,
        grid=(chunk // PER_STEP,),
        in_specs=[spec(3), spec(3)] + [spec(2)] * len(from_next),
        out_specs=spec(3),
        out_shape=jax.ShapeDtypeStruct(kept.shape, jnp.bfloat16),
        compiler_params=pltpu.CompilerParams(vmem_limit_bytes=PACK_VMEM),
        name="merge",
    )(kept, from_prior, *from_next)


def place_kernel(early_ref, out_q, out_k, out_v, sems):
    pieces = []
    for half in range(2):
        for n, out in enumerate((out_k, out_v, out_q)):
            pieces.append((early_ref.at[half, :, n], out.at[half, pl.ds(0, early_ref.shape[1])]))
    copies = [
        pltpu.make_async_copy(source, target, sems.at[i])
        for i, (source, target) in enumerate(pieces)
    ]
    for copy in copies:
        copy.start()
    for copy in copies:
        copy.wait()


def place(early, mine):
    _, _, _, depth, half = early.shape
    return pl.pallas_call(
        place_kernel,
        in_specs=[pl.BlockSpec(memory_space=pltpu.VMEM)],
        out_specs=[pl.BlockSpec(memory_space=pl.ANY)] * 3,
        out_shape=[jax.ShapeDtypeStruct((2, mine, depth, half), jnp.bfloat16)] * 3,
        scratch_shapes=[pltpu.SemaphoreType.DMA((6,))],
        compiler_params=pltpu.CompilerParams(vmem_limit_bytes=VMEM),
        name="place",
    )(early)


def finish_kernel(head_half_ref, kept_ref, from_prior_ref, from_next_ref, *refs):
    out_q, out_k, out_v = refs[3:]
    for n, out in enumerate((out_k, out_v, out_q)):
        total = kept_ref[:, n].astype(jnp.float32) + from_prior_ref[:, n].astype(jnp.float32)
        if n < 2:
            total = total + from_next_ref[:, n].astype(jnp.float32)
        out[0] = total.astype(jnp.bfloat16)


def finish(head_half, kept, from_prior, from_next, grads):
    chunk, _, depth, half = kept.shape
    before = (grads[0].shape[1] - chunk) // PER_STEP

    def spec(kinds):
        return pl.BlockSpec((PER_STEP, kinds, depth, half), lambda g, p: (g, 0, 0, 0))

    into = pl.BlockSpec((1, PER_STEP, depth, half), lambda g, p: (p[0], before + g, 0, 0))
    return pl.pallas_call(
        finish_kernel,
        grid_spec=pltpu.PrefetchScalarGridSpec(
            num_scalar_prefetch=1,
            grid=(chunk // PER_STEP,),
            in_specs=[spec(3), spec(3), spec(2)] + [pl.BlockSpec(memory_space=pl.ANY)] * 3,
            out_specs=[into] * 3,
        ),
        out_shape=[jax.ShapeDtypeStruct(x.shape, x.dtype) for x in grads],
        input_output_aliases={4: 0, 5: 1, 6: 2},
        compiler_params=pltpu.CompilerParams(vmem_limit_bytes=PACK_VMEM),
        name="finish",
    )(head_half, kept, from_prior, from_next, *grads)


def after(value, *earlier):
    return lax.optimization_barrier((value, *earlier))[0]


def shards(queries, keys, values, doc_start):
    heads, depth, half = queries.shape
    score_scale = 1.0 / math.sqrt(depth)
    ctx_count = lax.axis_size("ctx")
    head_count = lax.axis_size("head")
    mine = heads // 2
    pairs = [[2 * z, 2 * z + 1] for z in range(head_count // 2)]

    def cores(value):
        return lax.all_to_all(
            value, "head", split_axis=0, concat_axis=0, tiled=True, axis_index_groups=pairs
        )

    column_up = [
        (c * head_count + s, c * head_count + s + 2)
        for c in range(ctx_count)
        for s in range(head_count - 2)
    ]
    across = [
        (c * head_count - 2 + core, c * head_count + core)
        for c in range(1, ctx_count)
        for core in range(2)
    ]
    inner_up = [
        (c * head_count + s, c * head_count + s + 2)
        for c in range(ctx_count)
        for s in range(2, head_count - 4)
    ]
    column_down = [(t, s) for s, t in column_up]
    inner_down = [(t, s) for s, t in inner_up]
    across_down = [(t, s) for s, t in across]
    flat = ("ctx", "head")
    begins = (0, CHUNKS[0])
    by_core = (2, mine, depth, half)
    keys, values, queries = (x.reshape(by_core) for x in (keys, values, queries))
    position = (lax.axis_index("ctx") * head_count + lax.axis_index("head")) * half
    first = position.astype(jnp.int32).reshape(1)
    starts = doc_start.reshape(1, half)

    parity = (lax.axis_index("head") % 2).astype(jnp.int32).reshape(1)
    edge = (lax.axis_index("head") < 2).astype(jnp.int32).reshape(1)

    def packed(c):
        return pack(first, parity, starts, keys, values, queries, begins[c], CHUNKS[c], c == 0)

    own, following, prior, to_next, kept, to_prior, back_next, back_prior, done = (
        [None, None] for _ in range(9)
    )
    crossed_down = [(t, s ^ 1) for s, t in column_up]
    by_halves, same, crossed, same_pair, crossed_pair = packed(0)
    same = lax.ppermute(same, flat, column_down)
    crossed = lax.ppermute(crossed, flat, crossed_down)
    following[0] = ((same, 0), (crossed, 0))
    same_pair = lax.ppermute(same_pair, flat, inner_up + across)
    crossed_pair = lax.ppermute(crossed_pair, flat, [(s, t ^ 1) for s, t in inner_up + across])
    prior[0] = ((same_pair, 0), (crossed_pair, 0))
    own[1] = cores(packed(1)[0])
    own[0] = cores(after(by_halves, own[1]))
    gone = lax.ppermute(after(own[1][:, : 2 * CHUNKS[1] * depth], same), flat, inner_up + across)
    prior[1] = ((gone, 0), (gone, 1))
    came = lax.ppermute(after(own[1], same, crossed, own[0], same_pair, crossed_pair), flat, column_down)
    following[1] = ((came, 0), (came, 1))

    nothing = jnp.zeros_like(parity)
    to_next[0], kept[0], to_prior[0] = attention(
        edge, parity, nothing, following[0], own[0], prior[0], score_scale, depth, False,
    )
    far_end = lax.ppermute(to_prior[0], flat, across_down)
    back_next[0] = lax.ppermute(after(to_next[0], gone), flat, column_up)
    back_prior[0] = lax.ppermute(after(to_prior[0], came, far_end), flat, inner_down)
    next_same, next_crossed, kept_same, kept_crossed, prior_same, prior_crossed = attention(
        edge, nothing, parity, following[1], own[1], prior[1], score_scale, depth, True
    )
    crossed_column = [(s, t ^ 1) for s, t in column_up]
    down = inner_down + across_down
    next_same = lax.ppermute(after(next_same, back_next[0]), flat, column_up)
    next_crossed = lax.ppermute(after(next_crossed, back_next[0]), flat, crossed_column)
    prior_same = lax.ppermute(after(prior_same, back_prior[0]), flat, down)
    prior_crossed = lax.ppermute(
        after(prior_crossed, back_prior[0]), flat, [(s, t ^ 1) for s, t in down]
    )
    kept_crossed = lax.ppermute(kept_crossed, "head", [(s, s ^ 1) for s in range(head_count)])
    early = cores(merge(kept[0], back_next[0], back_prior[0], far_end))
    grads = place(early, mine)
    grads = finish(parity, kept_same, next_same, prior_same, grads)
    grads = finish(1 - parity, kept_crossed, next_crossed, prior_crossed, grads)
    return tuple(x.reshape(heads, depth, half) for x in grads)


def solution(mesh):
    return jax.shard_map(
        shards,
        mesh=mesh,
        in_specs=(
            P(None, None, ("ctx", "head")),
            P(None, None, ("ctx", "head")),
            P(None, None, ("ctx", "head")),
            P(("ctx", "head")),
        ),
        out_specs=(
            P(None, None, ("ctx", "head")),
            P(None, None, ("ctx", "head")),
            P(None, None, ("ctx", "head")),
        ),
        check_vma=False,
    )
```

time: 131 us -> 120 us (0.916)
  Pallas kernels: 22.3 us -> 35.5 us
  waiting for transfers between devices: 41.4 us -> 32.4 us
  local copies, waits for them, and re-layouts: 12.7 us -> 3.81 us
  starting transfers between devices: 35.1 us -> 26.4 us
  blocking collectives: 17.9 us -> 19.3 us
    pallas_call x3 -> x5, Pallas kernels: 1.8 us -> 12.8 us  [the longest x2 7.58 us: pack(): pl.pallas_call(functools.partial(pack_kernel, begin=begin * depth, rows=r...]
    ppermute x8 -> x14, waiting for transfers between devices: 41.4 us -> 32.4 us  [the longest x1 15.5 us: shards(): far_end = lax.ppermute(to_prior[0], flat, across_down)]
    unnamed x20 -> x30, local copies, waits for them, and re-layouts: 10.6 us -> 2.88 us
    all_to_all x1 -> x0, starting transfers between devices: 6.92 us -> none  [cores(): lax.all_to_all(value, 'head', split_axis=0, concat_axis=0, tiled=True, ax...]
    pallas_call x2, Pallas kernels: 17.5 us -> 19.6 us  [attention(): pl.pallas_call(functools.partial(attention_kernel, score_scale=score_scal...]
    ppermute x8 -> x14, starting transfers between devices: 28.2 us -> 26.4 us  [the longest x1 4.36 us: shards(): far_end = lax.ppermute(to_prior[0], flat, across_down)]
    all_to_all x3, blocking collectives: 17.9 us -> 19.3 us  [cores(): lax.all_to_all(value, 'head', split_axis=0, concat_axis=0, tiled=True, ax...]
    pallas_call x2 -> x1, Pallas kernels: 3.02 us -> 3.16 us  [merge(): pl.pallas_call(merge_kernel, grid=(chunk // PER_STEP,), in_specs=[spec(3)...]
  transfers between devices with their start and end apart: 9 -> 14, of which waited for: 7 -> 6; matrix products, arithmetic and copies ran while one was open for 2% -> 1% of each run, Pallas kernels for 16% -> 25%
where the time goes in v3:
time: 120 us; the launch traced here: 118 us
  Pallas kernels  35.5 us (30%)
  waiting for transfers between devices  32.4 us (27%)
  starting transfers between devices  26.4 us (22%)
  blocking collectives  19.3 us (16%)
  local copies, waits for them, and re-layouts  3.81 us (3%)
    pallas_call x2, Pallas kernels, attention(): pl.pallas_call(functools.partial(attention_kernel, score_scale=score_scal...  19.6 us
    all_to_all x3, blocking collectives, cores(): lax.all_to_all(value, 'head', split_axis=0, concat_axis=0, tiled=True, ax...  19.3 us
    ppermute x1, waiting for transfers between devices, shards(): far_end = lax.ppermute(to_prior[0], flat, across_down)  15.5 us
    ppermute x1, waiting for transfers between devices, shards(): lax.ppermute(crossed_pair, flat, [(s, t ^ 1) for s, t in inner_up + across])  8.19 us
    pallas_call x2, Pallas kernels, pack(): pl.pallas_call(functools.partial(pack_kernel, begin=begin * depth, rows=r...  7.58 us
    ppermute x1, starting transfers between devices, shards(): far_end = lax.ppermute(to_prior[0], flat, across_down)  4.36 us
    pallas_call x2, Pallas kernels, finish(): pl.pallas_call(finish_kernel, grid_spec=pltpu.PrefetchScalarGridSpec(num_...  4.18 us
    ppermute x1, waiting for transfers between devices, shards(): same_pair = lax.ppermute(same_pair, flat, inner_up + across)  3.9 us
  transfers between devices with their start and end apart: 14, of which 6 were waited for; matrix products, arithmetic and copies ran while one was open for 1% of the time, Pallas kernels for 25%

profile of v3, /device:TPU:25, one launch (start us, length us, event | category | flops | bytes accessed | tf_op | source)
XLA Modules:
  0.0 118.4 jit_solution(11374162371019567908)
XLA Ops:
  0.6 4.4 %pack.3 = (bf16[2,2320,128]{2,1,0:T(8,128)(2,1)}, bf16[1,2320,128]{2,1,0:T(8,128)(2,1)}, bf16[1,2320,128]{2,1,0:T(8,128)(2,1)}, bf16[1,1536,128]{2,1,0:T(8,128)(2,1)}, bf16[1,1536,128]{2,1,0:T(8,128)(2,1)}) custom-call(s32[1]{0:T(128)} %bitcast.2.first_ref, s32[1]{0:T(128)} %bitcast.parity_ref.out_turn_ref.turned_ref.head_half_ref, s32[1,128]{1,0:T(1,128)} %bitcast.19, ...), custom_call_target="tpu_custom_call" | custom-call | tf_op jit(solution)/shard_map/pack/pallas_call | solution.py:73
  5.1 1.3 %collective-permute-start = (bf16[1,2320,128]{2,1,0:T(8,128)(2,1)}, bf16[1,2320,128]{2,1,0:T(8,128)(2,1)S(1)}, u32[]{:S(2)}, u32[]{:S(2)}) collective-permute-start(bf16[1,2320,128]{2,1,0:T(8,128)(2,1)} %get-tuple-element.35), channel_id=1, source_target_pairs={{2,0},{3,1},{4,2},{5,3},{6,4},{7,5},{8,6},{9,7},{10,8},{11,9},{12,... | collective-permute-start | bytes 1781768 | tf_op jit(solution)/shard_map/ppermute | solution.py:434
  6.4 1.3 %collective-permute-start.1 = (bf16[1,2320,128]{2,1,0:T(8,128)(2,1)}, bf16[1,2320,128]{2,1,0:T(8,128)(2,1)}, u32[]{:S(2)}, u32[]{:S(2)}) collective-permute-start(bf16[1,2320,128]{2,1,0:T(8,128)(2,1)} %get-tuple-element.36), channel_id=1, source_target_pairs={{2,1},{3,0},{4,3},{5,2},{6,5},{7,4},{8,7},{9,6},{10,9},{11,8},{12,... | collective-permute-start | bytes 1781768 | tf_op jit(solution)/shard_map/ppermute | solution.py:435
  7.7 1.3 %collective-permute-start.2 = (bf16[1,1536,128]{2,1,0:T(8,128)(2,1)}, bf16[1,1536,128]{2,1,0:T(8,128)(2,1)S(1)}, u32[]{:S(2)}, u32[]{:S(2)}) collective-permute-start(bf16[1,1536,128]{2,1,0:T(8,128)(2,1)} %get-tuple-element.39), channel_id=1, source_target_pairs={{2,4},{3,5},{4,6},{5,7},{6,8},{7,9},{8,10},{9,11},{10,12},{11,13},... | collective-permute-start | bytes 1179656 | tf_op jit(solution)/shard_map/ppermute | solution.py:437
  9.0 1.3 %collective-permute-start.3 = (bf16[1,1536,128]{2,1,0:T(8,128)(2,1)}, bf16[1,1536,128]{2,1,0:T(8,128)(2,1)S(1)}, u32[]{:S(2)}, u32[]{:S(2)}) collective-permute-start(bf16[1,1536,128]{2,1,0:T(8,128)(2,1)} %get-tuple-element.40), channel_id=1, source_target_pairs={{2,5},{3,4},{4,7},{5,6},{6,9},{7,8},{8,11},{9,10},{10,13},{11,12},... | collective-permute-start | bytes 1179656 | tf_op jit(solution)/shard_map/ppermute | solution.py:438
  10.3 3.2 %pack.2 = bf16[2,2320,128]{2,1,0:T(8,128)(2,1)} custom-call(s32[1]{0:T(128)} %bitcast.2.first_ref, s32[1]{0:T(128)} %bitcast.parity_ref.out_turn_ref.turned_ref.head_half_ref, s32[1,128]{1,0:T(1,128)} %bitcast.20, bf16[2,1536,128]{2,1,0:T(8,128)(2,1)} %bitcast.11, bf16[2,1536,128]{2,1,0:T(8,128)(2,1)} %bitcast.13, bf16[2,1536,128]{2,1,0:T(8,128)(2,1)} %bitcast.15), custom_call_target="tpu_custom_call" | custom-call | tf_op jit(solution)/shard_map/pack/pallas_call | solution.py:73
  13.4 6.1 %all_to_all.15.refs_2_.refs_9_.refs_10_.refs_11_ = bf16[2,2320,128]{2,1,0:T(8,128)(2,1)S(1)} all-to-all(bf16[2,2320,128]{2,1,0:T(8,128)(2,1)} %pack.2), channel_id=1, replica_groups={{0,1},{2,3},{4,5},{6,7},{8,9},{10,11},{12,13},{14,15},{16,17},{18,19},{..., dimensions={0} | all-to-all | bytes 2375680 | tf_op jit(solution)/shard_map/all_to_all | solution.py:393
  19.6 0.9 slice.4
  20.5 1.3 %collective-permute-done.refs_0_.refs_3_.refs_4_.refs_5_ = bf16[1,2320,128]{2,1,0:T(8,128)(2,1)S(1)} collective-permute-done((bf16[1,2320,128]{2,1,0:T(8,128)(2,1)}, bf16[1,2320,128]{2,1,0:T(8,128)(2,1)S(1)}, u32[]{:S(2)}, u32[]{:S(2)}) %collective-permute-start) | collective-permute-done | bytes 593952 | tf_op jit(solution)/shard_map/ppermute | solution.py:434
  21.8 1.3 %collective-permute-start.5 = (bf16[2,1536,128]{2,1,0:T(8,128)(2,1)}, bf16[2,1536,128]{2,1,0:T(8,128)(2,1)S(1)}, u32[]{:S(2)}, u32[]{:S(2)}) collective-permute-start(bf16[2,1536,128]{2,1,0:T(8,128)(2,1)} %slice.4), channel_id=1, source_target_pairs={{2,4},{3,5},{4,6},{5,7},{6,8},{7,9},{8,10},{9,11},{10,12},{11,13},... | collective-permute-start | bytes 2359304 | tf_op jit(solution)/shard_map/ppermute | solution.py:442
  23.1 7.4 %all_to_all.16.refs_2_.refs_9_.refs_10_.refs_11_ = bf16[2,2320,128]{2,1,0:T(8,128)(2,1)} all-to-all(bf16[2,2320,128]{2,1,0:T(8,128)(2,1)S(1)} %copy-done.6), channel_id=1, replica_groups={{0,1},{2,3},{4,5},{6,7},{8,9},{10,11},{12,13},{14,15},{16,17},{18,19},{..., dimensions={0} | all-to-all | bytes 2375680 | tf_op jit(solution)/shard_map/all_to_all | solution.py:393
  30.6 3.9 %collective-permute-done.2.refs_12_.refs_13_ = bf16[1,1536,128]{2,1,0:T(8,128)(2,1)S(1)} collective-permute-done((bf16[1,1536,128]{2,1,0:T(8,128)(2,1)}, bf16[1,1536,128]{2,1,0:T(8,128)(2,1)S(1)}, u32[]{:S(2)}, u32[]{:S(2)}) %collective-permute-start.2) | collective-permute-done | bytes 393248 | tf_op jit(solution)/shard_map/ppermute | solution.py:437
  34.5 8.2 %collective-permute-done.3.refs_14_.refs_15_ = bf16[1,1536,128]{2,1,0:T(8,128)(2,1)S(1)} collective-permute-done((bf16[1,1536,128]{2,1,0:T(8,128)(2,1)}, bf16[1,1536,128]{2,1,0:T(8,128)(2,1)S(1)}, u32[]{:S(2)}, u32[]{:S(2)}) %collective-permute-start.3) | collective-permute-done | bytes 393248 | tf_op jit(solution)/shard_map/ppermute | solution.py:438
  42.7 0.8 copy-done.5
  43.4 1.3 %collective-permute-start.4 = (bf16[2,2320,128]{2,1,0:T(8,128)(2,1)S(1)}, bf16[2,2320,128]{2,1,0:T(8,128)(2,1)S(1)}, u32[]{:S(2)}, u32[]{:S(2)}) collective-permute-start(bf16[2,2320,128]{2,1,0:T(8,128)(2,1)S(1)} %all_to_all.15.refs_2_.refs_9_.refs_10_.refs_11_), channel_id=1, source_target_pairs={{2,0},{3,1},{4,2},{5,3},{6,4},{7,5},{8,6},{9,7},{10,8},{11,9},{12,... | collective-permute-start | bytes 3563528 | tf_op jit(solution)/shard_map/ppermute | solution.py:444
  44.7 9.8 %attention.3 = (bf16[2,8,3,96,128]{4,3,2,1,0:T(8,128)(2,1)}, bf16[2,8,3,96,128]{4,3,2,1,0:T(8,128)(2,1)}, bf16[2,8,2,96,128]{4,3,2,1,0:T(8,128)(2,1)}) custom-call(s32[1]{0:T(128)} %bitcast.1.edge_ref, s32[1]{0:T(128)} %bitcast.parity_ref.out_turn_ref.turned_ref.head_half_ref, s32[1]{0:T(128)} %constant.25.clone.1.turned_ref.out_turn_ref, ...), custom_call_target="tpu_custom_call" | custom-call | flops 1811939328 | bytes 3932160 | tf_op jit(solution)/shard_map/attention/pallas_call | solution.py:273
  54.5 4.4 %collective-permute-start.9 = (bf16[2,8,2,96,128]{4,3,2,1,0:T(8,128)(2,1)}, bf16[2,8,2,96,128]{4,3,2,1,0:T(8,128)(2,1)S(1)}, u32[]{:S(2)}, u32[]{:S(2)}) collective-permute-start(bf16[2,8,2,96,128]{4,3,2,1,0:T(8,128)(2,1)} %get-tuple-element.50), channel_id=1, source_target_pairs={{32,30},{33,31},{64,62},{65,63},{96,94},{97,95},{128,126},{129,127... | collective-permute-start | bytes 2359304 | tf_op jit(solution)/shard_map/ppermute | solution.py:451
  59.5 1.4 %collective-permute-start.7 = (bf16[2,8,3,96,128]{4,3,2,1,0:T(8,128)(2,1)}, bf16[2,8,3,96,128]{4,3,2,1,0:T(8,128)(2,1)S(1)}, u32[]{:S(2)}, u32[]{:S(2)}) collective-permute-start(bf16[2,8,3,96,128]{4,3,2,1,0:T(8,128)(2,1)} %get-tuple-element.46), channel_id=1, source_target_pairs={{0,2},{1,3},{2,4},{3,5},{4,6},{5,7},{6,8},{7,9},{8,10},{9,11},{10,... | collective-permute-start | bytes 3538952 | tf_op jit(solution)/shard_map/ppermute | solution.py:452
  60.9 15.5 %collective-permute-done.9.rest_1_ = bf16[2,8,2,96,128]{4,3,2,1,0:T(8,128)(2,1)S(1)} collective-permute-done((bf16[2,8,2,96,128]{4,3,2,1,0:T(8,128)(2,1)}, bf16[2,8,2,96,128]{4,3,2,1,0:T(8,128)(2,1)S(1)}, u32[]{:S(2)}, u32[]{:S(2)}) %collective-permute-start.9) | collective-permute-done | bytes 786464 | tf_op jit(solution)/shard_map/ppermute | solution.py:451
  76.4 0.9 collective-permute-start.10
  77.5 9.8 %attention.2 = (bf16[8,3,96,128]{3,2,1,0:T(8,128)(2,1)}, bf16[8,3,96,128]{3,2,1,0:T(8,128)(2,1)}, bf16[8,3,96,128]{3,2,1,0:T(8,128)(2,1)}, bf16[8,3,96,128]{3,2,...) custom-call(s32[1]{0:T(128)} %bitcast.1.edge_ref, ...), custom_call_target="tpu_custom_call" | custom-call | flops 1811939328 | bytes 3932160 | tf_op jit(solution)/shard_map/attention/pallas_call | solution.py:273
  87.3 3.1 %collective-permute-start.12 = (bf16[8,3,96,128]{3,2,1,0:T(8,128)(2,1)}, bf16[8,3,96,128]{3,2,1,0:T(8,128)(2,1)S(1)}, u32[]{:S(2)}, u32[]{:S(2)}) collective-permute-start(bf16[8,3,96,128]{3,2,1,0:T(8,128)(2,1)} %get-tuple-element.54), channel_id=1, source_target_pairs={{0,2},{1,3},{2,4},{3,5},{4,6},{5,7},{6,8},{7,9},{8,10},{9,11},{10,... | collective-permute-start | bytes 1769480 | tf_op jit(solution)/shard_map/ppermute | solution.py:459
  90.4 3.1 %collective-permute-start.6 = (bf16[8,3,96,128]{3,2,1,0:T(8,128)(2,1)}, bf16[8,3,96,128]{3,2,1,0:T(8,128)(2,1)S(1)}, u32[]{:S(2)}, u32[]{:S(2)}) collective-permute-start(bf16[8,3,96,128]{3,2,1,0:T(8,128)(2,1)} %get-tuple-element.43), channel_id=1, source_target_pairs={{0,1},{1,0},{2,3},{3,2},{4,5},{5,4},{6,7},{7,6},{8,9},{9,8},{10,11... | collective-permute-start | bytes 1769480 | tf_op jit(solution)/shard_map/ppermute | solution.py:465
  93.5 1.5 %collective-permute-start.8 = (bf16[8,3,96,128]{3,2,1,0:T(8,128)(2,1)}, bf16[8,3,96,128]{3,2,1,0:T(8,128)(2,1)S(1)}, u32[]{:S(2)}, u32[]{:S(2)}) collective-permute-start(bf16[8,3,96,128]{3,2,1,0:T(8,128)(2,1)} %get-tuple-element.47), channel_id=1, source_target_pairs={{0,3},{1,2},{2,5},{3,4},{4,7},{5,6},{6,9},{7,8},{8,11},{9,10},{10,... | collective-permute-start | bytes 1769480 | tf_op jit(solution)/shard_map/ppermute | solution.py:460
  95.1 3.0 %collective-permute-start.13 = (bf16[8,2,96,128]{3,2,1,0:T(8,128)(2,1)}, bf16[8,2,96,128]{3,2,1,0:T(8,128)(2,1)S(1)}, u32[]{:S(2)}, u32[]{:S(2)}) collective-permute-start(bf16[8,2,96,128]{3,2,1,0:T(8,128)(2,1)} %get-tuple-element.56), channel_id=1, source_target_pairs={{4,2},{5,3},{6,4},{7,5},{8,6},{9,7},{10,8},{11,9},{12,10},{13,11},... | collective-permute-start | bytes 1179656 | tf_op jit(solution)/shard_map/ppermute | solution.py:461
  98.1 1.3 %collective-permute-start.11 = (bf16[8,2,96,128]{3,2,1,0:T(8,128)(2,1)}, bf16[8,2,96,128]{3,2,1,0:T(8,128)(2,1)S(1)}, u32[]{:S(2)}, u32[]{:S(2)}) collective-permute-start(bf16[8,2,96,128]{3,2,1,0:T(8,128)(2,1)} %get-tuple-element.51), channel_id=1, source_target_pairs={{4,3},{5,2},{6,5},{7,4},{8,7},{9,6},{10,9},{11,8},{12,11},{13,10},... | collective-permute-start | bytes 1179656 | tf_op jit(solution)/shard_map/ppermute | solution.py:462
  99.4 3.2 %merge.1 = bf16[2,8,3,96,128]{4,3,2,1,0:T(8,128)(2,1)} custom-call(bf16[2,8,3,96,128]{4,3,2,1,0:T(8,128)(2,1)} %get-tuple-element.57.kept_ref, bf16[2,8,3,96,128]{4,3,2,1,0:T(8,128)(2,1)} %copy-done.7, bf16[2,8,2,96,128]{4,3,2,1,0:T(8,128)(2,1)} %copy-done.9, bf16[2,8,2,96,128]{4,3,2,1,0:T(8,128)(2,1)} %copy-done.8), custom_call_target="tpu_custom_call" | custom-call | tf_op jit(solution)/shard_map/merge/pallas_call | solution.py:309
  102.6 5.8 %all_to_all.17.early_ref = bf16[2,8,3,96,128]{4,3,2,1,0:T(8,128)(2,1)S(1)} all-to-all(bf16[2,8,3,96,128]{4,3,2,1,0:T(8,128)(2,1)} %merge.1), channel_id=1, replica_groups={{0,1},{2,3},{4,5},{6,7},{8,9},{10,11},{12,13},{14,15},{16,17},{18,19},{..., dimensions={0} | all-to-all | bytes 2359296 | tf_op jit(solution)/shard_map/all_to_all | solution.py:393
  108.4 1.0 place.1
  110.4 2.1 %finish.2 = (bf16[2,16,96,128]{3,2,1,0:T(8,128)(2,1)}, bf16[2,16,96,128]{3,2,1,0:T(8,128)(2,1)}, bf16[2,16,96,128]{3,2,1,0:T(8,128)(2,1)}) custom-call(s32[1]{0:T(128)} %bitcast.parity_ref.out_turn_ref.turned_ref.head_half_ref, bf16[8,3,96,128]{3,2,1,0:T(8,128)(2,1)} %get-tuple-element.52.kept_ref, ...), custom_call_target="tpu_custom_call", output_to_operand_aliasing={{0}: (4, {}), {1}: (5, {}), {2}: (6, {})} | custom-call | tf_op jit(solution)/shard_map/finish/pallas_call | solution.py:365
  112.5 2.8 %collective-permute-done.11.from_next_ref = bf16[8,2,96,128]{3,2,1,0:T(8,128)(2,1)S(1)} collective-permute-done((bf16[8,2,96,128]{3,2,1,0:T(8,128)(2,1)}, bf16[8,2,96,128]{3,2,1,0:T(8,128)(2,1)S(1)}, u32[]{:S(2)}, u32[]{:S(2)}) %collective-permute-start.11) | collective-permute-done | bytes 393248 | tf_op jit(solution)/shard_map/ppermute | solution.py:462
  116.3 2.1 %finish.3 = (bf16[2,16,96,128]{3,2,1,0:T(8,128)(2,1)}, bf16[2,16,96,128]{3,2,1,0:T(8,128)(2,1)}, bf16[2,16,96,128]{3,2,1,0:T(8,128)(2,1)}) custom-call(s32[1]{0:T(128)S(6)} %sub.3.head_half_ref, bf16[8,3,96,128]{3,2,1,0:T(8,128)(2,1)} %copy-done.10, bf16[8,3,96,128]{3,2,1,0:T(8,128)(2,1)} %copy-done.11, ...), custom_call_target="tpu_custom_call", output_to_operand_aliasing={{0}: (4, {}), {1}: (5, {}), {2}: (6, {})} | custom-call | tf_op jit(solution)/shard_map/finish/pallas_call | solution.py:365
  (38 shorter events, 2.8 us)
Async XLA Ops:
  5.1 16.8 %collective-permute-start = (bf16[1,2320,128]{2,1,0:T(8,128)(2,1)}, bf16[1,2320,128]{2,1,0:T(8,128)(2,1)S(1)}, u32[]{:S(2)}, u32[]{:S(2)}) collective-permute-start(bf16[1,2320,128]{2,1,0:T(8,128)(2,1)} %get-tuple-element.35), channel_id=1, source_target_pairs={{2,0},{3,1},{4,2},{5,3},{6,4},{7,5},{8,6},{9,7},{10,8},{11,9},{12,... | collective-permute-start | bytes 1781768 | tf_op jit(solution)/shard_map/ppermute | solution.py:434
  6.4 37.1 %collective-permute-start.1 = (bf16[1,2320,128]{2,1,0:T(8,128)(2,1)}, bf16[1,2320,128]{2,1,0:T(8,128)(2,1)}, u32[]{:S(2)}, u32[]{:S(2)}) collective-permute-start(bf16[1,2320,128]{2,1,0:T(8,128)(2,1)} %get-tuple-element.36), channel_id=1, source_target_pairs={{2,1},{3,0},{4,3},{5,2},{6,5},{7,4},{8,7},{9,6},{10,9},{11,8},{12,... | collective-permute-start | bytes 1781768 | tf_op jit(solution)/shard_map/ppermute | solution.py:435
  7.7 26.8 %collective-permute-start.2 = (bf16[1,1536,128]{2,1,0:T(8,128)(2,1)}, bf16[1,1536,128]{2,1,0:T(8,128)(2,1)S(1)}, u32[]{:S(2)}, u32[]{:S(2)}) collective-permute-start(bf16[1,1536,128]{2,1,0:T(8,128)(2,1)} %get-tuple-element.39), channel_id=1, source_target_pairs={{2,4},{3,5},{4,6},{5,7},{6,8},{7,9},{8,10},{9,11},{10,12},{11,13},... | collective-permute-start | bytes 1179656 | tf_op jit(solution)/shard_map/ppermute | solution.py:437
  9.0 33.7 %collective-permute-start.3 = (bf16[1,1536,128]{2,1,0:T(8,128)(2,1)}, bf16[1,1536,128]{2,1,0:T(8,128)(2,1)S(1)}, u32[]{:S(2)}, u32[]{:S(2)}) collective-permute-start(bf16[1,1536,128]{2,1,0:T(8,128)(2,1)} %get-tuple-element.40), channel_id=1, source_target_pairs={{2,5},{3,4},{4,7},{5,6},{6,9},{7,8},{8,11},{9,10},{10,13},{11,12},... | collective-permute-start | bytes 1179656 | tf_op jit(solution)/shard_map/ppermute | solution.py:438
  19.6 23.9 %copy-start.1 = (bf16[2,2320,128]{2,1,0:T(8,128)(2,1)}, bf16[2,2320,128]{2,1,0:T(8,128)(2,1)S(1)}, u32[]{:S(2)}) copy-start(bf16[2,2320,128]{2,1,0:T(8,128)(2,1)S(1)} %all_to_all.15.refs_2_.refs_9_.refs_10_.refs_11_) | copy-start | bytes 3563524
  19.6 3.6 %copy-start.6 = (bf16[2,2320,128]{2,1,0:T(8,128)(2,1)S(1)}, bf16[2,2320,128]{2,1,0:T(8,128)(2,1)}, u32[]{:S(2)}) copy-start(bf16[2,2320,128]{2,1,0:T(8,128)(2,1)} %get-tuple-element.38) | copy-start | bytes 3563524
  21.8 8.7 %copy-start.3 = (bf16[1,2320,128]{2,1,0:T(8,128)(2,1)}, bf16[1,2320,128]{2,1,0:T(8,128)(2,1)S(1)}, u32[]{:S(2)}) copy-start(bf16[1,2320,128]{2,1,0:T(8,128)(2,1)S(1)} %collective-permute-done.refs_0_.refs_3_.refs_4_.refs_5_) | copy-start | bytes 1781764
  21.8 37.7 %collective-permute-start.5 = (bf16[2,1536,128]{2,1,0:T(8,128)(2,1)}, bf16[2,1536,128]{2,1,0:T(8,128)(2,1)S(1)}, u32[]{:S(2)}, u32[]{:S(2)}) collective-permute-start(bf16[2,1536,128]{2,1,0:T(8,128)(2,1)} %slice.4), channel_id=1, source_target_pairs={{2,4},{3,5},{4,6},{5,7},{6,8},{7,9},{8,10},{9,11},{10,12},{11,13},... | collective-permute-start | bytes 2359304 | tf_op jit(solution)/shard_map/ppermute | solution.py:442
  34.5 10.3 %copy-start.4 = (bf16[1,1536,128]{2,1,0:T(8,128)(2,1)}, bf16[1,1536,128]{2,1,0:T(8,128)(2,1)S(1)}, u32[]{:S(2)}) copy-start(bf16[1,1536,128]{2,1,0:T(8,128)(2,1)S(1)} %collective-permute-done.2.refs_12_.refs_13_) | copy-start | bytes 1179652
  42.7 0.8 copy-start.5
  43.4 33.0 %collective-permute-start.4 = (bf16[2,2320,128]{2,1,0:T(8,128)(2,1)S(1)}, bf16[2,2320,128]{2,1,0:T(8,128)(2,1)S(1)}, u32[]{:S(2)}, u32[]{:S(2)}) collective-permute-start(bf16[2,2320,128]{2,1,0:T(8,128)(2,1)S(1)} %all_to_all.15.refs_2_.refs_9_.refs_10_.refs_11_), channel_id=1, source_target_pairs={{2,0},{3,1},{4,2},{5,3},{6,4},{7,5},{8,6},{9,7},{10,8},{11,9},{12,... | collective-permute-start | bytes 3563528 | tf_op jit(solution)/shard_map/ppermute | solution.py:444
  54.5 21.9 %collective-permute-start.9 = (bf16[2,8,2,96,128]{4,3,2,1,0:T(8,128)(2,1)}, bf16[2,8,2,96,128]{4,3,2,1,0:T(8,128)(2,1)S(1)}, u32[]{:S(2)}, u32[]{:S(2)}) collective-permute-start(bf16[2,8,2,96,128]{4,3,2,1,0:T(8,128)(2,1)} %get-tuple-element.50), channel_id=1, source_target_pairs={{32,30},{33,31},{64,62},{65,63},{96,94},{97,95},{128,126},{129,127... | collective-permute-start | bytes 2359304 | tf_op jit(solution)/shard_map/ppermute | solution.py:451
  59.5 17.8 %copy-start.2 = (bf16[2,1536,128]{2,1,0:T(8,128)(2,1)}, bf16[2,1536,128]{2,1,0:T(8,128)(2,1)S(1)}, u32[]{:S(2)}) copy-start(bf16[2,1536,128]{2,1,0:T(8,128)(2,1)S(1)} %collective-permute-done.5.refs_12_.refs_13_.refs_14_.refs_15_) | copy-start | bytes 2359300
  59.5 27.7 %collective-permute-start.7 = (bf16[2,8,3,96,128]{4,3,2,1,0:T(8,128)(2,1)}, bf16[2,8,3,96,128]{4,3,2,1,0:T(8,128)(2,1)S(1)}, u32[]{:S(2)}, u32[]{:S(2)}) collective-permute-start(bf16[2,8,3,96,128]{4,3,2,1,0:T(8,128)(2,1)} %get-tuple-element.46), channel_id=1, source_target_pairs={{0,2},{1,3},{2,4},{3,5},{4,6},{5,7},{6,8},{7,9},{8,10},{9,11},{10,... | collective-permute-start | bytes 3538952 | tf_op jit(solution)/shard_map/ppermute | solution.py:452
  76.4 10.8 %copy-start.8 = (bf16[2,8,2,96,128]{4,3,2,1,0:T(8,128)(2,1)}, bf16[2,8,2,96,128]{4,3,2,1,0:T(8,128)(2,1)S(1)}, u32[]{:S(2)}) copy-start(bf16[2,8,2,96,128]{4,3,2,1,0:T(8,128)(2,1)S(1)} %collective-permute-done.9.rest_1_) | copy-start | bytes 2359300
  76.4 1.1 copy-start
  76.4 18.6 %collective-permute-start.10 = (bf16[2,8,2,96,128]{4,3,2,1,0:T(8,128)(2,1)}, bf16[2,8,2,96,128]{4,3,2,1,0:T(8,128)(2,1)S(1)}, u32[]{:S(2)}, u32[]{:S(2)}) collective-permute-start(bf16[2,8,2,96,128]{4,3,2,1,0:T(8,128)(2,1)} %get-tuple-element.50), channel_id=1, source_target_pairs={{4,2},{5,3},{6,4},{7,5},{8,6},{9,7},{10,8},{11,9},{12,10},{13,11},... | collective-permute-start | bytes 2359304 | tf_op jit(solution)/shard_map/ppermute | solution.py:453
  87.3 12.1 %copy-start.7 = (bf16[2,8,3,96,128]{4,3,2,1,0:T(8,128)(2,1)}, bf16[2,8,3,96,128]{4,3,2,1,0:T(8,128)(2,1)S(1)}, u32[]{:S(2)}) copy-start(bf16[2,8,3,96,128]{4,3,2,1,0:T(8,128)(2,1)S(1)} %collective-permute-done.7.from_prior_ref) | copy-start | bytes 3538948
  87.3 22.2 %collective-permute-start.12 = (bf16[8,3,96,128]{3,2,1,0:T(8,128)(2,1)}, bf16[8,3,96,128]{3,2,1,0:T(8,128)(2,1)S(1)}, u32[]{:S(2)}, u32[]{:S(2)}) collective-permute-start(bf16[8,3,96,128]{3,2,1,0:T(8,128)(2,1)} %get-tuple-element.54), channel_id=1, source_target_pairs={{0,2},{1,3},{2,4},{3,5},{4,6},{5,7},{6,8},{7,9},{8,10},{9,11},{10,... | collective-permute-start | bytes 1769480 | tf_op jit(solution)/shard_map/ppermute | solution.py:459
  90.4 22.1 %collective-permute-start.6 = (bf16[8,3,96,128]{3,2,1,0:T(8,128)(2,1)}, bf16[8,3,96,128]{3,2,1,0:T(8,128)(2,1)S(1)}, u32[]{:S(2)}, u32[]{:S(2)}) collective-permute-start(bf16[8,3,96,128]{3,2,1,0:T(8,128)(2,1)} %get-tuple-element.43), channel_id=1, source_target_pairs={{0,1},{1,0},{2,3},{3,2},{4,5},{5,4},{6,7},{7,6},{8,9},{9,8},{10,11... | collective-permute-start | bytes 1769480 | tf_op jit(solution)/shard_map/ppermute | solution.py:465
  93.5 21.8 %collective-permute-start.8 = (bf16[8,3,96,128]{3,2,1,0:T(8,128)(2,1)}, bf16[8,3,96,128]{3,2,1,0:T(8,128)(2,1)S(1)}, u32[]{:S(2)}, u32[]{:S(2)}) collective-permute-start(bf16[8,3,96,128]{3,2,1,0:T(8,128)(2,1)} %get-tuple-element.47), channel_id=1, source_target_pairs={{0,3},{1,2},{2,5},{3,4},{4,7},{5,6},{6,9},{7,8},{8,11},{9,10},{10,... | collective-permute-start | bytes 1769480 | tf_op jit(solution)/shard_map/ppermute | solution.py:460
  95.1 4.3 %copy-start.9 = (bf16[2,8,2,96,128]{4,3,2,1,0:T(8,128)(2,1)}, bf16[2,8,2,96,128]{4,3,2,1,0:T(8,128)(2,1)S(1)}, u32[]{:S(2)}) copy-start(bf16[2,8,2,96,128]{4,3,2,1,0:T(8,128)(2,1)S(1)} %collective-permute-done.10.rest_0_) | copy-start | bytes 2359300
  95.1 14.3 %collective-permute-start.13 = (bf16[8,2,96,128]{3,2,1,0:T(8,128)(2,1)}, bf16[8,2,96,128]{3,2,1,0:T(8,128)(2,1)S(1)}, u32[]{:S(2)}, u32[]{:S(2)}) collective-permute-start(bf16[8,2,96,128]{3,2,1,0:T(8,128)(2,1)} %get-tuple-element.56), channel_id=1, source_target_pairs={{4,2},{5,3},{6,4},{7,5},{8,6},{9,7},{10,8},{11,9},{12,10},{13,11},... | collective-permute-start | bytes 1179656 | tf_op jit(solution)/shard_map/ppermute | solution.py:461
  98.1 17.2 %collective-permute-start.11 = (bf16[8,2,96,128]{3,2,1,0:T(8,128)(2,1)}, bf16[8,2,96,128]{3,2,1,0:T(8,128)(2,1)S(1)}, u32[]{:S(2)}, u32[]{:S(2)}) collective-permute-start(bf16[8,2,96,128]{3,2,1,0:T(8,128)(2,1)} %get-tuple-element.51), channel_id=1, source_target_pairs={{4,3},{5,2},{6,5},{7,4},{8,7},{9,6},{10,9},{11,8},{12,11},{13,10},... | collective-permute-start | bytes 1179656 | tf_op jit(solution)/shard_map/ppermute | solution.py:462
  109.4 0.8 copy-start.14
  109.4 0.9 copy-start.12
  112.5 2.8 %copy-start.10 = (bf16[8,3,96,128]{3,2,1,0:T(8,128)(2,1)}, bf16[8,3,96,128]{3,2,1,0:T(8,128)(2,1)S(1)}, u32[]{:S(2)}) copy-start(bf16[8,3,96,128]{3,2,1,0:T(8,128)(2,1)S(1)} %collective-permute-done.6.kept_ref) | copy-start | bytes 1769476
  115.3 0.7 copy-start.13
  115.3 1.0 copy-start.11

commit v4 on v3

--- a/solution.py
+++ b/solution.py
@@ -30,18 +30,18 @@
     return lax.dot_general(a, b, (((1,), (0,)), ((), ())), preferred_element_type=jnp.float32)
 
 
-def pack_kernel(first_ref, parity_ref, start_ref, k_ref, v_ref, q_ref, *rest, begin, rows):
+def pack_kernel(first_ref, parity_ref, start_ref, k_ref, v_ref, q_ref, *rest, begin, rows, whole, pairs):
     outs, sems = rest[:-1], rest[-1]
     half = start_ref.shape[1]
     parity = parity_ref[0]
     pieces = []
     for n, ref in enumerate((k_ref, v_ref, q_ref)):
         into = pl.ds(n * rows, rows)
-        for core in range(2):
-            source = ref.at[core, pl.ds(begin, rows)]
-            pieces.append((source, outs[0].at[core, into]))
-        for turn, out in enumerate(outs[1:]):
-            if n < 2 or turn < 2:
+        if whole:
+            for core in range(2):
+                pieces.append((ref.at[core, pl.ds(begin, rows)], outs[0].at[core, into]))
+        else:
+            for turn, out in enumerate(outs if n < 2 else outs[:2]):
                 source = ref.at[lax.rem(parity + turn, 2), pl.ds(begin, rows)]
                 pieces.append((source, out.at[0, into]))
     copies = [
@@ -54,28 +54,28 @@
     row = lax.broadcasted_iota(jnp.int32, (MARK_ROWS, half), 0)
     marks = jnp.where(row == 0, into // 2, jnp.where(row == 1, into % 2, 0))
     marks = marks.astype(jnp.float32).astype(jnp.bfloat16)
-    for out in outs[:3]:
+    for out in outs[: 1 if whole else 2]:
         for lead in range(out.shape[0]):
             out[lead, pl.ds(3 * rows, MARK_ROWS), :] = marks
     for copy in copies:
         copy.wait()
 
 
-def pack(first, parity, starts, keys, values, queries, begin, chunk, direct):
+def pack(first, parity, starts, keys, values, queries, begin, chunk, whole, pairs):
     _, _, depth, half = keys.shape
     rows = chunk * depth
     flat = [x.reshape(2, -1, half) for x in (keys, values, queries)]
-    whole, pair = 3 * rows + MARK_ROWS, 2 * rows
-    out = [(2, whole, half), (1, whole, half), (1, whole, half), (1, pair, half), (1, pair, half)]
-    out = [jax.ShapeDtypeStruct(shape, jnp.bfloat16) for shape in (out if direct else out[:1])]
+    full = 3 * rows + MARK_ROWS
+    shapes = [(2, full, half)] if whole else [(1, full, half)] * 2
+    shapes += [(1, 2 * rows, half)] * (2 * pairs)
     smem = pl.BlockSpec(memory_space=pltpu.SMEM)
     vmem = pl.BlockSpec(memory_space=pltpu.VMEM)
     return pl.pallas_call(
-        functools.partial(pack_kernel, begin=begin * depth, rows=rows),
+        functools.partial(pack_kernel, begin=begin * depth, rows=rows, whole=whole, pairs=pairs),
         in_specs=[smem, smem, vmem] + [pl.BlockSpec(memory_space=pltpu.HBM)] * 3,
-        out_specs=[vmem] * len(out),
-        out_shape=out,
-        scratch_shapes=[pltpu.SemaphoreType.DMA((16,))],
+        out_specs=[vmem] * len(shapes),
+        out_shape=[jax.ShapeDtypeStruct(shape, jnp.bfloat16) for shape in shapes],
+        scratch_shapes=[pltpu.SemaphoreType.DMA((10,))],
         compiler_params=pltpu.CompilerParams(vmem_limit_bytes=PACK_VMEM),
         name="pack",
     )(first, parity, starts, *flat)
@@ -84,10 +84,9 @@
 def attention_kernel(
     edge_ref, turned_ref, out_turn_ref, *refs, score_scale, parted
 ):
-    next_marks, own_marks = refs[:2], refs[2]
-    next_refs = (refs[3:6], refs[6:9])
-    own_refs, prior_refs = refs[9:12], (refs[12:14], refs[14:16])
-    results = refs[16:]
+    next_marks, own_marks = refs[:2], refs[2:4]
+    next_refs, own_refs = (refs[4:7], refs[7:10]), (refs[10:13], refs[13:16])
+    prior_refs, results = (refs[16:18], refs[18:20]), refs[20:]
     if parted:
         to_next, kept, to_prior = results[:2], results[2:4], results[4:]
     else:
@@ -97,31 +96,25 @@
     prior, own, following = range(3)
     outs = (to_prior, kept, to_next)
     turned = turned_ref[0]
-    turns = (turned, 0, turned)
     out_turn = out_turn_ref[0]
 
-    def positions(b, axis):
+    def positions(axis):
         shape = (1, span) if axis == 1 else (span, span)
-        return lax.broadcasted_iota(jnp.int32, shape, axis) ^ (turns[b] * half)
+        return lax.broadcasted_iota(jnp.int32, shape, axis) ^ (turned * half)
 
     def first_visible(b, before):
-        first, second = next_marks if b == following else (own_marks.at[0], own_marks.at[1])
-        first, second = (first[0], second[0]) if b == following else (first[...], second[...])
-        marks = jnp.concatenate([first, second], axis=1).astype(jnp.float32)
+        first, second = next_marks if b == following else own_marks
+        marks = jnp.concatenate([first[0], second[0]], axis=1).astype(jnp.float32)
         into = (marks[0:1] * 2 + marks[1:2]).astype(jnp.int32)
-        return before * span + positions(b, 1) - into
+        return before * span + positions(1) - into
 
     def load(b, h, n):
         rows = pl.ds(h * depth, depth)
-        if b == own:
-            first, second = own_refs[n][0, rows, :], own_refs[n][1, rows, :]
-        else:
-            first, second = (prior_refs, None, next_refs)[b]
-            first, second = first[n][0, rows, :], second[n][0, rows, :]
-        return jnp.concatenate([first, second], axis=1)
-
-    def put(b, pair, index, value, add):
-        straight = (turns[b] ^ out_turn) == 0
+        first, second = (prior_refs, own_refs, next_refs)[b]
+        return jnp.concatenate([first[n][0, rows, :], second[n][0, rows, :]], axis=1)
+
+    def put(pair, index, value, add):
+        straight = (turned ^ out_turn) == 0
         first, second = value[:, :half], value[:, half:]
         parts = (jnp.where(straight, first, second), jnp.where(straight, second, first))
         for ref, part in zip(pair, parts):
@@ -133,10 +126,10 @@
         diagonal = len(blocks) - 1
         hidden = []
         for at in range(len(blocks)):
-            key_pos = positions(blocks[at], 0) + at * span
+            key_pos = positions(0) + at * span
             visible = key_pos >= lo
             if at == diagonal:
-                visible = visible & (key_pos <= positions(blocks[at], 1) + at * span)
+                visible = visible & (key_pos <= positions(1) + at * span)
             hidden.append(jnp.where(visible, 0.0, HIDDEN))
         ones = jnp.ones((MARK_ROWS, span), jnp.bfloat16)
         for begin in range(0, heads, GROUP):
@@ -187,9 +180,9 @@
             grad_keys = {h: [dot_nt(q[h], grad) for grad in grad_scores[h]] for h in group}
             for h in group:
                 for at, b in enumerate(blocks):
-                    put(b, outs[b], (h, 1), grad_values[h][at], b == add)
-                    put(b, outs[b], (h, 0), grad_keys[h][at] * score_scale, b == add)
-                put(blocks[-1], rows_out, (h, 2), dq[h] * score_scale, False)
+                    put(outs[b], (h, 1), grad_values[h][at], b == add)
+                    put(outs[b], (h, 0), grad_keys[h][at] * score_scale, b == add)
+                put(rows_out, (h, 2), dq[h] * score_scale, False)
 
     def clear(pair, kinds):
         for ref in pair:
@@ -239,7 +232,9 @@
 
 
 def attention(edge, turned, out_turn, following, own, prior, score_scale, depth, parted):
-    _, rows, half = own.shape
+    (first, first_row), (second, second_row) = following
+    (own0, own0_row), (own1, own1_row) = own
+    _, rows, half = own0.shape
     chunk = rows // 3 // depth
     steps = chunk // PER_STEP
     block = PER_STEP * depth
@@ -254,19 +249,19 @@
             return [jax.ShapeDtypeStruct((chunk, kinds, depth, half), jnp.bfloat16)] * 2
         return [jax.ShapeDtypeStruct((2, chunk, kinds, depth, half), jnp.bfloat16)]
 
-    def side(lead, n, cores=1):
-        return pl.BlockSpec((cores, block, half), lambda g, e, t, o: (lead, n * steps + g, 0))
-
-    def marks(lead, cores=1):
+    def side(lead, n):
+        return pl.BlockSpec((1, block, half), lambda g, e, t, o: (lead, n * steps + g, 0))
+
+    def marks(lead):
         return pl.BlockSpec(
-            (cores, MARK_ROWS, half), lambda g, e, t, o: (lead, 3 * chunk * depth // MARK_ROWS, 0)
+            (1, MARK_ROWS, half), lambda g, e, t, o: (lead, 3 * chunk * depth // MARK_ROWS, 0)
         )
 
-    (first, first_row), (second, second_row) = following
     (prior0, prior0_row), (prior1, prior1_row) = prior
-    specs = [marks(first_row), marks(second_row), marks(0, 2)]
-    specs += [side(first_row, n) for n in range(3)] + [side(second_row, n) for n in range(3)]
-    specs += [side(0, n, 2) for n in range(3)]
+    own_and_next = (first_row, second_row, own0_row, own1_row)
+    specs = [marks(row) for row in own_and_next]
+    for row in own_and_next:
+        specs += [side(row, n) for n in range(3)]
     for row in (prior0_row, prior1_row):
         specs += [side(row, n) for n in range(2)]
     pairs = chunk * (2 * half) * (6 * half)
@@ -285,8 +280,8 @@
         ),
         name="attention",
     )(
-        edge, turned, out_turn, first, second, own, *[first] * 3, *[second] * 3, *[own] * 3,
-        *[prior0] * 2, *[prior1] * 2,
+        edge, turned, out_turn, first, second, own0, own1, *[first] * 3, *[second] * 3,
+        *[own0] * 3, *[own1] * 3, *[prior0] * 2, *[prior1] * 2,
     )
 
 
@@ -423,25 +418,30 @@
     parity = (lax.axis_index("head") % 2).astype(jnp.int32).reshape(1)
     edge = (lax.axis_index("head") < 2).astype(jnp.int32).reshape(1)
 
-    def packed(c):
-        return pack(first, parity, starts, keys, values, queries, begins[c], CHUNKS[c], c == 0)
+    def packed(c, whole, pairs, *earlier):
+        marked = after(starts, *earlier) if earlier else starts
+        return pack(
+            first, parity, marked, keys, values, queries, begins[c], CHUNKS[c], whole, pairs
+        )
 
     own, following, prior, to_next, kept, to_prior, back_next, back_prior, done = (
         [None, None] for _ in range(9)
     )
     crossed_down = [(t, s ^ 1) for s, t in column_up]
-    by_halves, same, crossed, same_pair, crossed_pair = packed(0)
+    same, crossed, same_pair, crossed_pair = packed(0, 0, 1)
+    swapped = lax.ppermute(crossed, "head", [(s, s ^ 1) for s in range(head_count)])
+    own[0] = ((same, 0), (swapped, 0))
     same = lax.ppermute(same, flat, column_down)
     crossed = lax.ppermute(crossed, flat, crossed_down)
     following[0] = ((same, 0), (crossed, 0))
     same_pair = lax.ppermute(same_pair, flat, inner_up + across)
     crossed_pair = lax.ppermute(crossed_pair, flat, [(s, t ^ 1) for s, t in inner_up + across])
     prior[0] = ((same_pair, 0), (crossed_pair, 0))
-    own[1] = cores(packed(1)[0])
-    own[0] = cores(after(by_halves, own[1]))
-    gone = lax.ppermute(after(own[1][:, : 2 * CHUNKS[1] * depth], same), flat, inner_up + across)
+    whole = cores(packed(1, 1, 0)[0])
+    own[1] = ((whole, 0), (whole, 1))
+    gone = lax.ppermute(after(whole[:, : 2 * CHUNKS[1] * depth], same), flat, inner_up + across)
     prior[1] = ((gone, 0), (gone, 1))
-    came = lax.ppermute(after(own[1], same, crossed, own[0], same_pair, crossed_pair), flat, column_down)
+    came = lax.ppermute(after(whole, same, crossed, same_pair, crossed_pair), flat, column_down)
     following[1] = ((came, 0), (came, 1))
 
     nothing = jnp.zeros_like(parity)
@@ -456,7 +456,7 @@
     )
     crossed_column = [(s, t ^ 1) for s, t in column_up]
     down = inner_down + across_down
-    next_same = lax.ppermute(after(next_same, back_next[0]), flat, column_up)
+    next_same = lax.ppermute(next_same, flat, column_up)
     next_crossed = lax.ppermute(after(next_crossed, back_next[0]), flat, crossed_column)
     prior_same = lax.ppermute(after(prior_same, back_prior[0]), flat, down)
     prior_crossed = lax.ppermute(

time: 120 us -> 119 us (level)
  blocking collectives: 19.3 us -> 11.3 us
  waiting for transfers between devices: 32.4 us -> 37.9 us
  starting transfers between devices: 26.4 us -> 28.9 us
    all_to_all x3 -> x2, blocking collectives: 19.3 us -> 11.3 us  [cores(): lax.all_to_all(value, 'head', split_axis=0, concat_axis=0, tiled=True, ax...]
    ppermute x1, waiting for transfers between devices: 3.9 us -> 10.8 us  [shards(): same_pair = lax.ppermute(same_pair, flat, inner_up + across)]
    ppermute x1, starting transfers between devices: 2.97 us -> 5.65 us  [shards(): prior_same = lax.ppermute(after(prior_same, back_prior[0]), flat, down)]
    ppermute x1, waiting for transfers between devices: 1.35 us -> 0.01 us  [shards(): same = lax.ppermute(same, flat, column_down)]
    ppermute x3 -> x4, starting transfers between devices: 5.69 us -> 6.47 us  [the longest x1 2.59 us: shards(): lax.ppermute(crossed, 'head', [(s, s ^ 1) for s in range(head_count)])]
    unnamed x30 -> x28, local copies, waits for them, and re-layouts: 2.88 us -> 2.88 us
  transfers between devices with their start and end apart: 14 -> 15, of which waited for: 6 -> 5; matrix products, arithmetic and copies ran while one was open for 1% -> 1% of each run, Pallas kernels for 25% -> 25%
where the time goes in v4:
time: 119 us; the launch traced here: 118 us
  waiting for transfers between devices  37.9 us (32%)
  Pallas kernels  34.7 us (29%)
  starting transfers between devices  28.9 us (24%)
  blocking collectives  11.3 us (9%)
  local copies, waits for them, and re-layouts  3.86 us (3%)
    pallas_call x2, Pallas kernels, attention(): pl.pallas_call(functools.partial(attention_kernel, score_scale=score_scal...  19.6 us
    ppermute x1, waiting for transfers between devices, shards(): far_end = lax.ppermute(to_prior[0], flat, across_down)  15.5 us
    all_to_all x2, blocking collectives, cores(): lax.all_to_all(value, 'head', split_axis=0, concat_axis=0, tiled=True, ax...  11.3 us
    ppermute x1, waiting for transfers between devices, shards(): same_pair = lax.ppermute(same_pair, flat, inner_up + across)  10.8 us
    ppermute x1, waiting for transfers between devices, shards(): lax.ppermute(crossed_pair, flat, [(s, t ^ 1) for s, t in inner_up + across])  8.19 us
    pallas_call x2, Pallas kernels, pack(): pl.pallas_call(functools.partial(pack_kernel, begin=begin * depth, rows=r...  6.71 us
    ppermute x1, starting transfers between devices, shards(): prior_same = lax.ppermute(after(prior_same, back_prior[0]), flat, down)  5.65 us
    ppermute x1, starting transfers between devices, shards(): far_end = lax.ppermute(to_prior[0], flat, across_down)  4.33 us
  transfers between devices with their start and end apart: 15, of which 5 were waited for; matrix products, arithmetic and copies ran while one was open for 1% of the time, Pallas kernels for 25%

profile of v4, /device:TPU:25, one launch (start us, length us, event | category | flops | bytes accessed | tf_op | source)
XLA Modules:
  0.0 117.6 jit_solution(11814231861340364260)
XLA Ops:
  0.6 3.6 %pack.3 = (bf16[1,2320,128]{2,1,0:T(8,128)(2,1)}, bf16[1,2320,128]{2,1,0:T(8,128)(2,1)}, bf16[1,1536,128]{2,1,0:T(8,128)(2,1)}, bf16[1,1536,128]{2,1,0:T(8,128)(2,1)}) custom-call(s32[1]{0:T(128)} %bitcast.2.first_ref, s32[1]{0:T(128)} %bitcast.parity_ref.out_turn_ref.turned_ref.head_half_ref, s32[1,128]{1,0:T(1,128)} %bitcast.19, ...), custom_call_target="tpu_custom_call" | custom-call | tf_op jit(solution)/shard_map/pack/pallas_call | solution.py:73
  4.2 1.3 %collective-permute-start = (bf16[1,2320,128]{2,1,0:T(8,128)(2,1)}, bf16[1,2320,128]{2,1,0:T(8,128)(2,1)S(1)}, u32[]{:S(2)}, u32[]{:S(2)}) collective-permute-start(bf16[1,2320,128]{2,1,0:T(8,128)(2,1)} %get-tuple-element.32.refs_2_.refs_10_.refs_11_.refs_12_), channel_id=1, source_target_pairs={{2,0},{3,1},{4,2},{5,3},{6,4},{7,5},{8,6},{9,7},{10,8},{11,9},{12,... | collective-permute-start | bytes 1781768 | tf_op jit(solution)/shard_map/ppermute | solution.py:434
  5.5 1.3 %collective-permute-start.1 = (bf16[1,2320,128]{2,1,0:T(8,128)(2,1)}, bf16[1,2320,128]{2,1,0:T(8,128)(2,1)}, u32[]{:S(2)}, u32[]{:S(2)}) collective-permute-start(bf16[1,2320,128]{2,1,0:T(8,128)(2,1)} %get-tuple-element.33), channel_id=1, source_target_pairs={{2,1},{3,0},{4,3},{5,2},{6,5},{7,4},{8,7},{9,6},{10,9},{11,8},{12,... | collective-permute-start | bytes 1781768 | tf_op jit(solution)/shard_map/ppermute | solution.py:435
  6.8 1.3 %collective-permute-start.2 = (bf16[1,1536,128]{2,1,0:T(8,128)(2,1)}, bf16[1,1536,128]{2,1,0:T(8,128)(2,1)S(1)}, u32[]{:S(2)}, u32[]{:S(2)}) collective-permute-start(bf16[1,1536,128]{2,1,0:T(8,128)(2,1)} %get-tuple-element.34), channel_id=1, source_target_pairs={{2,4},{3,5},{4,6},{5,7},{6,8},{7,9},{8,10},{9,11},{10,12},{11,13},... | collective-permute-start | bytes 1179656 | tf_op jit(solution)/shard_map/ppermute | solution.py:437
  8.1 1.3 %collective-permute-start.3 = (bf16[1,1536,128]{2,1,0:T(8,128)(2,1)}, bf16[1,1536,128]{2,1,0:T(8,128)(2,1)S(1)}, u32[]{:S(2)}, u32[]{:S(2)}) collective-permute-start(bf16[1,1536,128]{2,1,0:T(8,128)(2,1)} %get-tuple-element.35), channel_id=1, source_target_pairs={{2,5},{3,4},{4,7},{5,6},{6,9},{7,8},{8,11},{9,10},{10,13},{11,12},... | collective-permute-start | bytes 1179656 | tf_op jit(solution)/shard_map/ppermute | solution.py:438
  9.4 2.6 %collective-permute-start.7 = (bf16[1,2320,128]{2,1,0:T(8,128)(2,1)}, bf16[1,2320,128]{2,1,0:T(8,128)(2,1)}, u32[]{:S(2)}, u32[]{:S(2)}) collective-permute-start(bf16[1,2320,128]{2,1,0:T(8,128)(2,1)} %get-tuple-element.33), channel_id=1, source_target_pairs={{0,1},{1,0},{2,3},{3,2},{4,5},{5,4},{6,7},{7,6},{8,9},{9,8},{10,11... | collective-permute-start | bytes 1781768 | tf_op jit(solution)/shard_map/ppermute | solution.py:432
  12.0 3.1 %pack.2 = bf16[2,2320,128]{2,1,0:T(8,128)(2,1)} custom-call(s32[1]{0:T(128)} %bitcast.2.first_ref, s32[1]{0:T(128)} %bitcast.parity_ref.out_turn_ref.turned_ref.head_half_ref, s32[1,128]{1,0:T(1,128)} %bitcast.20, bf16[2,1536,128]{2,1,0:T(8,128)(2,1)} %bitcast.11, bf16[2,1536,128]{2,1,0:T(8,128)(2,1)} %bitcast.13, bf16[2,1536,128]{2,1,0:T(8,128)(2,1)} %bitcast.15), custom_call_target="tpu_custom_call" | custom-call | tf_op jit(solution)/shard_map/pack/pallas_call | solution.py:73
  15.2 5.5 %all_to_all.10.refs_2_.refs_3_.refs_10_.refs_11_.refs_12_.refs_13_.refs_14_.refs_15_ = bf16[2,2320,128]{2,1,0:T(8,128)(2,1)S(1)} all-to-all(bf16[2,2320,128]{2,1,0:T(8,128)(2,1)} %pack.2), channel_id=1, replica_groups={{0,1},{2,3},{4,5},{6,7},{8,9},{10,11},{12,13},{14,15},{16,17},{18,19},{..., dimensions={0} | all-to-all | bytes 2375680 | tf_op jit(solution)/shard_map/all_to_all | solution.py:388
  20.6 1.0 slice.4
  21.6 1.3 %collective-permute-start.5 = (bf16[2,1536,128]{2,1,0:T(8,128)(2,1)}, bf16[2,1536,128]{2,1,0:T(8,128)(2,1)S(1)}, u32[]{:S(2)}, u32[]{:S(2)}) collective-permute-start(bf16[2,1536,128]{2,1,0:T(8,128)(2,1)} %slice.4), channel_id=1, source_target_pairs={{2,4},{3,5},{4,6},{5,7},{6,8},{7,9},{8,10},{9,11},{10,12},{11,13},... | collective-permute-start | bytes 2359304 | tf_op jit(solution)/shard_map/ppermute | solution.py:442
  22.9 10.8 %collective-permute-done.2.refs_16_.refs_17_ = bf16[1,1536,128]{2,1,0:T(8,128)(2,1)S(1)} collective-permute-done((bf16[1,1536,128]{2,1,0:T(8,128)(2,1)}, bf16[1,1536,128]{2,1,0:T(8,128)(2,1)S(1)}, u32[]{:S(2)}, u32[]{:S(2)}) %collective-permute-start.2) | collective-permute-done | bytes 393248 | tf_op jit(solution)/shard_map/ppermute | solution.py:437
  33.7 8.2 %collective-permute-done.3.refs_18_.refs_19_ = bf16[1,1536,128]{2,1,0:T(8,128)(2,1)S(1)} collective-permute-done((bf16[1,1536,128]{2,1,0:T(8,128)(2,1)}, bf16[1,1536,128]{2,1,0:T(8,128)(2,1)S(1)}, u32[]{:S(2)}, u32[]{:S(2)}) %collective-permute-start.3) | collective-permute-done | bytes 393248 | tf_op jit(solution)/shard_map/ppermute | solution.py:438
  41.9 0.7 copy-done.5
  42.6 1.3 %collective-permute-start.4 = (bf16[2,2320,128]{2,1,0:T(8,128)(2,1)S(1)}, bf16[2,2320,128]{2,1,0:T(8,128)(2,1)S(1)}, u32[]{:S(2)}, u32[]{:S(2)}) collective-permute-start(bf16[2,2320,128]{2,1,0:T(8,128)(2,1)S(1)} %all_to_all.10.refs_2_.refs_3_.refs_10_.refs_11_.refs_12_.refs_13_.refs_14_.refs_15_), channel_id=1, source_target_pairs={{2,0},{3,1},{4,2},{5,3},{6,4},{7,5},{8,6},{9,7},{10,8},{11,9},{12,... | collective-permute-start | bytes 3563528 | tf_op jit(solution)/shard_map/ppermute | solution.py:444
  43.9 9.8 %attention.3 = (bf16[2,8,3,96,128]{4,3,2,1,0:T(8,128)(2,1)}, bf16[2,8,3,96,128]{4,3,2,1,0:T(8,128)(2,1)}, bf16[2,8,2,96,128]{4,3,2,1,0:T(8,128)(2,1)}) custom-call(s32[1]{0:T(128)} %bitcast.1.edge_ref, s32[1]{0:T(128)} %bitcast.parity_ref.out_turn_ref.turned_ref.head_half_ref, s32[1]{0:T(128)} %constant.25.clone.1.turned_ref.out_turn_ref, ...), custom_call_target="tpu_custom_call" | custom-call | flops 1811939328 | bytes 3932160 | tf_op jit(solution)/shard_map/attention/pallas_call | solution.py:268
  53.7 4.3 %collective-permute-start.10 = (bf16[2,8,2,96,128]{4,3,2,1,0:T(8,128)(2,1)}, bf16[2,8,2,96,128]{4,3,2,1,0:T(8,128)(2,1)S(1)}, u32[]{:S(2)}, u32[]{:S(2)}) collective-permute-start(bf16[2,8,2,96,128]{4,3,2,1,0:T(8,128)(2,1)} %get-tuple-element.45), channel_id=1, source_target_pairs={{32,30},{33,31},{64,62},{65,63},{96,94},{97,95},{128,126},{129,127... | collective-permute-start | bytes 2359304 | tf_op jit(solution)/shard_map/ppermute | solution.py:451
  58.7 1.4 %collective-permute-start.8 = (bf16[2,8,3,96,128]{4,3,2,1,0:T(8,128)(2,1)}, bf16[2,8,3,96,128]{4,3,2,1,0:T(8,128)(2,1)S(1)}, u32[]{:S(2)}, u32[]{:S(2)}) collective-permute-start(bf16[2,8,3,96,128]{4,3,2,1,0:T(8,128)(2,1)} %get-tuple-element.41), channel_id=1, source_target_pairs={{0,2},{1,3},{2,4},{3,5},{4,6},{5,7},{6,8},{7,9},{8,10},{9,11},{10,... | collective-permute-start | bytes 3538952 | tf_op jit(solution)/shard_map/ppermute | solution.py:452
  60.1 15.5 %collective-permute-done.10.rest_1_ = bf16[2,8,2,96,128]{4,3,2,1,0:T(8,128)(2,1)S(1)} collective-permute-done((bf16[2,8,2,96,128]{4,3,2,1,0:T(8,128)(2,1)}, bf16[2,8,2,96,128]{4,3,2,1,0:T(8,128)(2,1)S(1)}, u32[]{:S(2)}, u32[]{:S(2)}) %collective-permute-start.10) | collective-permute-done | bytes 786464 | tf_op jit(solution)/shard_map/ppermute | solution.py:451
  75.6 0.9 collective-permute-start.11
  76.7 9.8 %attention.2 = (bf16[8,3,96,128]{3,2,1,0:T(8,128)(2,1)}, bf16[8,3,96,128]{3,2,1,0:T(8,128)(2,1)}, bf16[8,3,96,128]{3,2,1,0:T(8,128)(2,1)}, bf16[8,3,96,128]{3,2,...) custom-call(s32[1]{0:T(128)} %bitcast.1.edge_ref, ...), custom_call_target="tpu_custom_call" | custom-call | flops 1811939328 | bytes 3932160 | tf_op jit(solution)/shard_map/attention/pallas_call | solution.py:268
  86.5 1.3 %collective-permute-start.13 = (bf16[8,3,96,128]{3,2,1,0:T(8,128)(2,1)}, bf16[8,3,96,128]{3,2,1,0:T(8,128)(2,1)S(1)}, u32[]{:S(2)}, u32[]{:S(2)}) collective-permute-start(bf16[8,3,96,128]{3,2,1,0:T(8,128)(2,1)} %get-tuple-element.48), channel_id=1, source_target_pairs={{0,2},{1,3},{2,4},{3,5},{4,6},{5,7},{6,8},{7,9},{8,10},{9,11},{10,... | collective-permute-start | bytes 1769480 | tf_op jit(solution)/shard_map/ppermute | solution.py:459
  87.8 2.4 %collective-permute-start.6 = (bf16[8,3,96,128]{3,2,1,0:T(8,128)(2,1)}, bf16[8,3,96,128]{3,2,1,0:T(8,128)(2,1)S(1)}, u32[]{:S(2)}, u32[]{:S(2)}) collective-permute-start(bf16[8,3,96,128]{3,2,1,0:T(8,128)(2,1)} %get-tuple-element.38), channel_id=1, source_target_pairs={{0,1},{1,0},{2,3},{3,2},{4,5},{5,4},{6,7},{7,6},{8,9},{9,8},{10,11... | collective-permute-start | bytes 1769480 | tf_op jit(solution)/shard_map/ppermute | solution.py:465
  90.2 1.3 %collective-permute-start.9 = (bf16[8,3,96,128]{3,2,1,0:T(8,128)(2,1)}, bf16[8,3,96,128]{3,2,1,0:T(8,128)(2,1)S(1)}, u32[]{:S(2)}, u32[]{:S(2)}) collective-permute-start(bf16[8,3,96,128]{3,2,1,0:T(8,128)(2,1)} %get-tuple-element.42), channel_id=1, source_target_pairs={{0,3},{1,2},{2,5},{3,4},{4,7},{5,6},{6,9},{7,8},{8,11},{9,10},{10,... | collective-permute-start | bytes 1769480 | tf_op jit(solution)/shard_map/ppermute | solution.py:460
  91.6 5.6 %collective-permute-start.14 = (bf16[8,2,96,128]{3,2,1,0:T(8,128)(2,1)}, bf16[8,2,96,128]{3,2,1,0:T(8,128)(2,1)S(1)}, u32[]{:S(2)}, u32[]{:S(2)}) collective-permute-start(bf16[8,2,96,128]{3,2,1,0:T(8,128)(2,1)} %get-tuple-element.50), channel_id=1, source_target_pairs={{4,2},{5,3},{6,4},{7,5},{8,6},{9,7},{10,8},{11,9},{12,10},{13,11},... | collective-permute-start | bytes 1179656 | tf_op jit(solution)/shard_map/ppermute | solution.py:461
  97.2 1.3 %collective-permute-start.12 = (bf16[8,2,96,128]{3,2,1,0:T(8,128)(2,1)}, bf16[8,2,96,128]{3,2,1,0:T(8,128)(2,1)S(1)}, u32[]{:S(2)}, u32[]{:S(2)}) collective-permute-start(bf16[8,2,96,128]{3,2,1,0:T(8,128)(2,1)} %get-tuple-element.46), channel_id=1, source_target_pairs={{4,3},{5,2},{6,5},{7,4},{8,7},{9,6},{10,9},{11,8},{12,11},{13,10},... | collective-permute-start | bytes 1179656 | tf_op jit(solution)/shard_map/ppermute | solution.py:462
  98.6 3.2 %merge.1 = bf16[2,8,3,96,128]{4,3,2,1,0:T(8,128)(2,1)} custom-call(bf16[2,8,3,96,128]{4,3,2,1,0:T(8,128)(2,1)} %get-tuple-element.51.kept_ref, bf16[2,8,3,96,128]{4,3,2,1,0:T(8,128)(2,1)} %copy-done.6, bf16[2,8,2,96,128]{4,3,2,1,0:T(8,128)(2,1)} %copy-done.8, bf16[2,8,2,96,128]{4,3,2,1,0:T(8,128)(2,1)} %copy-done.7), custom_call_target="tpu_custom_call" | custom-call | tf_op jit(solution)/shard_map/merge/pallas_call | solution.py:304
  101.7 5.8 %all_to_all.11.early_ref = bf16[2,8,3,96,128]{4,3,2,1,0:T(8,128)(2,1)S(1)} all-to-all(bf16[2,8,3,96,128]{4,3,2,1,0:T(8,128)(2,1)} %merge.1), channel_id=1, replica_groups={{0,1},{2,3},{4,5},{6,7},{8,9},{10,11},{12,13},{14,15},{16,17},{18,19},{..., dimensions={0} | all-to-all | bytes 2359296 | tf_op jit(solution)/shard_map/all_to_all | solution.py:388
  107.5 1.0 place.1
  108.6 0.8 copy-done.11
  109.6 2.1 %finish.2 = (bf16[2,16,96,128]{3,2,1,0:T(8,128)(2,1)}, bf16[2,16,96,128]{3,2,1,0:T(8,128)(2,1)}, bf16[2,16,96,128]{3,2,1,0:T(8,128)(2,1)}) custom-call(s32[1]{0:T(128)} %bitcast.parity_ref.out_turn_ref.turned_ref.head_half_ref, bf16[8,3,96,128]{3,2,1,0:T(8,128)(2,1)} %get-tuple-element.47.kept_ref, ...), custom_call_target="tpu_custom_call", output_to_operand_aliasing={{0}: (4, {}), {1}: (5, {}), {2}: (6, {})} | custom-call | tf_op jit(solution)/shard_map/finish/pallas_call | solution.py:360
  111.7 2.8 %collective-permute-done.12.from_next_ref = bf16[8,2,96,128]{3,2,1,0:T(8,128)(2,1)S(1)} collective-permute-done((bf16[8,2,96,128]{3,2,1,0:T(8,128)(2,1)}, bf16[8,2,96,128]{3,2,1,0:T(8,128)(2,1)S(1)}, u32[]{:S(2)}, u32[]{:S(2)}) %collective-permute-start.12) | collective-permute-done | bytes 393248 | tf_op jit(solution)/shard_map/ppermute | solution.py:462
  115.5 2.1 %finish.3 = (bf16[2,16,96,128]{3,2,1,0:T(8,128)(2,1)}, bf16[2,16,96,128]{3,2,1,0:T(8,128)(2,1)}, bf16[2,16,96,128]{3,2,1,0:T(8,128)(2,1)}) custom-call(s32[1]{0:T(128)S(6)} %sub.3.head_half_ref, bf16[8,3,96,128]{3,2,1,0:T(8,128)(2,1)} %copy-done.9, bf16[8,3,96,128]{3,2,1,0:T(8,128)(2,1)} %copy-done.10, ...), custom_call_target="tpu_custom_call", output_to_operand_aliasing={{0}: (4, {}), {1}: (5, {}), {2}: (6, {})} | custom-call | tf_op jit(solution)/shard_map/finish/pallas_call | solution.py:360
  (37 shorter events, 2.0 us)
Async XLA Ops:
  4.2 17.4 %collective-permute-start = (bf16[1,2320,128]{2,1,0:T(8,128)(2,1)}, bf16[1,2320,128]{2,1,0:T(8,128)(2,1)S(1)}, u32[]{:S(2)}, u32[]{:S(2)}) collective-permute-start(bf16[1,2320,128]{2,1,0:T(8,128)(2,1)} %get-tuple-element.32.refs_2_.refs_10_.refs_11_.refs_12_), channel_id=1, source_target_pairs={{2,0},{3,1},{4,2},{5,3},{6,4},{7,5},{8,6},{9,7},{10,8},{11,9},{12,... | collective-permute-start | bytes 1781768 | tf_op jit(solution)/shard_map/ppermute | solution.py:434
  5.5 37.1 %collective-permute-start.1 = (bf16[1,2320,128]{2,1,0:T(8,128)(2,1)}, bf16[1,2320,128]{2,1,0:T(8,128)(2,1)}, u32[]{:S(2)}, u32[]{:S(2)}) collective-permute-start(bf16[1,2320,128]{2,1,0:T(8,128)(2,1)} %get-tuple-element.33), channel_id=1, source_target_pairs={{2,1},{3,0},{4,3},{5,2},{6,5},{7,4},{8,7},{9,6},{10,9},{11,8},{12,... | collective-permute-start | bytes 1781768 | tf_op jit(solution)/shard_map/ppermute | solution.py:435
  6.8 26.8 %collective-permute-start.2 = (bf16[1,1536,128]{2,1,0:T(8,128)(2,1)}, bf16[1,1536,128]{2,1,0:T(8,128)(2,1)S(1)}, u32[]{:S(2)}, u32[]{:S(2)}) collective-permute-start(bf16[1,1536,128]{2,1,0:T(8,128)(2,1)} %get-tuple-element.34), channel_id=1, source_target_pairs={{2,4},{3,5},{4,6},{5,7},{6,8},{7,9},{8,10},{9,11},{10,12},{11,13},... | collective-permute-start | bytes 1179656 | tf_op jit(solution)/shard_map/ppermute | solution.py:437
  8.1 33.7 %collective-permute-start.3 = (bf16[1,1536,128]{2,1,0:T(8,128)(2,1)}, bf16[1,1536,128]{2,1,0:T(8,128)(2,1)S(1)}, u32[]{:S(2)}, u32[]{:S(2)}) collective-permute-start(bf16[1,1536,128]{2,1,0:T(8,128)(2,1)} %get-tuple-element.35), channel_id=1, source_target_pairs={{2,5},{3,4},{4,7},{5,6},{6,9},{7,8},{8,11},{9,10},{10,13},{11,12},... | collective-permute-start | bytes 1179656 | tf_op jit(solution)/shard_map/ppermute | solution.py:438
  9.4 34.5 %collective-permute-start.7 = (bf16[1,2320,128]{2,1,0:T(8,128)(2,1)}, bf16[1,2320,128]{2,1,0:T(8,128)(2,1)}, u32[]{:S(2)}, u32[]{:S(2)}) collective-permute-start(bf16[1,2320,128]{2,1,0:T(8,128)(2,1)} %get-tuple-element.33), channel_id=1, source_target_pairs={{0,1},{1,0},{2,3},{3,2},{4,5},{5,4},{6,7},{7,6},{8,9},{9,8},{10,11... | collective-permute-start | bytes 1781768 | tf_op jit(solution)/shard_map/ppermute | solution.py:432
  20.6 33.1 %copy-start = (bf16[2,2320,128]{2,1,0:T(8,128)(2,1)}, bf16[2,2320,128]{2,1,0:T(8,128)(2,1)S(1)}, u32[]{:S(2)}) copy-start(bf16[2,2320,128]{2,1,0:T(8,128)(2,1)S(1)} %all_to_all.10.refs_2_.refs_3_.refs_10_.refs_11_.refs_12_.refs_13_.refs_14_.refs_15_) | copy-start | bytes 3563524
  21.6 20.2 %copy-start.3 = (bf16[1,2320,128]{2,1,0:T(8,128)(2,1)}, bf16[1,2320,128]{2,1,0:T(8,128)(2,1)S(1)}, u32[]{:S(2)}) copy-start(bf16[1,2320,128]{2,1,0:T(8,128)(2,1)S(1)} %collective-permute-done.refs_0_.refs_4_.refs_5_.refs_6_) | copy-start | bytes 1781764
  21.6 37.1 %collective-permute-start.5 = (bf16[2,1536,128]{2,1,0:T(8,128)(2,1)}, bf16[2,1536,128]{2,1,0:T(8,128)(2,1)S(1)}, u32[]{:S(2)}, u32[]{:S(2)}) collective-permute-start(bf16[2,1536,128]{2,1,0:T(8,128)(2,1)} %slice.4), channel_id=1, source_target_pairs={{2,4},{3,5},{4,6},{5,7},{6,8},{7,9},{8,10},{9,11},{10,12},{11,13},... | collective-permute-start | bytes 2359304 | tf_op jit(solution)/shard_map/ppermute | solution.py:442
  33.7 10.3 %copy-start.4 = (bf16[1,1536,128]{2,1,0:T(8,128)(2,1)}, bf16[1,1536,128]{2,1,0:T(8,128)(2,1)S(1)}, u32[]{:S(2)}) copy-start(bf16[1,1536,128]{2,1,0:T(8,128)(2,1)S(1)} %collective-permute-done.2.refs_16_.refs_17_) | copy-start | bytes 1179652
  41.9 0.7 copy-start.5
  42.6 33.0 %collective-permute-start.4 = (bf16[2,2320,128]{2,1,0:T(8,128)(2,1)S(1)}, bf16[2,2320,128]{2,1,0:T(8,128)(2,1)S(1)}, u32[]{:S(2)}, u32[]{:S(2)}) collective-permute-start(bf16[2,2320,128]{2,1,0:T(8,128)(2,1)S(1)} %all_to_all.10.refs_2_.refs_3_.refs_10_.refs_11_.refs_12_.refs_13_.refs_14_.refs_15_), channel_id=1, source_target_pairs={{2,0},{3,1},{4,2},{5,3},{6,4},{7,5},{8,6},{9,7},{10,8},{11,9},{12,... | collective-permute-start | bytes 3563528 | tf_op jit(solution)/shard_map/ppermute | solution.py:444
  53.7 21.9 %collective-permute-start.10 = (bf16[2,8,2,96,128]{4,3,2,1,0:T(8,128)(2,1)}, bf16[2,8,2,96,128]{4,3,2,1,0:T(8,128)(2,1)S(1)}, u32[]{:S(2)}, u32[]{:S(2)}) collective-permute-start(bf16[2,8,2,96,128]{4,3,2,1,0:T(8,128)(2,1)} %get-tuple-element.45), channel_id=1, source_target_pairs={{32,30},{33,31},{64,62},{65,63},{96,94},{97,95},{128,126},{129,127... | collective-permute-start | bytes 2359304 | tf_op jit(solution)/shard_map/ppermute | solution.py:451
  58.7 17.8 %copy-start.2 = (bf16[2,1536,128]{2,1,0:T(8,128)(2,1)}, bf16[2,1536,128]{2,1,0:T(8,128)(2,1)S(1)}, u32[]{:S(2)}) copy-start(bf16[2,1536,128]{2,1,0:T(8,128)(2,1)S(1)} %collective-permute-done.5.refs_16_.refs_17_.refs_18_.refs_19_) | copy-start | bytes 2359300
  58.7 31.5 %collective-permute-start.8 = (bf16[2,8,3,96,128]{4,3,2,1,0:T(8,128)(2,1)}, bf16[2,8,3,96,128]{4,3,2,1,0:T(8,128)(2,1)S(1)}, u32[]{:S(2)}, u32[]{:S(2)}) collective-permute-start(bf16[2,8,3,96,128]{4,3,2,1,0:T(8,128)(2,1)} %get-tuple-element.41), channel_id=1, source_target_pairs={{0,2},{1,3},{2,4},{3,5},{4,6},{5,7},{6,8},{7,9},{8,10},{9,11},{10,... | collective-permute-start | bytes 3538952 | tf_op jit(solution)/shard_map/ppermute | solution.py:452
  75.6 10.8 %copy-start.7 = (bf16[2,8,2,96,128]{4,3,2,1,0:T(8,128)(2,1)}, bf16[2,8,2,96,128]{4,3,2,1,0:T(8,128)(2,1)S(1)}, u32[]{:S(2)}) copy-start(bf16[2,8,2,96,128]{4,3,2,1,0:T(8,128)(2,1)S(1)} %collective-permute-done.10.rest_1_) | copy-start | bytes 2359300
  75.6 1.1 copy-start.1
  75.6 15.9 %collective-permute-start.11 = (bf16[2,8,2,96,128]{4,3,2,1,0:T(8,128)(2,1)}, bf16[2,8,2,96,128]{4,3,2,1,0:T(8,128)(2,1)S(1)}, u32[]{:S(2)}, u32[]{:S(2)}) collective-permute-start(bf16[2,8,2,96,128]{4,3,2,1,0:T(8,128)(2,1)} %get-tuple-element.45), channel_id=1, source_target_pairs={{4,2},{5,3},{6,4},{7,5},{8,6},{9,7},{10,8},{11,9},{12,10},{13,11},... | collective-permute-start | bytes 2359304 | tf_op jit(solution)/shard_map/ppermute | solution.py:453
  86.5 22.1 %collective-permute-start.13 = (bf16[8,3,96,128]{3,2,1,0:T(8,128)(2,1)}, bf16[8,3,96,128]{3,2,1,0:T(8,128)(2,1)S(1)}, u32[]{:S(2)}, u32[]{:S(2)}) collective-permute-start(bf16[8,3,96,128]{3,2,1,0:T(8,128)(2,1)} %get-tuple-element.48), channel_id=1, source_target_pairs={{0,2},{1,3},{2,4},{3,5},{4,6},{5,7},{6,8},{7,9},{8,10},{9,11},{10,... | collective-permute-start | bytes 1769480 | tf_op jit(solution)/shard_map/ppermute | solution.py:459
  87.8 23.9 %collective-permute-start.6 = (bf16[8,3,96,128]{3,2,1,0:T(8,128)(2,1)}, bf16[8,3,96,128]{3,2,1,0:T(8,128)(2,1)S(1)}, u32[]{:S(2)}, u32[]{:S(2)}) collective-permute-start(bf16[8,3,96,128]{3,2,1,0:T(8,128)(2,1)} %get-tuple-element.38), channel_id=1, source_target_pairs={{0,1},{1,0},{2,3},{3,2},{4,5},{5,4},{6,7},{7,6},{8,9},{9,8},{10,11... | collective-permute-start | bytes 1769480 | tf_op jit(solution)/shard_map/ppermute | solution.py:465
  90.2 8.3 %copy-start.6 = (bf16[2,8,3,96,128]{4,3,2,1,0:T(8,128)(2,1)}, bf16[2,8,3,96,128]{4,3,2,1,0:T(8,128)(2,1)S(1)}, u32[]{:S(2)}) copy-start(bf16[2,8,3,96,128]{4,3,2,1,0:T(8,128)(2,1)S(1)} %collective-permute-done.8.from_prior_ref) | copy-start | bytes 3538948
  90.2 24.2 %collective-permute-start.9 = (bf16[8,3,96,128]{3,2,1,0:T(8,128)(2,1)}, bf16[8,3,96,128]{3,2,1,0:T(8,128)(2,1)S(1)}, u32[]{:S(2)}, u32[]{:S(2)}) collective-permute-start(bf16[8,3,96,128]{3,2,1,0:T(8,128)(2,1)} %get-tuple-element.42), channel_id=1, source_target_pairs={{0,3},{1,2},{2,5},{3,4},{4,7},{5,6},{6,9},{7,8},{8,11},{9,10},{10,... | collective-permute-start | bytes 1769480 | tf_op jit(solution)/shard_map/ppermute | solution.py:460
  91.6 7.0 %copy-start.8 = (bf16[2,8,2,96,128]{4,3,2,1,0:T(8,128)(2,1)}, bf16[2,8,2,96,128]{4,3,2,1,0:T(8,128)(2,1)S(1)}, u32[]{:S(2)}) copy-start(bf16[2,8,2,96,128]{4,3,2,1,0:T(8,128)(2,1)S(1)} %collective-permute-done.11.rest_0_) | copy-start | bytes 2359300
  91.6 17.0 %collective-permute-start.14 = (bf16[8,2,96,128]{3,2,1,0:T(8,128)(2,1)}, bf16[8,2,96,128]{3,2,1,0:T(8,128)(2,1)S(1)}, u32[]{:S(2)}, u32[]{:S(2)}) collective-permute-start(bf16[8,2,96,128]{3,2,1,0:T(8,128)(2,1)} %get-tuple-element.50), channel_id=1, source_target_pairs={{4,2},{5,3},{6,4},{7,5},{8,6},{9,7},{10,8},{11,9},{12,10},{13,11},... | collective-permute-start | bytes 1179656 | tf_op jit(solution)/shard_map/ppermute | solution.py:461
  97.2 17.2 %collective-permute-start.12 = (bf16[8,2,96,128]{3,2,1,0:T(8,128)(2,1)}, bf16[8,2,96,128]{3,2,1,0:T(8,128)(2,1)S(1)}, u32[]{:S(2)}, u32[]{:S(2)}) collective-permute-start(bf16[8,2,96,128]{3,2,1,0:T(8,128)(2,1)} %get-tuple-element.46), channel_id=1, source_target_pairs={{4,3},{5,2},{6,5},{7,4},{8,7},{9,6},{10,9},{11,8},{12,11},{13,10},... | collective-permute-start | bytes 1179656 | tf_op jit(solution)/shard_map/ppermute | solution.py:462
  108.6 0.8 copy-start.11
  108.6 0.9 copy-start.13
  111.7 2.8 %copy-start.9 = (bf16[8,3,96,128]{3,2,1,0:T(8,128)(2,1)}, bf16[8,3,96,128]{3,2,1,0:T(8,128)(2,1)S(1)}, u32[]{:S(2)}) copy-start(bf16[8,3,96,128]{3,2,1,0:T(8,128)(2,1)S(1)} %collective-permute-done.6.kept_ref) | copy-start | bytes 1769476
  114.4 0.7 copy-start.12
  114.5 1.0 copy-start.10

commit v5 on v4

--- a/solution.py
+++ b/solution.py
@@ -450,14 +450,14 @@
     )
     far_end = lax.ppermute(to_prior[0], flat, across_down)
     back_next[0] = lax.ppermute(after(to_next[0], gone), flat, column_up)
-    back_prior[0] = lax.ppermute(after(to_prior[0], came, far_end), flat, inner_down)
+    back_prior[0] = lax.ppermute(after(to_prior[0], came), flat, inner_down)
     next_same, next_crossed, kept_same, kept_crossed, prior_same, prior_crossed = attention(
         edge, nothing, parity, following[1], own[1], prior[1], score_scale, depth, True
     )
     crossed_column = [(s, t ^ 1) for s, t in column_up]
     down = inner_down + across_down
     next_same = lax.ppermute(next_same, flat, column_up)
-    next_crossed = lax.ppermute(after(next_crossed, back_next[0]), flat, crossed_column)
+    next_crossed = lax.ppermute(after(next_crossed, back_next[0], far_end), flat, crossed_column)
     prior_same = lax.ppermute(after(prior_same, back_prior[0]), flat, down)
     prior_crossed = lax.ppermute(
         after(prior_crossed, back_prior[0]), flat, [(s, t ^ 1) for s, t in down]

time: 119 us -> 115 us (0.966)
  waiting for transfers between devices: 37.9 us -> 34.1 us
    ppermute x1, waiting for transfers between devices: 15.5 us -> 0.01 us  [shards(): far_end = lax.ppermute(to_prior[0], flat, across_down)]
    ppermute x1, waiting for transfers between devices: 0.01 us -> 9.62 us  [shards(): lax.ppermute(after(whole, same, crossed, same_pair, crossed_pair), flat,...]
    ppermute x1, waiting for transfers between devices: 0.62 us -> 4.96 us  [shards(): lax.ppermute(after(whole[:, :2 * CHUNKS[1] * depth], same), flat, inner_u...]
    ppermute x1, waiting for transfers between devices: 10.8 us -> 7.15 us  [shards(): same_pair = lax.ppermute(same_pair, flat, inner_up + across)]
    ppermute x1, starting transfers between devices: 5.65 us -> 2.07 us  [shards(): prior_same = lax.ppermute(after(prior_same, back_prior[0]), flat, down)]
    ppermute x1, starting transfers between devices: 4.33 us -> 1.52 us  [shards(): far_end = lax.ppermute(to_prior[0], flat, across_down)]
    ppermute x2, starting transfers between devices: 2.21 us -> 4.62 us  [the longest x1 3.74 us: shards(): lax.ppermute(after(next_crossed, back_next[0], far_end), flat, crossed_co...]
    ppermute x1, starting transfers between devices: 2.59 us -> 4.19 us  [shards(): lax.ppermute(crossed, 'head', [(s, s ^ 1) for s in range(head_count)])]
  transfers between devices with their start and end apart: 15 -> 15, of which waited for: 5 -> 7; matrix products, arithmetic and copies ran while one was open for 1% -> 1% of each run, Pallas kernels for 25% -> 25%
where the time goes in v5:
time: 115 us; the launch traced here: 114 us
  Pallas kernels  34.7 us (30%)
  waiting for transfers between devices  34.1 us (30%)
  starting transfers between devices  28.4 us (25%)
  blocking collectives  12 us (10%)
  local copies, waits for them, and re-layouts  3.68 us (3%)
    pallas_call x2, Pallas kernels, attention(): pl.pallas_call(functools.partial(attention_kernel, score_scale=score_scal...  19.6 us
    all_to_all x2, blocking collectives, cores(): lax.all_to_all(value, 'head', split_axis=0, concat_axis=0, tiled=True, ax...  12 us
    ppermute x1, waiting for transfers between devices, shards(): lax.ppermute(after(whole, same, crossed, same_pair, crossed_pair), flat,...  9.62 us
    ppermute x1, waiting for transfers between devices, shards(): lax.ppermute(crossed_pair, flat, [(s, t ^ 1) for s, t in inner_up + across])  8.19 us
    ppermute x1, waiting for transfers between devices, shards(): same_pair = lax.ppermute(same_pair, flat, inner_up + across)  7.15 us
    pallas_call x2, Pallas kernels, pack(): pl.pallas_call(functools.partial(pack_kernel, begin=begin * depth, rows=r...  6.71 us
    ppermute x1, waiting for transfers between devices, shards(): lax.ppermute(after(whole[:, :2 * CHUNKS[1] * depth], same), flat, inner_u...  4.96 us
    ppermute x1, starting transfers between devices, shards(): lax.ppermute(crossed, 'head', [(s, s ^ 1) for s in range(head_count)])  4.19 us
  transfers between devices with their start and end apart: 15, of which 7 were waited for; matrix products, arithmetic and copies ran while one was open for 1% of the time, Pallas kernels for 25%

profile of v5, /device:TPU:25, one launch (start us, length us, event | category | flops | bytes accessed | tf_op | source)
XLA Modules:
  0.0 113.8 jit_solution(16630940057783124569)
XLA Ops:
  0.6 3.6 %pack.3 = (bf16[1,2320,128]{2,1,0:T(8,128)(2,1)}, bf16[1,2320,128]{2,1,0:T(8,128)(2,1)}, bf16[1,1536,128]{2,1,0:T(8,128)(2,1)}, bf16[1,1536,128]{2,1,0:T(8,128)(2,1)}) custom-call(s32[1]{0:T(128)} %bitcast.2.first_ref, s32[1]{0:T(128)} %bitcast.parity_ref.out_turn_ref.turned_ref.head_half_ref, s32[1,128]{1,0:T(1,128)} %bitcast.19, ...), custom_call_target="tpu_custom_call" | custom-call | tf_op jit(solution)/shard_map/pack/pallas_call | solution.py:73
  4.2 1.3 %collective-permute-start = (bf16[1,2320,128]{2,1,0:T(8,128)(2,1)}, bf16[1,2320,128]{2,1,0:T(8,128)(2,1)S(1)}, u32[]{:S(2)}, u32[]{:S(2)}) collective-permute-start(bf16[1,2320,128]{2,1,0:T(8,128)(2,1)} %get-tuple-element.32.refs_2_.refs_10_.refs_11_.refs_12_), channel_id=1, source_target_pairs={{2,0},{3,1},{4,2},{5,3},{6,4},{7,5},{8,6},{9,7},{10,8},{11,9},{12,... | collective-permute-start | bytes 1781768 | tf_op jit(solution)/shard_map/ppermute | solution.py:434
  5.5 1.3 %collective-permute-start.1 = (bf16[1,2320,128]{2,1,0:T(8,128)(2,1)}, bf16[1,2320,128]{2,1,0:T(8,128)(2,1)}, u32[]{:S(2)}, u32[]{:S(2)}) collective-permute-start(bf16[1,2320,128]{2,1,0:T(8,128)(2,1)} %get-tuple-element.33), channel_id=1, source_target_pairs={{2,1},{3,0},{4,3},{5,2},{6,5},{7,4},{8,7},{9,6},{10,9},{11,8},{12,... | collective-permute-start | bytes 1781768 | tf_op jit(solution)/shard_map/ppermute | solution.py:435
  6.8 1.3 %collective-permute-start.2 = (bf16[1,1536,128]{2,1,0:T(8,128)(2,1)}, bf16[1,1536,128]{2,1,0:T(8,128)(2,1)S(1)}, u32[]{:S(2)}, u32[]{:S(2)}) collective-permute-start(bf16[1,1536,128]{2,1,0:T(8,128)(2,1)} %get-tuple-element.34), channel_id=1, source_target_pairs={{2,4},{3,5},{4,6},{5,7},{6,8},{7,9},{8,10},{9,11},{10,12},{11,13},... | collective-permute-start | bytes 1179656 | tf_op jit(solution)/shard_map/ppermute | solution.py:437
  8.1 1.3 %collective-permute-start.3 = (bf16[1,1536,128]{2,1,0:T(8,128)(2,1)}, bf16[1,1536,128]{2,1,0:T(8,128)(2,1)S(1)}, u32[]{:S(2)}, u32[]{:S(2)}) collective-permute-start(bf16[1,1536,128]{2,1,0:T(8,128)(2,1)} %get-tuple-element.35), channel_id=1, source_target_pairs={{2,5},{3,4},{4,7},{5,6},{6,9},{7,8},{8,11},{9,10},{10,13},{11,12},... | collective-permute-start | bytes 1179656 | tf_op jit(solution)/shard_map/ppermute | solution.py:438
  9.4 3.1 %pack.2 = bf16[2,2320,128]{2,1,0:T(8,128)(2,1)} custom-call(s32[1]{0:T(128)} %bitcast.2.first_ref, s32[1]{0:T(128)} %bitcast.parity_ref.out_turn_ref.turned_ref.head_half_ref, s32[1,128]{1,0:T(1,128)} %bitcast.20, bf16[2,1536,128]{2,1,0:T(8,128)(2,1)} %bitcast.11, bf16[2,1536,128]{2,1,0:T(8,128)(2,1)} %bitcast.13, bf16[2,1536,128]{2,1,0:T(8,128)(2,1)} %bitcast.15), custom_call_target="tpu_custom_call" | custom-call | tf_op jit(solution)/shard_map/pack/pallas_call | solution.py:73
  12.6 6.1 %all_to_all.10.refs_2_.refs_3_.refs_10_.refs_11_.refs_12_.refs_13_.refs_14_.refs_15_ = bf16[2,2320,128]{2,1,0:T(8,128)(2,1)S(1)} all-to-all(bf16[2,2320,128]{2,1,0:T(8,128)(2,1)} %pack.2), channel_id=1, replica_groups={{0,1},{2,3},{4,5},{6,7},{8,9},{10,11},{12,13},{14,15},{16,17},{18,19},{..., dimensions={0} | all-to-all | bytes 2375680 | tf_op jit(solution)/shard_map/all_to_all | solution.py:388
  18.7 1.0 slice.4
  19.7 1.4 %collective-permute-done.refs_0_.refs_4_.refs_5_.refs_6_ = bf16[1,2320,128]{2,1,0:T(8,128)(2,1)S(1)} collective-permute-done((bf16[1,2320,128]{2,1,0:T(8,128)(2,1)}, bf16[1,2320,128]{2,1,0:T(8,128)(2,1)S(1)}, u32[]{:S(2)}, u32[]{:S(2)}) %collective-permute-start) | collective-permute-done | bytes 593952 | tf_op jit(solution)/shard_map/ppermute | solution.py:434
  21.0 1.3 %collective-permute-start.5 = (bf16[2,1536,128]{2,1,0:T(8,128)(2,1)}, bf16[2,1536,128]{2,1,0:T(8,128)(2,1)S(1)}, u32[]{:S(2)}, u32[]{:S(2)}) collective-permute-start(bf16[2,1536,128]{2,1,0:T(8,128)(2,1)} %slice.4), channel_id=1, source_target_pairs={{2,4},{3,5},{4,6},{5,7},{6,8},{7,9},{8,10},{9,11},{10,12},{11,13},... | collective-permute-start | bytes 2359304 | tf_op jit(solution)/shard_map/ppermute | solution.py:442
  22.3 4.2 %collective-permute-start.7 = (bf16[1,2320,128]{2,1,0:T(8,128)(2,1)}, bf16[1,2320,128]{2,1,0:T(8,128)(2,1)}, u32[]{:S(2)}, u32[]{:S(2)}) collective-permute-start(bf16[1,2320,128]{2,1,0:T(8,128)(2,1)} %get-tuple-element.33), channel_id=1, source_target_pairs={{0,1},{1,0},{2,3},{3,2},{4,5},{5,4},{6,7},{7,6},{8,9},{9,8},{10,11... | collective-permute-start | bytes 1781768 | tf_op jit(solution)/shard_map/ppermute | solution.py:432
  26.5 7.1 %collective-permute-done.2.refs_16_.refs_17_ = bf16[1,1536,128]{2,1,0:T(8,128)(2,1)S(1)} collective-permute-done((bf16[1,1536,128]{2,1,0:T(8,128)(2,1)}, bf16[1,1536,128]{2,1,0:T(8,128)(2,1)S(1)}, u32[]{:S(2)}, u32[]{:S(2)}) %collective-permute-start.2) | collective-permute-done | bytes 393248 | tf_op jit(solution)/shard_map/ppermute | solution.py:437
  33.7 8.2 %collective-permute-done.3.refs_18_.refs_19_ = bf16[1,1536,128]{2,1,0:T(8,128)(2,1)S(1)} collective-permute-done((bf16[1,1536,128]{2,1,0:T(8,128)(2,1)}, bf16[1,1536,128]{2,1,0:T(8,128)(2,1)S(1)}, u32[]{:S(2)}, u32[]{:S(2)}) %collective-permute-start.3) | collective-permute-done | bytes 393248 | tf_op jit(solution)/shard_map/ppermute | solution.py:438
  42.6 1.3 %collective-permute-start.4 = (bf16[2,2320,128]{2,1,0:T(8,128)(2,1)S(1)}, bf16[2,2320,128]{2,1,0:T(8,128)(2,1)S(1)}, u32[]{:S(2)}, u32[]{:S(2)}) collective-permute-start(bf16[2,2320,128]{2,1,0:T(8,128)(2,1)S(1)} %all_to_all.10.refs_2_.refs_3_.refs_10_.refs_11_.refs_12_.refs_13_.refs_14_.refs_15_), channel_id=1, source_target_pairs={{2,0},{3,1},{4,2},{5,3},{6,4},{7,5},{8,6},{9,7},{10,8},{11,9},{12,... | collective-permute-start | bytes 3563528 | tf_op jit(solution)/shard_map/ppermute | solution.py:444
  43.9 9.8 %attention.3 = (bf16[2,8,3,96,128]{4,3,2,1,0:T(8,128)(2,1)}, bf16[2,8,3,96,128]{4,3,2,1,0:T(8,128)(2,1)}, bf16[2,8,2,96,128]{4,3,2,1,0:T(8,128)(2,1)}) custom-call(s32[1]{0:T(128)} %bitcast.1.edge_ref, s32[1]{0:T(128)} %bitcast.parity_ref.out_turn_ref.turned_ref.head_half_ref, s32[1]{0:T(128)} %constant.25.clone.1.turned_ref.out_turn_ref, ...), custom_call_target="tpu_custom_call" | custom-call | flops 1811939328 | bytes 3932160 | tf_op jit(solution)/shard_map/attention/pallas_call | solution.py:268
  53.7 5.0 %collective-permute-done.5.refs_16_.refs_17_.refs_18_.refs_19_ = bf16[2,1536,128]{2,1,0:T(8,128)(2,1)S(1)} collective-permute-done((bf16[2,1536,128]{2,1,0:T(8,128)(2,1)}, bf16[2,1536,128]{2,1,0:T(8,128)(2,1)S(1)}, u32[]{:S(2)}, u32[]{:S(2)}) %collective-permute-start.5) | collective-permute-done | bytes 786464 | tf_op jit(solution)/shard_map/ppermute | solution.py:442
  58.7 1.4 %collective-permute-start.8 = (bf16[2,8,3,96,128]{4,3,2,1,0:T(8,128)(2,1)}, bf16[2,8,3,96,128]{4,3,2,1,0:T(8,128)(2,1)S(1)}, u32[]{:S(2)}, u32[]{:S(2)}) collective-permute-start(bf16[2,8,3,96,128]{4,3,2,1,0:T(8,128)(2,1)} %get-tuple-element.41), channel_id=1, source_target_pairs={{0,2},{1,3},{2,4},{3,5},{4,6},{5,7},{6,8},{7,9},{8,10},{9,11},{10,... | collective-permute-start | bytes 3538952 | tf_op jit(solution)/shard_map/ppermute | solution.py:452
  60.1 1.5 %collective-permute-start.9 = (bf16[2,8,2,96,128]{4,3,2,1,0:T(8,128)(2,1)}, bf16[2,8,2,96,128]{4,3,2,1,0:T(8,128)(2,1)S(1)}, u32[]{:S(2)}, u32[]{:S(2)}) collective-permute-start(bf16[2,8,2,96,128]{4,3,2,1,0:T(8,128)(2,1)} %get-tuple-element.45), channel_id=1, source_target_pairs={{32,30},{33,31},{64,62},{65,63},{96,94},{97,95},{128,126},{129,127... | collective-permute-start | bytes 2359304 | tf_op jit(solution)/shard_map/ppermute | solution.py:451
  61.6 9.6 %collective-permute-done.4.refs_0_.refs_1_.refs_4_.refs_5_.refs_6_.refs_7_.refs_8_.refs_9_ = bf16[2,2320,128]{2,1,0:T(8,128)(2,1)S(1)} collective-permute-done((bf16[2,2320,128]{2,1,0:T(8,128)(2,1)S(1)}, bf16[2,2320,128]{2,1,0:T(8,128)(2,1)S(1)}, u32[]{:S(2)}, u32[]{:S(2)}) %collective-permute-start.4) | collective-permute-done | bytes 1187872 | tf_op jit(solution)/shard_map/ppermute | solution.py:444
  72.2 9.8 %attention.2 = (bf16[8,3,96,128]{3,2,1,0:T(8,128)(2,1)}, bf16[8,3,96,128]{3,2,1,0:T(8,128)(2,1)}, bf16[8,3,96,128]{3,2,1,0:T(8,128)(2,1)}, bf16[8,3,96,128]{3,2,...) custom-call(s32[1]{0:T(128)} %bitcast.1.edge_ref, ...), custom_call_target="tpu_custom_call" | custom-call | flops 1811939328 | bytes 3932160 | tf_op jit(solution)/shard_map/attention/pallas_call | solution.py:268
  82.0 1.3 %collective-permute-start.13 = (bf16[8,3,96,128]{3,2,1,0:T(8,128)(2,1)}, bf16[8,3,96,128]{3,2,1,0:T(8,128)(2,1)S(1)}, u32[]{:S(2)}, u32[]{:S(2)}) collective-permute-start(bf16[8,3,96,128]{3,2,1,0:T(8,128)(2,1)} %get-tuple-element.48), channel_id=1, source_target_pairs={{0,2},{1,3},{2,4},{3,5},{4,6},{5,7},{6,8},{7,9},{8,10},{9,11},{10,... | collective-permute-start | bytes 1769480 | tf_op jit(solution)/shard_map/ppermute | solution.py:459
  83.4 3.7 %collective-permute-start.6 = (bf16[8,3,96,128]{3,2,1,0:T(8,128)(2,1)}, bf16[8,3,96,128]{3,2,1,0:T(8,128)(2,1)S(1)}, u32[]{:S(2)}, u32[]{:S(2)}) collective-permute-start(bf16[8,3,96,128]{3,2,1,0:T(8,128)(2,1)} %get-tuple-element.38), channel_id=1, source_target_pairs={{0,1},{1,0},{2,3},{3,2},{4,5},{5,4},{6,7},{7,6},{8,9},{9,8},{10,11... | collective-permute-start | bytes 1769480 | tf_op jit(solution)/shard_map/ppermute | solution.py:465
  87.2 3.7 %collective-permute-start.10 = (bf16[8,3,96,128]{3,2,1,0:T(8,128)(2,1)}, bf16[8,3,96,128]{3,2,1,0:T(8,128)(2,1)S(1)}, u32[]{:S(2)}, u32[]{:S(2)}) collective-permute-start(bf16[8,3,96,128]{3,2,1,0:T(8,128)(2,1)} %get-tuple-element.43), channel_id=1, source_target_pairs={{0,3},{1,2},{2,5},{3,4},{4,7},{5,6},{6,9},{7,8},{8,11},{9,10},{10,... | collective-permute-start | bytes 1769480 | tf_op jit(solution)/shard_map/ppermute | solution.py:460
  90.9 2.1 %collective-permute-start.14 = (bf16[8,2,96,128]{3,2,1,0:T(8,128)(2,1)}, bf16[8,2,96,128]{3,2,1,0:T(8,128)(2,1)S(1)}, u32[]{:S(2)}, u32[]{:S(2)}) collective-permute-start(bf16[8,2,96,128]{3,2,1,0:T(8,128)(2,1)} %get-tuple-element.50), channel_id=1, source_target_pairs={{4,2},{5,3},{6,4},{7,5},{8,6},{9,7},{10,8},{11,9},{12,10},{13,11},... | collective-permute-start | bytes 1179656 | tf_op jit(solution)/shard_map/ppermute | solution.py:461
  93.0 1.9 %collective-permute-start.12 = (bf16[8,2,96,128]{3,2,1,0:T(8,128)(2,1)}, bf16[8,2,96,128]{3,2,1,0:T(8,128)(2,1)S(1)}, u32[]{:S(2)}, u32[]{:S(2)}) collective-permute-start(bf16[8,2,96,128]{3,2,1,0:T(8,128)(2,1)} %get-tuple-element.46), channel_id=1, source_target_pairs={{4,3},{5,2},{6,5},{7,4},{8,7},{9,6},{10,9},{11,8},{12,11},{13,10},... | collective-permute-start | bytes 1179656 | tf_op jit(solution)/shard_map/ppermute | solution.py:462
  94.9 3.2 %merge.1 = bf16[2,8,3,96,128]{4,3,2,1,0:T(8,128)(2,1)} custom-call(bf16[2,8,3,96,128]{4,3,2,1,0:T(8,128)(2,1)} %get-tuple-element.51.kept_ref, bf16[2,8,3,96,128]{4,3,2,1,0:T(8,128)(2,1)} %copy-done.6, bf16[2,8,2,96,128]{4,3,2,1,0:T(8,128)(2,1)} %copy-done.8, bf16[2,8,2,96,128]{4,3,2,1,0:T(8,128)(2,1)} %copy-done.7), custom_call_target="tpu_custom_call" | custom-call | tf_op jit(solution)/shard_map/merge/pallas_call | solution.py:304
  98.1 5.8 %all_to_all.11.early_ref = bf16[2,8,3,96,128]{4,3,2,1,0:T(8,128)(2,1)S(1)} all-to-all(bf16[2,8,3,96,128]{4,3,2,1,0:T(8,128)(2,1)} %merge.1), channel_id=1, replica_groups={{0,1},{2,3},{4,5},{6,7},{8,9},{10,11},{12,13},{14,15},{16,17},{18,19},{..., dimensions={0} | all-to-all | bytes 2359296 | tf_op jit(solution)/shard_map/all_to_all | solution.py:388
  103.9 1.0 place.1
  106.0 2.1 %finish.2 = (bf16[2,16,96,128]{3,2,1,0:T(8,128)(2,1)}, bf16[2,16,96,128]{3,2,1,0:T(8,128)(2,1)}, bf16[2,16,96,128]{3,2,1,0:T(8,128)(2,1)}) custom-call(s32[1]{0:T(128)} %bitcast.parity_ref.out_turn_ref.turned_ref.head_half_ref, bf16[8,3,96,128]{3,2,1,0:T(8,128)(2,1)} %get-tuple-element.47.kept_ref, ...), custom_call_target="tpu_custom_call", output_to_operand_aliasing={{0}: (4, {}), {1}: (5, {}), {2}: (6, {})} | custom-call | tf_op jit(solution)/shard_map/finish/pallas_call | solution.py:360
  108.1 1.4 %collective-permute-done.12.from_next_ref = bf16[8,2,96,128]{3,2,1,0:T(8,128)(2,1)S(1)} collective-permute-done((bf16[8,2,96,128]{3,2,1,0:T(8,128)(2,1)}, bf16[8,2,96,128]{3,2,1,0:T(8,128)(2,1)S(1)}, u32[]{:S(2)}, u32[]{:S(2)}) %collective-permute-start.12) | collective-permute-done | bytes 393248 | tf_op jit(solution)/shard_map/ppermute | solution.py:462
  109.5 1.4 %collective-permute-done.10.from_prior_ref = bf16[8,3,96,128]{3,2,1,0:T(8,128)(2,1)S(1)} collective-permute-done((bf16[8,3,96,128]{3,2,1,0:T(8,128)(2,1)}, bf16[8,3,96,128]{3,2,1,0:T(8,128)(2,1)S(1)}, u32[]{:S(2)}, u32[]{:S(2)}) %collective-permute-start.10) | collective-permute-done | bytes 589856 | tf_op jit(solution)/shard_map/ppermute | solution.py:460
  111.7 2.1 %finish.3 = (bf16[2,16,96,128]{3,2,1,0:T(8,128)(2,1)}, bf16[2,16,96,128]{3,2,1,0:T(8,128)(2,1)}, bf16[2,16,96,128]{3,2,1,0:T(8,128)(2,1)}) custom-call(s32[1]{0:T(128)S(6)} %sub.3.head_half_ref, bf16[8,3,96,128]{3,2,1,0:T(8,128)(2,1)} %copy-done.9, bf16[8,3,96,128]{3,2,1,0:T(8,128)(2,1)} %copy-done.10, ...), custom_call_target="tpu_custom_call", output_to_operand_aliasing={{0}: (4, {}), {1}: (5, {}), {2}: (6, {})} | custom-call | tf_op jit(solution)/shard_map/finish/pallas_call | solution.py:360
  (37 shorter events, 3.6 us)
Async XLA Ops:
  4.2 16.8 %collective-permute-start = (bf16[1,2320,128]{2,1,0:T(8,128)(2,1)}, bf16[1,2320,128]{2,1,0:T(8,128)(2,1)S(1)}, u32[]{:S(2)}, u32[]{:S(2)}) collective-permute-start(bf16[1,2320,128]{2,1,0:T(8,128)(2,1)} %get-tuple-element.32.refs_2_.refs_10_.refs_11_.refs_12_), channel_id=1, source_target_pairs={{2,0},{3,1},{4,2},{5,3},{6,4},{7,5},{8,6},{9,7},{10,8},{11,9},{12,... | collective-permute-start | bytes 1781768 | tf_op jit(solution)/shard_map/ppermute | solution.py:434
  5.5 37.1 %collective-permute-start.1 = (bf16[1,2320,128]{2,1,0:T(8,128)(2,1)}, bf16[1,2320,128]{2,1,0:T(8,128)(2,1)}, u32[]{:S(2)}, u32[]{:S(2)}) collective-permute-start(bf16[1,2320,128]{2,1,0:T(8,128)(2,1)} %get-tuple-element.33), channel_id=1, source_target_pairs={{2,1},{3,0},{4,3},{5,2},{6,5},{7,4},{8,7},{9,6},{10,9},{11,8},{12,... | collective-permute-start | bytes 1781768 | tf_op jit(solution)/shard_map/ppermute | solution.py:435
  6.8 26.8 %collective-permute-start.2 = (bf16[1,1536,128]{2,1,0:T(8,128)(2,1)}, bf16[1,1536,128]{2,1,0:T(8,128)(2,1)S(1)}, u32[]{:S(2)}, u32[]{:S(2)}) collective-permute-start(bf16[1,1536,128]{2,1,0:T(8,128)(2,1)} %get-tuple-element.34), channel_id=1, source_target_pairs={{2,4},{3,5},{4,6},{5,7},{6,8},{7,9},{8,10},{9,11},{10,12},{11,13},... | collective-permute-start | bytes 1179656 | tf_op jit(solution)/shard_map/ppermute | solution.py:437
  8.1 33.7 %collective-permute-start.3 = (bf16[1,1536,128]{2,1,0:T(8,128)(2,1)}, bf16[1,1536,128]{2,1,0:T(8,128)(2,1)S(1)}, u32[]{:S(2)}, u32[]{:S(2)}) collective-permute-start(bf16[1,1536,128]{2,1,0:T(8,128)(2,1)} %get-tuple-element.35), channel_id=1, source_target_pairs={{2,5},{3,4},{4,7},{5,6},{6,9},{7,8},{8,11},{9,10},{10,13},{11,12},... | collective-permute-start | bytes 1179656 | tf_op jit(solution)/shard_map/ppermute | solution.py:438
  18.7 35.0 %copy-start = (bf16[2,2320,128]{2,1,0:T(8,128)(2,1)}, bf16[2,2320,128]{2,1,0:T(8,128)(2,1)S(1)}, u32[]{:S(2)}) copy-start(bf16[2,2320,128]{2,1,0:T(8,128)(2,1)S(1)} %all_to_all.10.refs_2_.refs_3_.refs_10_.refs_11_.refs_12_.refs_13_.refs_14_.refs_15_) | copy-start | bytes 3563524
  21.0 20.8 %copy-start.3 = (bf16[1,2320,128]{2,1,0:T(8,128)(2,1)}, bf16[1,2320,128]{2,1,0:T(8,128)(2,1)S(1)}, u32[]{:S(2)}) copy-start(bf16[1,2320,128]{2,1,0:T(8,128)(2,1)S(1)} %collective-permute-done.refs_0_.refs_4_.refs_5_.refs_6_) | copy-start | bytes 1781764
  21.0 37.7 %collective-permute-start.5 = (bf16[2,1536,128]{2,1,0:T(8,128)(2,1)}, bf16[2,1536,128]{2,1,0:T(8,128)(2,1)S(1)}, u32[]{:S(2)}, u32[]{:S(2)}) collective-permute-start(bf16[2,1536,128]{2,1,0:T(8,128)(2,1)} %slice.4), channel_id=1, source_target_pairs={{2,4},{3,5},{4,6},{5,7},{6,8},{7,9},{8,10},{9,11},{10,12},{11,13},... | collective-permute-start | bytes 2359304 | tf_op jit(solution)/shard_map/ppermute | solution.py:442
  22.3 21.6 %collective-permute-start.7 = (bf16[1,2320,128]{2,1,0:T(8,128)(2,1)}, bf16[1,2320,128]{2,1,0:T(8,128)(2,1)}, u32[]{:S(2)}, u32[]{:S(2)}) collective-permute-start(bf16[1,2320,128]{2,1,0:T(8,128)(2,1)} %get-tuple-element.33), channel_id=1, source_target_pairs={{0,1},{1,0},{2,3},{3,2},{4,5},{5,4},{6,7},{7,6},{8,9},{9,8},{10,11... | collective-permute-start | bytes 1781768 | tf_op jit(solution)/shard_map/ppermute | solution.py:432
  33.7 10.3 %copy-start.4 = (bf16[1,1536,128]{2,1,0:T(8,128)(2,1)}, bf16[1,1536,128]{2,1,0:T(8,128)(2,1)S(1)}, u32[]{:S(2)}) copy-start(bf16[1,1536,128]{2,1,0:T(8,128)(2,1)S(1)} %collective-permute-done.2.refs_16_.refs_17_) | copy-start | bytes 1179652
  41.9 0.7 copy-start.5
  42.6 28.6 %collective-permute-start.4 = (bf16[2,2320,128]{2,1,0:T(8,128)(2,1)S(1)}, bf16[2,2320,128]{2,1,0:T(8,128)(2,1)S(1)}, u32[]{:S(2)}, u32[]{:S(2)}) collective-permute-start(bf16[2,2320,128]{2,1,0:T(8,128)(2,1)S(1)} %all_to_all.10.refs_2_.refs_3_.refs_10_.refs_11_.refs_12_.refs_13_.refs_14_.refs_15_), channel_id=1, source_target_pairs={{2,0},{3,1},{4,2},{5,3},{6,4},{7,5},{8,6},{9,7},{10,8},{11,9},{12,... | collective-permute-start | bytes 3563528 | tf_op jit(solution)/shard_map/ppermute | solution.py:444
  58.7 13.4 %copy-start.2 = (bf16[2,1536,128]{2,1,0:T(8,128)(2,1)}, bf16[2,1536,128]{2,1,0:T(8,128)(2,1)S(1)}, u32[]{:S(2)}) copy-start(bf16[2,1536,128]{2,1,0:T(8,128)(2,1)S(1)} %collective-permute-done.5.refs_16_.refs_17_.refs_18_.refs_19_) | copy-start | bytes 2359300
  58.7 28.4 %collective-permute-start.8 = (bf16[2,8,3,96,128]{4,3,2,1,0:T(8,128)(2,1)}, bf16[2,8,3,96,128]{4,3,2,1,0:T(8,128)(2,1)S(1)}, u32[]{:S(2)}, u32[]{:S(2)}) collective-permute-start(bf16[2,8,3,96,128]{4,3,2,1,0:T(8,128)(2,1)} %get-tuple-element.41), channel_id=1, source_target_pairs={{0,2},{1,3},{2,4},{3,5},{4,6},{5,7},{6,8},{7,9},{8,10},{9,11},{10,... | collective-permute-start | bytes 3538952 | tf_op jit(solution)/shard_map/ppermute | solution.py:452
  60.1 27.0 %collective-permute-start.9 = (bf16[2,8,2,96,128]{4,3,2,1,0:T(8,128)(2,1)}, bf16[2,8,2,96,128]{4,3,2,1,0:T(8,128)(2,1)S(1)}, u32[]{:S(2)}, u32[]{:S(2)}) collective-permute-start(bf16[2,8,2,96,128]{4,3,2,1,0:T(8,128)(2,1)} %get-tuple-element.45), channel_id=1, source_target_pairs={{32,30},{33,31},{64,62},{65,63},{96,94},{97,95},{128,126},{129,127... | collective-permute-start | bytes 2359304 | tf_op jit(solution)/shard_map/ppermute | solution.py:451
  71.2 1.0 copy-start.1
  71.2 19.7 %collective-permute-start.11 = (bf16[2,8,2,96,128]{4,3,2,1,0:T(8,128)(2,1)}, bf16[2,8,2,96,128]{4,3,2,1,0:T(8,128)(2,1)S(1)}, u32[]{:S(2)}, u32[]{:S(2)}) collective-permute-start(bf16[2,8,2,96,128]{4,3,2,1,0:T(8,128)(2,1)} %get-tuple-element.45), channel_id=1, source_target_pairs={{4,2},{5,3},{6,4},{7,5},{8,6},{9,7},{10,8},{11,9},{12,10},{13,11},... | collective-permute-start | bytes 2359304 | tf_op jit(solution)/shard_map/ppermute | solution.py:453
  82.0 22.9 %collective-permute-start.13 = (bf16[8,3,96,128]{3,2,1,0:T(8,128)(2,1)}, bf16[8,3,96,128]{3,2,1,0:T(8,128)(2,1)S(1)}, u32[]{:S(2)}, u32[]{:S(2)}) collective-permute-start(bf16[8,3,96,128]{3,2,1,0:T(8,128)(2,1)} %get-tuple-element.48), channel_id=1, source_target_pairs={{0,2},{1,3},{2,4},{3,5},{4,6},{5,7},{6,8},{7,9},{8,10},{9,11},{10,... | collective-permute-start | bytes 1769480 | tf_op jit(solution)/shard_map/ppermute | solution.py:459
  83.4 24.7 %collective-permute-start.6 = (bf16[8,3,96,128]{3,2,1,0:T(8,128)(2,1)}, bf16[8,3,96,128]{3,2,1,0:T(8,128)(2,1)S(1)}, u32[]{:S(2)}, u32[]{:S(2)}) collective-permute-start(bf16[8,3,96,128]{3,2,1,0:T(8,128)(2,1)} %get-tuple-element.38), channel_id=1, source_target_pairs={{0,1},{1,0},{2,3},{3,2},{4,5},{5,4},{6,7},{7,6},{8,9},{9,8},{10,11... | collective-permute-start | bytes 1769480 | tf_op jit(solution)/shard_map/ppermute | solution.py:465
  87.1 7.8 %copy-start.7 = (bf16[2,8,2,96,128]{4,3,2,1,0:T(8,128)(2,1)}, bf16[2,8,2,96,128]{4,3,2,1,0:T(8,128)(2,1)S(1)}, u32[]{:S(2)}) copy-start(bf16[2,8,2,96,128]{4,3,2,1,0:T(8,128)(2,1)S(1)} %collective-permute-done.9.rest_1_) | copy-start | bytes 2359300
  87.1 7.8 %copy-start.6 = (bf16[2,8,3,96,128]{4,3,2,1,0:T(8,128)(2,1)}, bf16[2,8,3,96,128]{4,3,2,1,0:T(8,128)(2,1)S(1)}, u32[]{:S(2)}) copy-start(bf16[2,8,3,96,128]{4,3,2,1,0:T(8,128)(2,1)S(1)} %collective-permute-done.8.from_prior_ref) | copy-start | bytes 3538948
  87.2 23.7 %collective-permute-start.10 = (bf16[8,3,96,128]{3,2,1,0:T(8,128)(2,1)}, bf16[8,3,96,128]{3,2,1,0:T(8,128)(2,1)S(1)}, u32[]{:S(2)}, u32[]{:S(2)}) collective-permute-start(bf16[8,3,96,128]{3,2,1,0:T(8,128)(2,1)} %get-tuple-element.43), channel_id=1, source_target_pairs={{0,3},{1,2},{2,5},{3,4},{4,7},{5,6},{6,9},{7,8},{8,11},{9,10},{10,... | collective-permute-start | bytes 1769480 | tf_op jit(solution)/shard_map/ppermute | solution.py:460
  90.9 4.0 %copy-start.8 = (bf16[2,8,2,96,128]{4,3,2,1,0:T(8,128)(2,1)}, bf16[2,8,2,96,128]{4,3,2,1,0:T(8,128)(2,1)S(1)}, u32[]{:S(2)}) copy-start(bf16[2,8,2,96,128]{4,3,2,1,0:T(8,128)(2,1)S(1)} %collective-permute-done.11.rest_0_) | copy-start | bytes 2359300
  90.9 14.1 %collective-permute-start.14 = (bf16[8,2,96,128]{3,2,1,0:T(8,128)(2,1)}, bf16[8,2,96,128]{3,2,1,0:T(8,128)(2,1)S(1)}, u32[]{:S(2)}, u32[]{:S(2)}) collective-permute-start(bf16[8,2,96,128]{3,2,1,0:T(8,128)(2,1)} %get-tuple-element.50), channel_id=1, source_target_pairs={{4,2},{5,3},{6,4},{7,5},{8,6},{9,7},{10,8},{11,9},{12,10},{13,11},... | collective-permute-start | bytes 1179656 | tf_op jit(solution)/shard_map/ppermute | solution.py:461
  93.0 16.4 %collective-permute-start.12 = (bf16[8,2,96,128]{3,2,1,0:T(8,128)(2,1)}, bf16[8,2,96,128]{3,2,1,0:T(8,128)(2,1)S(1)}, u32[]{:S(2)}, u32[]{:S(2)}) collective-permute-start(bf16[8,2,96,128]{3,2,1,0:T(8,128)(2,1)} %get-tuple-element.46), channel_id=1, source_target_pairs={{4,3},{5,2},{6,5},{7,4},{8,7},{9,6},{10,9},{11,8},{12,11},{13,10},... | collective-permute-start | bytes 1179656 | tf_op jit(solution)/shard_map/ppermute | solution.py:462
  105.0 0.8 copy-start.11
  105.0 0.9 copy-start.13
  108.0 2.8 %copy-start.9 = (bf16[8,3,96,128]{3,2,1,0:T(8,128)(2,1)}, bf16[8,3,96,128]{3,2,1,0:T(8,128)(2,1)S(1)}, u32[]{:S(2)}) copy-start(bf16[8,3,96,128]{3,2,1,0:T(8,128)(2,1)S(1)} %collective-permute-done.6.kept_ref) | copy-start | bytes 1769476
  109.4 1.4 %copy-start.12 = (bf16[8,2,96,128]{3,2,1,0:T(8,128)(2,1)}, bf16[8,2,96,128]{3,2,1,0:T(8,128)(2,1)S(1)}, u32[]{:S(2)}) copy-start(bf16[8,2,96,128]{3,2,1,0:T(8,128)(2,1)S(1)} %collective-permute-done.12.from_next_ref) | copy-start | bytes 1179652
  110.8 0.9 copy-start.10
